TPU v7x, 32 devices: a whole 2x2x4 slice. The times are simulated.
32 devices in a mesh: dev: 4 (over z), ha: 4 (over y, x), wa: 2 (over core).
Axes of the slice: x: 2, y: 2, z: 4, core: 2. Of those that a mesh axis runs over, the one named last changes fastest.
Arguments:
- volume: float32 [16, 32, 16, 256], P('dev', 'ha', 'wa'), may hold values from -6 to 6
- kernel: float32 [256, 27, 256], replicated, may hold values from -0.078125 to 0.078125
- upstream: float32 [16, 32, 16, 256], P('dev', 'ha', 'wa'), may hold values from -6 to 6
Outputs:
- output: float32 [16, 32, 16, 256], P('dev', 'ha', 'wa')
- volume_grad: float32 [16, 32, 16, 256], P('dev', 'ha', 'wa')
- kernel_grad: float32 [256, 27, 256], P('wa')
All inputs are finite; a program needn't handle non-finite values.
Results may differ from a plain program's by a relative error of at most 0.0001.
Values sent between devices are 32-bit elements; how exact they have to be, the bound alone decides.
No kernel may reach another device: no remote copies, remote signals or barrier semaphores. Data moves between devices by JAX's collectives and lax.ppermute only.
A program may use at most 128 MiB of HBM per device.

v0:
```python
import math

import jax
import jax.numpy as jnp
from jax import lax
from jax.sharding import PartitionSpec as P


def padded_2(shard, sides, width):
    for axis, dim in sides:
        count, length = (lax.axis_size(axis), shard.shape[dim])
        up = [(i, (i + 1) % count) for i in range(count)]
        down = [(j, i) for i, j in up]
        last = lax.slice_in_dim(shard, length - width, length, axis=dim)
        initial = lax.slice_in_dim(shard, 0, width, axis=dim)
        before = lax.ppermute(last, axis, up)
        after = lax.ppermute(initial, axis, down)
        shard = jnp.concatenate([before, shard, after], axis=dim)
    return shard


def tap_offsets():
    return [(da, db, dc) for da in (-1, 0, 1) for db in (-1, 0, 1) for dc in (-1, 0, 1)]


def per_device(volume, kernel, upstream):
    depth_cells, height_cells, width_cells, channels = volume.shape
    cells = depth_cells * height_cells * width_cells
    stacked = jnp.stack([volume, upstream])
    padded = padded_2(stacked, (("dev", 1), ("ha", 2), ("wa", 3)), 1)
    forward_windows = []
    backward_windows = []
    for da, db, dc in tap_offsets():
        forward_windows.append(
            padded[
                0,
                1 + da : 1 + da + depth_cells,
                1 + db : 1 + db + height_cells,
                1 + dc : 1 + dc + width_cells,
            ].reshape(cells, channels)
        )
        backward_windows.append(
            padded[
                1,
                1 - da : 1 - da + depth_cells,
                1 - db : 1 - db + height_cells,
                1 - dc : 1 - dc + width_cells,
            ].reshape(cells, channels)
        )
    forward_patches = jnp.stack(forward_windows, axis=1)
    backward_patches = jnp.stack(backward_windows, axis=1)
    output = jnp.einsum(
        "ntc,cto->no",
        forward_patches,
        kernel,
        precision=lax.Precision.HIGHEST,
        preferred_element_type=jnp.float32,
    )
    volume_grad = jnp.einsum(
        "nto,cto->nc",
        backward_patches,
        kernel,
        precision=lax.Precision.HIGHEST,
        preferred_element_type=jnp.float32,
    )
    flat_up = upstream.reshape(cells, channels)
    total_cells = cells * lax.axis_size("dev") * lax.axis_size("ha") * lax.axis_size("wa")
    factor = 1.0 / math.sqrt(total_cells)
    owned = channels // lax.axis_size("wa")
    summed = lax.psum(
        jnp.einsum(
            "ntc,no->cto",
            forward_patches,
            flat_up,
            precision=lax.Precision.HIGHEST,
            preferred_element_type=jnp.float32,
        )
        * factor,
        ("dev", "ha", "wa"),
    )
    kernel_grad = lax.dynamic_slice_in_dim(summed, lax.axis_index("wa") * owned, owned, 0)
    return (output.reshape(volume.shape), volume_grad.reshape(volume.shape), kernel_grad)


def solution(mesh):
    placed = (P("dev", "ha", "wa", None), P(), P("dev", "ha", "wa", None))
    return jax.shard_map(
        per_device,
        mesh=mesh,
        in_specs=placed,
        out_specs=(P("dev", "ha", "wa", None), P("dev", "ha", "wa", None), P("wa", None, None)),
        check_vma=False,
    )
```

profile of v0, /device:TPU:8, one launch (start us, length us, event | category | flops | bytes accessed | tf_op | source)
XLA Modules:
  0.0 225.7 jit_solution(11577098144438105871)
XLA Ops:
  8.2 1.6 collective-permute-start
  10.3 3.9 %collective-permute-done = f32[2,1,8,8,256]{4,3,2,1,0:T(8,128)S(1)} collective-permute-done((f32[2,1,8,8,256]{4,3,2,1,0:T(8,128)S(1)}, f32[2,1,8,8,256]{4,3,2,1,0:T(8,128)S(1)}, u32[]{:S(2)}, u32[]{:S(2)}) %collective-permute-start) | collective-permute-done | bytes 131104 | tf_op jit(solution)/shard_map/ppermute | solution.py:16
  14.3 2.9 %collective-permute-done.1 = f32[2,1,8,8,256]{4,3,2,1,0:T(8,128)S(1)} collective-permute-done((f32[2,1,8,8,256]{4,3,2,1,0:T(8,128)S(1)}, f32[2,1,8,8,256]{4,3,2,1,0:T(8,128)S(1)}, u32[]{:S(2)}, u32[]{:S(2)}) %collective-permute-start.1) | collective-permute-done | bytes 131104 | tf_op jit(solution)/shard_map/ppermute | solution.py:17
  18.0 1.5 collective-permute-start.2
  21.0 2.0 pad_maximum_fusion.2
  35.6 2.8 %copy-done = f32[256,27,256]{2,0,1:T(8,128)} copy-done((f32[256,27,256]{2,0,1:T(8,128)}, f32[256,27,256]{2,0,1:T(8,128)S(1)}, u32[]{:S(2)}) %copy-start) | copy-done | bytes 7077912
  38.4 13.7 %multiply_bitcast_fusion = f32[256,27,256]{2,0,1:T(8,128)} fusion(f32[256,27,256]{2,0,1:T(8,128)S(1)} %constant_dynamic-update-slice_fusion, f32[256,256,1]{1,0,2:T(8,128)S(1)} %bitcast.83), kind=kOutput, calls=%fused_computation | convolution fusion | flops 5437587456 | bytes 14417920 | tf_op jit(solution)/shard_map/ntc,no->cto/dot_general | solution.py:71
  52.2 1.8 constant_dynamic-update-slice_fusion.52
  54.0 1.7 constant_dynamic-update-slice_fusion.51
  55.7 1.7 constant_dynamic-update-slice_fusion.50
  57.4 1.7 constant_dynamic-update-slice_fusion.49
  59.1 1.7 constant_dynamic-update-slice_fusion.48
  60.7 1.7 constant_dynamic-update-slice_fusion.47
  62.4 1.8 constant_dynamic-update-slice_fusion.46
  64.2 1.7 constant_dynamic-update-slice_fusion.45
  65.9 1.7 constant_dynamic-update-slice_fusion.44
  67.6 1.7 constant_dynamic-update-slice_fusion.43
  69.3 1.7 constant_dynamic-update-slice_fusion.42
  70.9 1.7 constant_dynamic-update-slice_fusion.41
  73.4 1.7 constant_dynamic-update-slice_fusion.39
  83.8 14.6 %fusion.4 = f32[256,256,1]{1,0,2:T(8,128)} fusion(f32[256,27,256]{2,0,1:T(8,128)S(1)} %bitcast.74, f32[256,27,256]{2,0,1:T(8,128)} %param.4), kind=kOutput, calls=%fused_computation.82 | convolution fusion | flops 5435817984 | bytes 14417920 | tf_op jit(solution)/shard_map/ntc,cto->no/dot_general | solution.py:52
  98.4 6.5 %fusion.5 = f32[256,256,1]{1,0,2:T(8,128)} fusion(f32[256,27,256]{2,0,1:T(8,128)S(1)} %copy-done.3, f32[256,27,256]{2,0,1:T(8,128)S(1)} %bitcast.76), kind=kOutput, calls=%fused_computation.83 | convolution fusion | flops 5435817984 | bytes 14417920 | tf_op jit(solution)/shard_map/nto,cto->nc/dot_general | solution.py:59
  105.0 109.7 %all-reduce.2.cloned.1.call-done = f32[256,27,256]{2,0,1:T(8,128)} async-done(((f32[256,27,256]{2,0,1:T(8,128)}), f32[256,27,256]{2,0,1:T(8,128)}) %all-reduce.2.cloned.1.call-update) | async-done | bytes 7077904 | tf_op jit(solution)/shard_map/psum | solution.py:70
  214.7 4.2 %constant_dynamic-slice_fusion = f32[128,27,256]{2,0,1:T(8,128)} fusion(f32[256,27,256]{2,0,1:T(8,128)} %all-reduce.2.cloned.1.call-done, s32[]{:T(128)S(6)} %select_n.3), kind=kLoop, calls=%fused_computation.77 | loop fusion | bytes 7077892 | tf_op jit(solution)/shard_map/dynamic_slice | solution.py:81
  (98 shorter events, 25.6 us)
Async XLA Ops:
  7.2 23.3 %copy-start.2 = (f32[4,8,8,256]{3,2,1,0:T(8,128)S(1)}, f32[4,8,8,256]{3,2,1,0:T(8,128)}, u32[]{:S(2)}) copy-start(f32[4,8,8,256]{3,2,1,0:T(8,128)} %param.3) | copy-start | bytes 786436
  7.2 23.3 %copy-start.1 = (f32[4,8,8,256]{3,2,1,0:T(8,128)S(1)}, f32[4,8,8,256]{3,2,1,0:T(8,128)}, u32[]{:S(2)}) copy-start(f32[4,8,8,256]{3,2,1,0:T(8,128)} %param.5) | copy-start | bytes 786436
  7.2 207.5 %all-reduce.2.cloned.1.call-start = ((), (), s32[]{:S(2)}) async-start(), calls=%async_computation | async-start | bytes 14155776 | tf_op jit(solution)/shard_map/psum | solution.py:70
  8.2 6.0 %collective-permute-start = (f32[2,1,8,8,256]{4,3,2,1,0:T(8,128)S(1)}, f32[2,1,8,8,256]{4,3,2,1,0:T(8,128)S(1)}, u32[]{:S(2)}, u32[]{:S(2)}) collective-permute-start(f32[2,1,8,8,256]{4,3,2,1,0:T(8,128)S(1)} %get-tuple-element.65), channel_id=1, source_target_pairs={{0,8},{8,16},{16,24},{24,0},{1,9},{9,17},{17,25},{25,1},{2,10},{10... | collective-permute-start | bytes 393224 | tf_op jit(solution)/shard_map/ppermute | solution.py:16
  9.9 7.3 %collective-permute-start.1 = (f32[2,1,8,8,256]{4,3,2,1,0:T(8,128)S(1)}, f32[2,1,8,8,256]{4,3,2,1,0:T(8,128)S(1)}, u32[]{:S(2)}, u32[]{:S(2)}) collective-permute-start(f32[2,1,8,8,256]{4,3,2,1,0:T(8,128)S(1)} %get-tuple-element.66), channel_id=1, source_target_pairs={{8,0},{16,8},{24,16},{0,24},{9,1},{17,9},{25,17},{1,25},{10,2},{18... | collective-permute-start | bytes 393224 | tf_op jit(solution)/shard_map/ppermute | solution.py:17
  18.0 6.5 %collective-permute-start.2 = (f32[2,6,1,8,256]{4,3,2,1,0:T(8,128)S(1)}, f32[2,6,1,8,256]{4,3,2,1,0:T(8,128)S(1)}, u32[]{:S(2)}, u32[]{:S(2)}) collective-permute-start(f32[2,6,1,8,256]{4,3,2,1,0:T(8,128)S(1)} %get-tuple-element.57), channel_id=1, source_target_pairs={{0,2},{2,4},{4,6},{6,0},{1,3},{3,5},{5,7},{7,1},{8,10},{10,12},{12... | collective-permute-start | bytes 294920 | tf_op jit(solution)/shard_map/ppermute | solution.py:16
  19.6 6.3 %collective-permute-start.3 = (f32[2,6,1,8,256]{4,3,2,1,0:T(8,128)S(1)}, f32[2,6,1,8,256]{4,3,2,1,0:T(8,128)S(1)}, u32[]{:S(2)}, u32[]{:S(2)}) collective-permute-start(f32[2,6,1,8,256]{4,3,2,1,0:T(8,128)S(1)} %get-tuple-element.58), channel_id=1, source_target_pairs={{2,0},{4,2},{6,4},{0,6},{3,1},{5,3},{7,5},{1,7},{10,8},{12,10},{14... | collective-permute-start | bytes 294920 | tf_op jit(solution)/shard_map/ppermute | solution.py:17
  27.2 3.3 %collective-permute-start.4 = (f32[2,6,10,1,256]{4,3,2,1,0:T(1,128)S(1)}, f32[2,6,10,1,256]{4,3,2,1,0:T(1,128)S(1)}, u32[]{:S(2)}, u32[]{:S(2)}) collective-permute-start(f32[2,6,10,1,256]{4,3,2,1,0:T(1,128)S(1)} %get-tuple-element.42), channel_id=1, source_target_pairs={{0,1},{1,0},{2,3},{3,2},{4,5},{5,4},{6,7},{7,6},{8,9},{9,8},{10,11... | collective-permute-start | bytes 368648 | tf_op jit(solution)/shard_map/ppermute | solution.py:16
  27.3 3.2 %collective-permute-start.5 = (f32[2,6,10,1,256]{4,3,2,1,0:T(1,128)S(1)}, f32[2,6,10,1,256]{4,3,2,1,0:T(1,128)S(1)}, u32[]{:S(2)}, u32[]{:S(2)}) collective-permute-start(f32[2,6,10,1,256]{4,3,2,1,0:T(1,128)S(1)} %get-tuple-element.41), channel_id=1, source_target_pairs={{1,0},{0,1},{3,2},{2,3},{5,4},{4,5},{7,6},{6,7},{9,8},{8,9},{11,10... | collective-permute-start | bytes 368648 | tf_op jit(solution)/shard_map/ppermute | solution.py:17
  52.1 31.8 %slice-start = ((s8[7077888]{0:T(1024)(128)(4,1)}), s8[2883584]{0:T(1024)(128)(4,1)S(1)}, s32[]{:S(2)}) async-start(s8[7077888]{0:T(1024)(128)(4,1)} %bitcast.73), calls=%async_computation.1 | async-start | bytes 5767168
  52.1 23.0 %copy-start.11 = (f32[1,4,8,8,256]{4,3,2,1,0:T(8,128)S(1)}, f32[1,4,8,8,256]{4,3,2,1,0:T(8,128)}, u32[]{:S(2)}) copy-start(f32[1,4,8,8,256]{4,3,2,1,0:T(8,128)} %get-tuple-element.24) | copy-start | bytes 786436
  52.1 23.8 %copy-start.6 = (f32[1,4,8,8,256]{4,3,2,1,0:T(8,128)S(1)}, f32[1,4,8,8,256]{4,3,2,1,0:T(8,128)}, u32[]{:S(2)}) copy-start(f32[1,4,8,8,256]{4,3,2,1,0:T(8,128)} %get-tuple-element.44) | copy-start | bytes 786436
  52.1 24.5 %copy-start.14 = (f32[1,4,8,8,256]{4,3,2,1,0:T(8,128)S(1)}, f32[1,4,8,8,256]{4,3,2,1,0:T(8,128)}, u32[]{:S(2)}) copy-start(f32[1,4,8,8,256]{4,3,2,1,0:T(8,128)} %get-tuple-element.6) | copy-start | bytes 786436
  52.1 25.2 %copy-start.10 = (f32[1,4,8,8,256]{4,3,2,1,0:T(8,128)S(1)}, f32[1,4,8,8,256]{4,3,2,1,0:T(8,128)}, u32[]{:S(2)}) copy-start(f32[1,4,8,8,256]{4,3,2,1,0:T(8,128)} %get-tuple-element.23) | copy-start | bytes 786436
  52.1 25.9 %copy-start.5 = (f32[1,4,8,8,256]{4,3,2,1,0:T(8,128)S(1)}, f32[1,4,8,8,256]{4,3,2,1,0:T(8,128)}, u32[]{:S(2)}) copy-start(f32[1,4,8,8,256]{4,3,2,1,0:T(8,128)} %get-tuple-element.72) | copy-start | bytes 786436
  52.1 26.6 %copy-start.13 = (f32[1,4,8,8,256]{4,3,2,1,0:T(8,128)S(1)}, f32[1,4,8,8,256]{4,3,2,1,0:T(8,128)}, u32[]{:S(2)}) copy-start(f32[1,4,8,8,256]{4,3,2,1,0:T(8,128)} %get-tuple-element.5) | copy-start | bytes 786436
  52.1 27.3 %copy-start.8 = (f32[1,4,8,8,256]{4,3,2,1,0:T(8,128)S(1)}, f32[1,4,8,8,256]{4,3,2,1,0:T(8,128)}, u32[]{:S(2)}) copy-start(f32[1,4,8,8,256]{4,3,2,1,0:T(8,128)} %get-tuple-element.22) | copy-start | bytes 786436
  52.2 28.8 %copy-start.12 = (f32[1,4,8,8,256]{4,3,2,1,0:T(8,128)S(1)}, f32[1,4,8,8,256]{4,3,2,1,0:T(8,128)}, u32[]{:S(2)}) copy-start(f32[1,4,8,8,256]{4,3,2,1,0:T(8,128)} %get-tuple-element.4) | copy-start | bytes 786436
  52.2 29.5 %copy-start.7 = (f32[1,4,8,8,256]{4,3,2,1,0:T(8,128)S(1)}, f32[1,4,8,8,256]{4,3,2,1,0:T(8,128)}, u32[]{:S(2)}) copy-start(f32[1,4,8,8,256]{4,3,2,1,0:T(8,128)} %get-tuple-element.21) | copy-start | bytes 786436
  52.2 30.2 %copy-start.4 = (f32[1,4,8,8,256]{4,3,2,1,0:T(8,128)S(1)}, f32[1,4,8,8,256]{4,3,2,1,0:T(8,128)}, u32[]{:S(2)}) copy-start(f32[1,4,8,8,256]{4,3,2,1,0:T(8,128)} %get-tuple-element.43) | copy-start | bytes 786436
  52.2 30.9 %copy-start.9 = (f32[1,4,8,8,256]{4,3,2,1,0:T(8,128)S(1)}, f32[1,4,8,8,256]{4,3,2,1,0:T(8,128)}, u32[]{:S(2)}) copy-start(f32[1,4,8,8,256]{4,3,2,1,0:T(8,128)} %get-tuple-element.3) | copy-start | bytes 786436
  62.4 21.4 %slice-start.1 = ((s8[7077888]{0:T(1024)(128)(4,1)}), s8[4194304]{0:T(1024)(128)(4,1)S(1)}, s32[]{:S(2)}) async-start(s8[7077888]{0:T(1024)(128)(4,1)} %bitcast.73), calls=%async_computation.2 | async-start | bytes 8388608
  82.4 16.0 %slice-start.2 = ((s8[7077888]{0:T(1024)(128)(4,1)}), s8[4194304]{0:T(1024)(128)(4,1)S(1)}, s32[]{:S(2)}) async-start(s8[7077888]{0:T(1024)(128)(4,1)} %bitcast.75), calls=%async_computation.3 | async-start | bytes 8388608
  83.8 14.6 %slice-start.3 = ((s8[7077888]{0:T(1024)(128)(4,1)}), s8[2883584]{0:T(1024)(128)(4,1)S(1)}, s32[]{:S(2)}) async-start(s8[7077888]{0:T(1024)(128)(4,1)} %bitcast.75), calls=%async_computation.4 | async-start | bytes 5767168
  (2 other events, 17.4 us)
Sparse Core Ops, SparseCore 0:
  52.2 162.4 all-reduce.1
where the time goes:
time: 228 us; the launch traced here: 226 us
  waiting for transfers between devices  119 us (52%)
  local copies, waits for them, and re-layouts  44.1 us (19%)
  matrix products  34.8 us (15%)
  between operations  14.4 us (6%)
  other arithmetic  7.22 us (3%)
  starting transfers between devices  5.66 us (2%)
    psum x1, waiting for transfers between devices, per_device(): lax.psum(jnp.einsum('ntc,no->cto', forward_patches, flat_up, precision=la...  110 us
    unnamed x90, local copies, waits for them, and re-layouts  35 us
    dot_general x1, matrix products, per_device(): jnp.einsum('ntc,cto->no', forward_patches, kernel, precision=lax.Precisio...  14.6 us
    dot_general x1, matrix products, per_device(): jnp.einsum('ntc,no->cto', forward_patches, flat_up, precision=lax.Precisi...  13.7 us
    dot_general x1, matrix products, per_device(): jnp.einsum('nto,cto->nc', backward_patches, kernel, precision=lax.Precisi...  6.54 us
    ppermute x3, waiting for transfers between devices, padded_2(): before = lax.ppermute(last, axis, up)  5.46 us
    concatenate x4, other arithmetic, padded_2(): shard = jnp.concatenate([before, shard, after], axis=dim)  5.39 us
  transfers between devices with their start and end apart: 7, of which 5 were waited for; matrix products, arithmetic and copies ran while one was open for 25% of the time, Pallas kernels for 0%

commit v1 on v0

v1 whole, which is shorter than its diff:
```python
import functools
import math

import jax
import jax.numpy as jnp
from jax import lax
from jax.experimental import pallas as pl
from jax.experimental.pallas import tpu as pltpu
from jax.sharding import PartitionSpec as P

F32, BF16 = jnp.float32, jnp.bfloat16


def split(x):
    hi = x.astype(BF16)
    return hi, (x - hi.astype(F32)).astype(BF16)


def padded_by_halo(shard, sides):
    for axis, dim in sides:
        count, length = lax.axis_size(axis), shard.shape[dim]
        up = [(i, (i + 1) % count) for i in range(count)]
        down = [(j, i) for i, j in up]
        before = lax.ppermute(lax.slice_in_dim(shard, length - 1, length, axis=dim), axis, up)
        after = lax.ppermute(lax.slice_in_dim(shard, 0, 1, axis=dim), axis, down)
        shard = jnp.concatenate([before, shard, after], axis=dim)
    return shard


def plain(volume, kernel, upstream):
    depth, height, width, channels = volume.shape
    cells = depth * height * width
    padded = padded_by_halo(jnp.stack([volume, upstream]), (("dev", 1), ("ha", 2), ("wa", 3)))

    def windows(which, sign):
        return jnp.stack(
            [
                padded[which, 1 + sign * a :, 1 + sign * b :, 1 + sign * c :][:depth, :height, :width].reshape(cells, channels)
                for a in (-1, 0, 1) for b in (-1, 0, 1) for c in (-1, 0, 1)
            ],
            axis=1,
        )

    dot = functools.partial(jnp.einsum, precision=lax.Precision.HIGHEST, preferred_element_type=F32)
    forward, backward = windows(0, 1), windows(1, -1)
    output = dot("ntc,cto->no", forward, kernel)
    volume_grad = dot("nto,cto->nc", backward, kernel)
    total = cells * lax.axis_size("dev") * lax.axis_size("ha") * lax.axis_size("wa")
    summed = lax.psum(dot("ntc,no->cto", forward, upstream.reshape(cells, channels)) * (1.0 / math.sqrt(total)), ("dev", "ha", "wa"))
    owned = channels // lax.axis_size("wa")
    kernel_grad = lax.dynamic_slice_in_dim(summed, lax.axis_index("wa") * owned, owned, 0)
    return output.reshape(volume.shape), volume_grad.reshape(volume.shape), kernel_grad


def conv_kernel(v_ref, u_ref, k_ref, out_ref, grad_ref):
    step = pl.program_id(0)
    a, b = step // 3, step % 3

    @pl.when(step == 0)
    def _():
        out_ref[...] = jnp.zeros_like(out_ref)
        grad_ref[...] = jnp.zeros_like(grad_ref)

    cells, channels = out_ref.shape
    d, h = v_ref.shape[1] - 2, v_ref.shape[2] - 2
    out, grad = out_ref[...], grad_ref[...]
    for c in range(3):
        k_hi, k_lo = split(k_ref[c])
        v_hi, v_lo = split(v_ref[c, pl.ds(a, d), pl.ds(b, h)].reshape(cells, channels))
        u_hi, u_lo = split(u_ref[2 - c, pl.ds(2 - a, d), pl.ds(2 - b, h)].reshape(cells, channels))
        for left, right in ((v_hi, k_hi), (v_hi, k_lo), (v_lo, k_hi)):
            out += jnp.dot(left, right, preferred_element_type=F32)
        for left, right in ((u_hi, k_hi), (u_hi, k_lo), (u_lo, k_hi)):
            grad += lax.dot_general(left, right, (((1,), (1,)), ((), ())), preferred_element_type=F32)
    out_ref[...] = out
    grad_ref[...] = grad


def shifted_3(padded):
    width = padded.shape[2] - 2
    return jnp.stack([padded[:, :, c : c + width] for c in range(3)])


def conv_both(volume_padded, upstream_padded, taps):
    v, u = shifted_3(volume_padded), shifted_3(upstream_padded)
    cells = (v.shape[1] - 2) * (v.shape[2] - 2) * v.shape[3]
    channels = v.shape[4]
    whole = pl.BlockSpec(v.shape, lambda i: (0,) * 5)
    result = pl.BlockSpec((cells, channels), lambda i: (0, 0))
    shape = jax.ShapeDtypeStruct((cells, channels), F32)
    return pl.pallas_call(
        conv_kernel,
        grid=(9,),
        in_specs=[whole, whole, pl.BlockSpec((3, channels, channels), lambda i: (i, 0, 0))],
        out_specs=[result, result],
        out_shape=[shape, shape],
        compiler_params=pltpu.CompilerParams(vmem_limit_bytes=40 * 2**20),
        cost_estimate=pl.CostEstimate(flops=2 * 6 * 27 * cells * channels * channels, bytes_accessed=9 * 2**20, transcendentals=0),
        name="conv_both",
    )(v, u, taps)


def plane_grad_kernel(scale, mine_ref, sibling_ref, *refs):
    u_refs, out_ref, shifted, u_cat = refs[:8], refs[8], refs[9], refs[10]
    lane = lax.broadcasted_iota(jnp.int32, (32, 8, 128), 2)
    row = lax.broadcasted_iota(jnp.int32, (32, 8, 128), 1)
    for half in range(2):
        for z in range(3):
            mine = mine_ref[:, z].reshape(32, 8, 128)
            other = sibling_ref[:, z].reshape(32, 8, 128)
            first = pltpu.roll(mine, (128 - 32 * half) % 128, 2)
            second = pltpu.roll(other, 64 - 32 * half, 2)
            first = jnp.where(lane < 32, first, 0.0)
            second = jnp.where(lane < 32, second, 0.0)
            down_1, down_2 = pltpu.roll(first, 1, 1), pltpu.roll(second, 1, 1)
            up_1, up_2 = pltpu.roll(first, 7, 1), pltpu.roll(second, 7, 1)
            for w, (before, here, after) in enumerate(
                (
                    (jnp.where(row == 0, down_2, down_1), first, jnp.where(row == 7, up_2, up_1)),
                    (jnp.where(row == 0, down_1, down_2), second, jnp.where(row == 7, up_1, up_2)),
                )
            ):
                joined = before + pltpu.roll(here, 32, 2) + pltpu.roll(after, 64, 2)
                plane = 3 * half + z
                shifted[w, plane, pl.ds(1, 32)] = joined
                shifted[w, plane, 0] = joined[31]
                shifted[w, plane, 33] = joined[0]
    for i, u_ref in enumerate(u_refs):
        hi, lo = split(u_ref[...].T)
        u_cat[i, :, 0:256] = hi
        u_cat[i, :, 256:512] = hi
        u_cat[i, :, 512:768] = lo
    windows = [(a, b) for a in range(3) for b in range(3)]
    for first in range(0, 9, 2):
        group = windows[first : first + 2]
        total = jnp.zeros((256, 128 * len(group)), F32)
        for w in range(2):
            for k in range(4):
                cells = [shifted[w, a : a + 4, 8 * k + b : 8 * k + b + 8].reshape(256, 128) for a, b in group]
                cells = jnp.concatenate(cells, axis=1)
                hi, lo = split(cells)
                right = jnp.concatenate([hi, lo, hi], axis=0)
                total += jnp.dot(u_cat[4 * w + k], right, preferred_element_type=F32)
        turned = total.T * scale
        for i, (a, b) in enumerate(group):
            for c in range(3):
                out_ref[9 * a + 3 * b + c] = turned[128 * i + 32 * c : 128 * i + 32 * c + 32]


def plane_grad(mine, sibling, u_blocks, scale):
    return pl.pallas_call(
        functools.partial(plane_grad_kernel, scale),
        out_shape=jax.ShapeDtypeStruct((27, 32, 256), F32),
        in_specs=[pl.BlockSpec(memory_space=pltpu.VMEM)] * 10,
        out_specs=pl.BlockSpec(memory_space=pltpu.VMEM),
        scratch_shapes=[pltpu.VMEM((2, 6, 34, 8, 128), F32), pltpu.VMEM((8, 256, 768), BF16)],
        compiler_params=pltpu.CompilerParams(vmem_limit_bytes=40 * 2**20),
        cost_estimate=pl.CostEstimate(flops=2 * 3 * 27 * 32 * 2048 * 256, bytes_accessed=4 * 2**20, transcendentals=0),
        name="plane_grad",
    )(mine, sibling, *u_blocks)


SWAP = [(0, 1), (1, 0)]
UP = [(i, (i + 1) % 4) for i in range(4)]
DOWN = [((i + 1) % 4, i) for i in range(4)]


def pair(bit):
    return [(i, i ^ bit) for i in range(4)]


def sum_over_dev(x):
    return lax.psum(x, "dev")


def gather_over_ha(x, order):
    first, second = order
    got = lax.ppermute(x, "ha", pair(first))
    both = lax.ppermute(jnp.stack([x, got]), "ha", pair(second))
    return {0: x, first: got, second: both[0], first ^ second: both[1]}


def shared(volume, kernel, upstream):
    h, w = lax.axis_index("ha"), lax.axis_index("wa")
    channels = volume.shape[-1]
    taps = kernel.transpose(1, 0, 2)
    scale = 1.0 / math.sqrt(256 * 32)

    u_flat = upstream.reshape(256, channels)
    u_own = [u_flat] + [lax.ppermute(u_flat, "ha", [((i + k) % 4, i) for i in range(4)]) for k in (1, 2, 3)]
    u_other = [lax.ppermute(x, "wa", SWAP) for x in u_own]

    below = lax.ppermute(volume[3:4], "dev", UP)
    above = lax.ppermute(volume[0:1], "dev", DOWN)
    v_deep = jnp.concatenate([below, volume, above], axis=0)
    parts = v_deep.reshape(2, 192, 2, 4, 32)
    parts = jnp.where(w == 0, parts, parts[:, :, ::-1])
    parts = parts.transpose(3, 1, 2, 0, 4).reshape(4, 192, 128)

    def for_chip(k):
        return lax.dynamic_index_in_dim(parts, lax.rem(h + k, 4), 0, keepdims=False)

    v_own = [for_chip(0)] + [lax.ppermute(for_chip(4 - k), "ha", [((i + k) % 4, i) for i in range(4)]) for k in (1, 2, 3)]
    v_own = jnp.stack(v_own)
    v_other = lax.ppermute(v_own, "wa", SWAP)
    packed = (4, 3, 8, 8, 128)
    piece = plane_grad(v_own.reshape(packed), v_other.reshape(packed), u_own + u_other, scale)

    kernel_grad = jnp.zeros((27, 128, channels), F32)
    for i in range(3):
        whole = sum_over_dev(piece[9 * i : 9 * i + 9])
        for s, x in gather_over_ha(whole, (1, 2) if i % 2 == 0 else (2, 1)).items():
            kernel_grad = lax.dynamic_update_slice(kernel_grad, x, (9 * i, 32 * (h ^ s), 0))
    kernel_grad = kernel_grad.transpose(1, 0, 2)

    behind = lax.ppermute(v_deep[:, 7:8], "ha", UP)
    ahead = lax.ppermute(v_deep[:, 0:1], "ha", DOWN)
    v_rows = jnp.concatenate([behind, v_deep, ahead], axis=1)
    sides = lax.ppermute(jnp.concatenate([v_rows[:, :, 7:8], v_rows[:, :, 0:1]], axis=2), "wa", SWAP)
    v_padded = jnp.concatenate([sides[:, :, 0:1], v_rows, sides[:, :, 1:2]], axis=2)

    def rows(blocks):
        blocks = [x.reshape(4, 8, 8, channels) for x in blocks]
        return jnp.concatenate([blocks[3][:, 7:8], blocks[0], blocks[1][:, 0:1]], axis=1)

    mine, other = rows(u_own), rows(u_other)
    u_flat_padded = jnp.concatenate([other[:, :, 7:8], mine, other[:, :, 0:1]], axis=2)
    u_below = lax.ppermute(u_flat_padded[3:4], "dev", UP)
    u_above = lax.ppermute(u_flat_padded[0:1], "dev", DOWN)
    u_padded = jnp.concatenate([u_below, u_flat_padded, u_above], axis=0)
    output, volume_grad = conv_both(v_padded, u_padded, taps)
    return output.reshape(volume.shape), volume_grad.reshape(volume.shape), kernel_grad


def solution(mesh):
    sizes = tuple(mesh.shape[name] for name in ("dev", "ha", "wa"))
    placed = (P("dev", "ha", "wa", None), P(), P("dev", "ha", "wa", None))

    def per_device(volume, kernel, upstream):
        fits = sizes == (4, 4, 2) and volume.shape == (4, 8, 8, 256) and kernel.shape == (256, 27, 256)
        return (shared if fits else plain)(volume, kernel, upstream)

    return jax.shard_map(
        per_device,
        mesh=mesh,
        in_specs=placed,
        out_specs=(P("dev", "ha", "wa", None), P("dev", "ha", "wa", None), P("wa", None, None)),
        check_vma=False,
    )
```

time: 228 us -> 161 us (0.71)
  waiting for transfers between devices: 119 us -> 82.3 us
  matrix products: 34.8 us -> 0 us
  local copies, waits for them, and re-layouts: 44.1 us -> 17.7 us
  starting transfers between devices: 5.66 us -> 24.1 us
  Pallas kernels: 0 us -> 12.9 us
    psum x1, waiting for transfers between devices: 110 us -> 30.1 us  [sum_over_dev(): return lax.psum(x, 'dev')]
    ppermute x6 -> x24, waiting for transfers between devices: 9.73 us -> 52.1 us  [the longest x3 16.2 us: gather_over_ha(): both = lax.ppermute(jnp.stack([x, got]), 'ha', pair(second))]
    dot_general x3 -> x0, matrix products: 34.8 us -> none  [the longest x1 14.6 us: per_device(): jnp.einsum('ntc,cto->no', forward_patches, kernel, precision=lax.Precisio...]
    unnamed x90 -> x34, local copies, waits for them, and re-layouts: 35 us -> 3.57 us
    ppermute x6 -> x24, starting transfers between devices: 5.62 us -> 24.1 us  [the longest x3 4.6 us: gather_over_ha(): both = lax.ppermute(jnp.stack([x, got]), 'ha', pair(second))]
    pallas_call x0 -> x2, Pallas kernels: none -> 12.9 us  [the longest x1 8.1 us: conv_both(): pl.pallas_call(conv_kernel, grid=(9,), in_specs=[whole, whole, pl.BlockSp...]
    ppermute x0 -> x4, local copies, waits for them, and re-layouts: none -> 5.52 us  [the longest x3 4.29 us: shared(): lax.ppermute(for_chip(4 - k), 'ha', [((i + k) % 4, i) for i in range(4)])]
    another operation x0 -> x7, other arithmetic: none -> 5.01 us  [the longest x2 3.84 us: shifted_3(): return jnp.stack([padded[:, :, c:c + width] for c in range(3)])]
  transfers between devices with their start and end apart: 7 -> 25, of which waited for: 5 -> 14; matrix products, arithmetic and copies ran while one was open for 25% -> 11% of each run, Pallas kernels for 0% -> 5%
where the time goes in v1:
time: 161 us; the launch traced here: 158 us
  waiting for transfers between devices  82.3 us (51%)
  starting transfers between devices  24.1 us (15%)
  local copies, waits for them, and re-layouts  17.7 us (11%)
  between operations  14.5 us (9%)
  Pallas kernels  12.9 us (8%)
  other arithmetic  6.79 us (4%)
    psum x1, waiting for transfers between devices, sum_over_dev(): return lax.psum(x, 'dev')  30.1 us
    ppermute x3, waiting for transfers between devices, gather_over_ha(): both = lax.ppermute(jnp.stack([x, got]), 'ha', pair(second))  16.2 us
    ppermute x3, waiting for transfers between devices, shared(): lax.ppermute(for_chip(4 - k), 'ha', [((i + k) % 4, i) for i in range(4)])  11.4 us
    ppermute x1, waiting for transfers between devices, shared(): u_above = lax.ppermute(u_flat_padded[0:1], 'dev', DOWN)  10.9 us
    pallas_call x1, Pallas kernels, conv_both(): pl.pallas_call(conv_kernel, grid=(9,), in_specs=[whole, whole, pl.BlockSp...  8.1 us
    pallas_call x1, Pallas kernels, plane_grad(): pl.pallas_call(functools.partial(plane_grad_kernel, scale), out_shape=jax...  4.78 us
    ppermute x3, starting transfers between devices, gather_over_ha(): both = lax.ppermute(jnp.stack([x, got]), 'ha', pair(second))  4.6 us
    ppermute x3, local copies, waits for them, and re-layouts, shared(): lax.ppermute(for_chip(4 - k), 'ha', [((i + k) % 4, i) for i in range(4)])  4.29 us
  transfers between devices with their start and end apart: 25, of which 14 were waited for; matrix products, arithmetic and copies ran while one was open for 11% of the time, Pallas kernels for 5%

profile of v1, /device:TPU:8, one launch (start us, length us, event | category | flops | bytes accessed | tf_op | source)
XLA Modules:
  0.0 158.3 jit_solution(16285359816652061985)
XLA Ops:
  8.1 1.6 %collective-permute-start = (f32[1,8,8,256]{3,2,1,0:T(8,128)S(1)}, f32[1,8,8,256]{3,2,1,0:T(8,128)S(1)}, u32[]{:S(2)}, u32[]{:S(2)}) collective-permute-start(f32[1,8,8,256]{3,2,1,0:T(8,128)S(1)} %get-tuple-element.32), channel_id=1, source_target_pairs={{0,8},{8,16},{16,24},{24,0},{1,9},{9,17},{17,25},{25,1},{2,10},{10... | collective-permute-start | bytes 196616 | tf_op jit(solution)/shard_map/ppermute | solution.py:193
  10.2 2.2 %collective-permute-done = f32[1,8,8,256]{3,2,1,0:T(8,128)S(1)} collective-permute-done((f32[1,8,8,256]{3,2,1,0:T(8,128)S(1)}, f32[1,8,8,256]{3,2,1,0:T(8,128)S(1)}, u32[]{:S(2)}, u32[]{:S(2)}) %collective-permute-start) | collective-permute-done | bytes 65568 | tf_op jit(solution)/shard_map/ppermute | solution.py:193
  22.7 1.8 %collective-permute-done.14 = f32[192,128]{0,1:T(8,128)S(1)} collective-permute-done((f32[192,128]{0,1:T(8,128)S(1)}, f32[192,128]{0,1:T(8,128)S(1)}, u32[]{:S(2)}, u32[]{:S(2)}) %collective-permute-start.14) | collective-permute-done | bytes 98336 | tf_op jit(solution)/shard_map/ppermute | solution.py:203
  27.6 9.6 %collective-permute-done.13 = f32[192,128]{0,1:T(8,128)S(1)} collective-permute-done((f32[192,128]{0,1:T(8,128)S(1)}, f32[192,128]{0,1:T(8,128)S(1)}, u32[]{:S(2)}, u32[]{:S(2)}) %collective-permute-start.13) | collective-permute-done | bytes 98336 | tf_op jit(solution)/shard_map/ppermute | solution.py:203
  37.2 3.2 %collective-permute-start.3 = (f32[6,1,8,256]{3,2,1,0:T(8,128)S(1)}, f32[6,1,8,256]{3,2,1,0:T(8,128)S(1)}, u32[]{:S(2)}, u32[]{:S(2)}) collective-permute-start(f32[6,1,8,256]{3,2,1,0:T(8,128)S(1)} %get-tuple-element.28), channel_id=1, source_target_pairs={{2,0},{4,2},{6,4},{0,6},{3,1},{5,3},{7,5},{1,7},{10,8},{12,10},{14... | collective-permute-start | bytes 147464 | tf_op jit(solution)/shard_map/ppermute | solution.py:217
  40.5 1.9 %collective-permute-done.3 = f32[6,1,8,256]{3,2,1,0:T(8,128)S(1)} collective-permute-done((f32[6,1,8,256]{3,2,1,0:T(8,128)S(1)}, f32[6,1,8,256]{3,2,1,0:T(8,128)S(1)}, u32[]{:S(2)}, u32[]{:S(2)}) %collective-permute-start.3) | collective-permute-done | bytes 49184 | tf_op jit(solution)/shard_map/ppermute | solution.py:217
  42.4 3.0 %collective-permute-done.2 = f32[6,1,8,256]{3,2,1,0:T(8,128)S(1)} collective-permute-done((f32[6,1,8,256]{3,2,1,0:T(8,128)S(1)}, f32[6,1,8,256]{3,2,1,0:T(8,128)S(1)}, u32[]{:S(2)}, u32[]{:S(2)}) %collective-permute-start.2) | collective-permute-done | bytes 49184 | tf_op jit(solution)/shard_map/ppermute | solution.py:216
  48.4 1.6 %copy.10 = f32[192,128]{1,0:T(8,128)} copy(f32[192,128]{0,1:T(8,128)} %copy-done.8) | data formatting | bytes 196608 | tf_op jit(solution)/shard_map/ppermute | solution.py:203
  50.0 1.6 %copy.9 = f32[192,128]{1,0:T(8,128)} copy(f32[192,128]{0,1:T(8,128)} %copy-done.9) | data formatting | bytes 196608 | tf_op jit(solution)/shard_map/ppermute | solution.py:203
  54.0 4.8 %plane_grad.1 = f32[27,32,256]{2,1,0:T(8,128)S(1)} custom-call(f32[4,3,8,8,128]{4,3,2,1,0:T(8,128)S(1)} %pad_maximum_fusion.14.mine_ref, f32[4,3,8,8,128]{4,3,2,1,0:T(8,128)S(1)} %bitcast.76, f32[256,256]{1,0:T(8,128)S(1)} %bitcast.75, f32[256,256]{1,0:T(8,128)S(1)} %collective-permute-done.8.refs_1_, f32[256,256]{1,0:T(8,128)S(1)} %collective-permute-done.16.refs_2_, ...), custom_call_target="tpu_custom_call" | custom-call | flops 2717908992 | bytes 4194304 | tf_op jit(solution)/shard_map/plane_grad/pallas_call | solution.py:151
  61.9 1.7 %collective-permute-start.10 = (f32[1,10,10,256]{3,2,1,0:T(8,128)S(1)}, f32[1,10,10,256]{3,2,1,0:T(8,128)S(1)}, u32[]{:S(2)}, u32[]{:S(2)}) collective-permute-start(f32[1,10,10,256]{3,2,1,0:T(8,128)S(1)} %get-tuple-element.25), channel_id=1, source_target_pairs={{0,8},{8,16},{16,24},{24,0},{1,9},{9,17},{17,25},{25,1},{2,10},{10... | collective-permute-start | bytes 307208 | tf_op jit(solution)/shard_map/ppermute | solution.py:228
  63.7 2.1 %fusion.2 = (f32[1,6,10,8,256]{4,3,2,1,0:T(8,128)}, f32[1,6,10,8,256]{4,3,2,1,0:T(8,128)}, f32[1,6,10,8,256]{4,3,2,1,0:T(8,128)}) fusion(f32[6,10,1,256]{3,2,1,0:T(1,128)S(1)} %get-tuple-element.33, f32[6,1,8,256]{3,2,1,0:T(8,128)} %copy-done.12, f32[6,8,8,256]{3,2,1,0:T(8,128)S(1)} %copy-done.2, f32[6,1,8,256]{3,2,1,0:T(8,128)} %copy-done.13, ...), kind=kLoop, calls=%fused_computation.17 | loop fusion | flops 983040 | bytes 2088960 | tf_op jit(solution)/shard_map/stack | solution.py:81
  65.8 10.9 %collective-permute-done.11 = f32[1,10,10,256]{3,2,1,0:T(8,128)S(1)} collective-permute-done((f32[1,10,10,256]{3,2,1,0:T(8,128)S(1)}, f32[1,10,10,256]{3,2,1,0:T(8,128)S(1)}, u32[]{:S(2)}, u32[]{:S(2)}) %collective-permute-start.11) | collective-permute-done | bytes 102432 | tf_op jit(solution)/shard_map/ppermute | solution.py:229
  76.7 2.7 %collective-permute-done.10 = f32[1,10,10,256]{3,2,1,0:T(8,128)S(1)} collective-permute-done((f32[1,10,10,256]{3,2,1,0:T(8,128)S(1)}, f32[1,10,10,256]{3,2,1,0:T(8,128)S(1)}, u32[]{:S(2)}, u32[]{:S(2)}) %collective-permute-start.10) | collective-permute-done | bytes 102432 | tf_op jit(solution)/shard_map/ppermute | solution.py:228
  80.6 30.1 %all-reduce.3.cloned.1.call-done = (f32[9,32,256]{2,1,0:T(8,128)}, f32[9,32,256]{2,1,0:T(8,128)}, f32[9,32,256]{2,1,0:T(8,128)}) async-done(((f32[9,32,256]{2,1,0:T(8,128)}, f32[9,32,256]{2,1,0:T(8,128)}, f32[9,32,256]{2,1,0:T(8,128)}), (f32[9,32,256]{2,1,0:T(8,128)}, f32[9,32,256]{2,1,0:T(8,128)}, f32[9,32,256]{2,1,0:T(8,128)})) %all-reduce.3.cloned.1.call-update) | async-done | bytes 884752 | tf_op jit(solution)/shard_map/psum | solution.py:173
  112.2 2.0 %slice_bitcast_fusion.2 = (f32[1,6,10,8,256]{4,3,2,1,0:T(8,128)S(1)}, f32[1,6,10,8,256]{4,3,2,1,0:T(8,128)S(1)}, f32[1,6,10,8,256]{4,3,2,1,0:T(8,128)S(1)}) fusion(f32[6,10,10,256]{3,2,1,0:T(8,128)} %pad_maximum_fusion.2), kind=kLoop, calls=%fused_computation.11 | loop fusion | bytes 2949120 | tf_op jit(solution)/shard_map/stack | solution.py:81
  114.3 1.7 %pad_maximum_fusion = (f32[3,6,10,8,256]{4,3,2,1,0:T(8,128)S(1)}, f32[3,6,10,8,256]{4,3,2,1,0:T(8,128)S(1)}) fusion(f32[1,6,10,8,256]{4,3,2,1,0:T(8,128)} %get-tuple-element.22, f32[1,6,10,8,256]{4,3,2,1,0:T(8,128)} %get-tuple-element.21, f32[1,6,10,8,256]{4,3,2,1,0:T(8,128)} %get-tuple-element.20, f32[1,6,10,8,256]{4,3,2,1,0:T(8,128)S(1)} %get-tuple-element.11, ...), kind=kLoop, calls=%fused_computation.2 | loop fusion | flops 1474560 | bytes 5898240 | tf_op jit(solution)/shard_map/stack | solution.py:81
  119.8 2.5 %collective-permute-start.19 = (f32[2,9,32,256]{3,2,1,0:T(8,128)S(1)}, f32[2,9,32,256]{3,2,1,0:T(8,128)S(1)}, u32[]{:S(2)}, u32[]{:S(2)}) collective-permute-start(f32[2,9,32,256]{3,2,1,0:T(8,128)S(1)} %pad_maximum_fusion.3), channel_id=1, source_target_pairs={{0,4},{2,6},{4,0},{6,2},{1,5},{3,7},{5,1},{7,3},{8,12},{10,14},{12... | collective-permute-start | bytes 1769480 | tf_op jit(solution)/shard_map/ppermute | solution.py:179
  122.2 8.1 %conv_both.1 = (f32[256,256]{1,0:T(8,128)}, f32[256,256]{1,0:T(8,128)}) custom-call(f32[3,6,10,8,256]{4,3,2,1,0:T(8,128)S(1)} %get-tuple-element.35.v_ref, f32[3,6,10,8,256]{4,3,2,1,0:T(8,128)S(1)} %get-tuple-element.36.u_ref, f32[27,256,256]{2,1,0:T(8,128)S(1)} %bitcast.84), custom_call_target="tpu_custom_call" | custom-call | flops 5435817984 | bytes 9437184 | tf_op jit(solution)/shard_map/conv_both/pallas_call | solution.py:91
  130.8 1.7 %collective-permute-start.21 = (f32[2,9,32,256]{3,2,1,0:T(8,128)S(1)}, f32[2,9,32,256]{3,2,1,0:T(8,128)S(1)}, u32[]{:S(2)}, u32[]{:S(2)}) collective-permute-start(f32[2,9,32,256]{3,2,1,0:T(8,128)S(1)} %pad_maximum_fusion.4), channel_id=1, source_target_pairs={{0,2},{2,0},{4,6},{6,4},{1,3},{3,1},{5,7},{7,5},{8,10},{10,8},{12,... | collective-permute-start | bytes 1769480 | tf_op jit(solution)/shard_map/ppermute | solution.py:179
  133.1 5.5 %collective-permute-done.19 = f32[2,9,32,256]{3,2,1,0:T(8,128)S(1)} collective-permute-done((f32[2,9,32,256]{3,2,1,0:T(8,128)S(1)}, f32[2,9,32,256]{3,2,1,0:T(8,128)S(1)}, u32[]{:S(2)}, u32[]{:S(2)}) %collective-permute-start.19) | collective-permute-done | bytes 589856 | tf_op jit(solution)/shard_map/ppermute | solution.py:179
  138.7 4.7 %collective-permute-done.21 = f32[2,9,32,256]{3,2,1,0:T(8,128)S(1)} collective-permute-done((f32[2,9,32,256]{3,2,1,0:T(8,128)S(1)}, f32[2,9,32,256]{3,2,1,0:T(8,128)S(1)}, u32[]{:S(2)}, u32[]{:S(2)}) %collective-permute-start.21) | collective-permute-done | bytes 589856 | tf_op jit(solution)/shard_map/ppermute | solution.py:179
  143.5 6.0 %collective-permute-done.23 = f32[2,9,32,256]{3,2,1,0:T(8,128)S(1)} collective-permute-done((f32[2,9,32,256]{3,2,1,0:T(8,128)S(1)}, f32[2,9,32,256]{3,2,1,0:T(8,128)S(1)}, u32[]{:S(2)}, u32[]{:S(2)}) %collective-permute-start.23) | collective-permute-done | bytes 589856 | tf_op jit(solution)/shard_map/ppermute | solution.py:179
  149.6 1.8 %copy-done.3 = f32[27,128,256]{2,1,0:T(8,128)} copy-done((f32[27,128,256]{2,1,0:T(8,128)}, f32[27,128,256]{2,1,0:T(8,128)S(1)}, u32[]{:S(2)}) %copy-start.3) | copy-done | bytes 3538968
  (109 shorter events, 30.7 us)
Async XLA Ops:
  7.2 103.6 %all-reduce.3.cloned.1.call-start = ((), (), s32[]{:S(2)}) async-start(), calls=%async_computation | async-start | bytes 1769472 | tf_op jit(solution)/shard_map/psum | solution.py:173
  8.1 4.3 %collective-permute-start = (f32[1,8,8,256]{3,2,1,0:T(8,128)S(1)}, f32[1,8,8,256]{3,2,1,0:T(8,128)S(1)}, u32[]{:S(2)}, u32[]{:S(2)}) collective-permute-start(f32[1,8,8,256]{3,2,1,0:T(8,128)S(1)} %get-tuple-element.32), channel_id=1, source_target_pairs={{0,8},{8,16},{16,24},{24,0},{1,9},{9,17},{17,25},{25,1},{2,10},{10... | collective-permute-start | bytes 196616 | tf_op jit(solution)/shard_map/ppermute | solution.py:193
  9.7 4.5 %collective-permute-start.1 = (f32[1,8,8,256]{3,2,1,0:T(8,128)S(1)}, f32[1,8,8,256]{3,2,1,0:T(8,128)S(1)}, u32[]{:S(2)}, u32[]{:S(2)}) collective-permute-start(f32[1,8,8,256]{3,2,1,0:T(8,128)S(1)} %get-tuple-element.31), channel_id=1, source_target_pairs={{8,0},{16,8},{24,16},{0,24},{9,1},{17,9},{25,17},{1,25},{10,2},{18... | collective-permute-start | bytes 196616 | tf_op jit(solution)/shard_map/ppermute | solution.py:194
  17.1 7.4 %collective-permute-start.14 = (f32[192,128]{0,1:T(8,128)S(1)}, f32[192,128]{0,1:T(8,128)S(1)}, u32[]{:S(2)}, u32[]{:S(2)}) collective-permute-start(f32[192,128]{0,1:T(8,128)S(1)} %get-tuple-element.17), channel_id=1, source_target_pairs={{6,0},{0,2},{2,4},{4,6},{7,1},{1,3},{3,5},{5,7},{14,8},{8,10},{10,... | collective-permute-start | bytes 294920 | tf_op jit(solution)/shard_map/ppermute | solution.py:203
  18.7 26.8 %collective-permute-start.8 = (f32[256,256]{1,0:T(8,128)S(1)}, f32[256,256]{1,0:T(8,128)S(1)}, u32[]{:S(2)}, u32[]{:S(2)}) collective-permute-start(f32[256,256]{1,0:T(8,128)S(1)} %bitcast.71), channel_id=1, source_target_pairs={{2,0},{4,2},{6,4},{0,6},{3,1},{5,3},{7,5},{1,7},{10,8},{12,10},{14... | collective-permute-start | bytes 786440 | tf_op jit(solution)/shard_map/ppermute | solution.py:190
  20.1 26.0 %collective-permute-start.5 = (f32[256,256]{1,0:T(8,128)S(1)}, f32[256,256]{1,0:T(8,128)S(1)}, u32[]{:S(2)}, u32[]{:S(2)}) collective-permute-start(f32[256,256]{1,0:T(8,128)S(1)} %bitcast.72), channel_id=1, source_target_pairs={{6,0},{0,2},{2,4},{4,6},{7,1},{1,3},{3,5},{5,7},{14,8},{8,10},{10,... | collective-permute-start | bytes 786440 | tf_op jit(solution)/shard_map/ppermute | solution.py:190
  20.7 25.5 %collective-permute-start.16 = (f32[256,256]{1,0:T(8,128)S(1)}, f32[256,256]{1,0:T(8,128)S(1)}, u32[]{:S(2)}, u32[]{:S(2)}) collective-permute-start(f32[256,256]{1,0:T(8,128)S(1)} %bitcast.73), channel_id=1, source_target_pairs={{4,0},{6,2},{0,4},{2,6},{5,1},{7,3},{1,5},{3,7},{12,8},{14,10},{8,... | collective-permute-start | bytes 786440 | tf_op jit(solution)/shard_map/ppermute | solution.py:190
  22.2 15.0 %collective-permute-start.13 = (f32[192,128]{0,1:T(8,128)S(1)}, f32[192,128]{0,1:T(8,128)S(1)}, u32[]{:S(2)}, u32[]{:S(2)}) collective-permute-start(f32[192,128]{0,1:T(8,128)S(1)} %get-tuple-element.18), channel_id=1, source_target_pairs={{4,0},{6,2},{0,4},{2,6},{5,1},{7,3},{1,5},{3,7},{12,8},{14,10},{8,... | collective-permute-start | bytes 294920 | tf_op jit(solution)/shard_map/ppermute | solution.py:203
  24.5 15.9 %collective-permute-start.12 = (f32[192,128]{0,1:T(8,128)S(1)}, f32[192,128]{0,1:T(8,128)S(1)}, u32[]{:S(2)}, u32[]{:S(2)}) collective-permute-start(f32[192,128]{0,1:T(8,128)S(1)} %get-tuple-element.19), channel_id=1, source_target_pairs={{2,0},{4,2},{6,4},{0,6},{3,1},{5,3},{7,5},{1,7},{10,8},{12,10},{14... | collective-permute-start | bytes 294920 | tf_op jit(solution)/shard_map/ppermute | solution.py:203
  37.2 5.2 %collective-permute-start.3 = (f32[6,1,8,256]{3,2,1,0:T(8,128)S(1)}, f32[6,1,8,256]{3,2,1,0:T(8,128)S(1)}, u32[]{:S(2)}, u32[]{:S(2)}) collective-permute-start(f32[6,1,8,256]{3,2,1,0:T(8,128)S(1)} %get-tuple-element.28), channel_id=1, source_target_pairs={{2,0},{4,2},{6,4},{0,6},{3,1},{5,3},{7,5},{1,7},{10,8},{12,10},{14... | collective-permute-start | bytes 147464 | tf_op jit(solution)/shard_map/ppermute | solution.py:217
  40.4 5.0 %collective-permute-start.2 = (f32[6,1,8,256]{3,2,1,0:T(8,128)S(1)}, f32[6,1,8,256]{3,2,1,0:T(8,128)S(1)}, u32[]{:S(2)}, u32[]{:S(2)}) collective-permute-start(f32[6,1,8,256]{3,2,1,0:T(8,128)S(1)} %get-tuple-element.27), channel_id=1, source_target_pairs={{0,2},{2,4},{4,6},{6,0},{1,3},{3,5},{5,7},{7,1},{8,10},{10,12},{12... | collective-permute-start | bytes 147464 | tf_op jit(solution)/shard_map/ppermute | solution.py:216
  42.4 11.5 %collective-permute-start.7 = (f32[256,256]{1,0:T(8,128)S(1)}, f32[256,256]{1,0:T(8,128)S(1)}, u32[]{:S(2)}, u32[]{:S(2)}) collective-permute-start(f32[256,256]{1,0:T(8,128)S(1)} %bitcast.74), channel_id=1, source_target_pairs={{0,1},{1,0},{2,3},{3,2},{4,5},{5,4},{6,7},{7,6},{8,9},{9,8},{10,11... | collective-permute-start | bytes 786440 | tf_op jit(solution)/shard_map/ppermute | solution.py:191
  45.4 7.3 %collective-permute-start.15 = (f32[4,192,128]{1,2,0:T(8,128)S(1)}, f32[4,192,128]{1,2,0:T(8,128)}, u32[]{:S(2)}, u32[]{:S(2)}) collective-permute-start(f32[4,192,128]{1,2,0:T(8,128)S(1)} %pad_maximum_fusion.6), channel_id=1, source_target_pairs={{0,1},{1,0},{2,3},{3,2},{4,5},{5,4},{6,7},{7,6},{8,9},{9,8},{10,11... | collective-permute-start | bytes 1179656 | tf_op jit(solution)/shard_map/ppermute | solution.py:205
  45.5 8.5 %collective-permute-start.9 = (f32[256,256]{1,0:T(8,128)S(1)}, f32[256,256]{1,0:T(8,128)S(1)}, u32[]{:S(2)}, u32[]{:S(2)}) collective-permute-start(f32[256,256]{1,0:T(8,128)S(1)} %collective-permute-done.8.refs_1_), channel_id=1, source_target_pairs={{0,1},{1,0},{2,3},{3,2},{4,5},{5,4},{6,7},{7,6},{8,9},{9,8},{10,11... | collective-permute-start | bytes 786440 | tf_op jit(solution)/shard_map/ppermute | solution.py:191
  46.1 7.9 %collective-permute-start.6 = (f32[256,256]{1,0:T(8,128)S(1)}, f32[256,256]{1,0:T(8,128)S(1)}, u32[]{:S(2)}, u32[]{:S(2)}) collective-permute-start(f32[256,256]{1,0:T(8,128)S(1)} %collective-permute-done.5.refs_3_), channel_id=1, source_target_pairs={{0,1},{1,0},{2,3},{3,2},{4,5},{5,4},{6,7},{7,6},{8,9},{9,8},{10,11... | collective-permute-start | bytes 786440 | tf_op jit(solution)/shard_map/ppermute | solution.py:191
  46.2 7.8 %collective-permute-start.17 = (f32[256,256]{1,0:T(8,128)S(1)}, f32[256,256]{1,0:T(8,128)S(1)}, u32[]{:S(2)}, u32[]{:S(2)}) collective-permute-start(f32[256,256]{1,0:T(8,128)S(1)} %collective-permute-done.16.refs_2_), channel_id=1, source_target_pairs={{0,1},{1,0},{2,3},{3,2},{4,5},{5,4},{6,7},{7,6},{8,9},{9,8},{10,11... | collective-permute-start | bytes 786440 | tf_op jit(solution)/shard_map/ppermute | solution.py:191
  61.6 15.2 %collective-permute-start.11 = (f32[1,10,10,256]{3,2,1,0:T(8,128)S(1)}, f32[1,10,10,256]{3,2,1,0:T(8,128)S(1)}, u32[]{:S(2)}, u32[]{:S(2)}) collective-permute-start(f32[1,10,10,256]{3,2,1,0:T(8,128)S(1)} %get-tuple-element.26), channel_id=1, source_target_pairs={{8,0},{16,8},{24,16},{0,24},{9,1},{17,9},{25,17},{1,25},{10,2},{18... | collective-permute-start | bytes 307208 | tf_op jit(solution)/shard_map/ppermute | solution.py:229
  61.9 17.5 %collective-permute-start.10 = (f32[1,10,10,256]{3,2,1,0:T(8,128)S(1)}, f32[1,10,10,256]{3,2,1,0:T(8,128)S(1)}, u32[]{:S(2)}, u32[]{:S(2)}) collective-permute-start(f32[1,10,10,256]{3,2,1,0:T(8,128)S(1)} %get-tuple-element.25), channel_id=1, source_target_pairs={{0,8},{8,16},{16,24},{24,0},{1,9},{9,17},{17,25},{25,1},{2,10},{10... | collective-permute-start | bytes 307208 | tf_op jit(solution)/shard_map/ppermute | solution.py:228
  110.7 9.0 %collective-permute-start.18 = (f32[9,32,256]{2,1,0:T(8,128)}, f32[9,32,256]{2,1,0:T(8,128)S(1)}, u32[]{:S(2)}, u32[]{:S(2)}) collective-permute-start(f32[9,32,256]{2,1,0:T(8,128)} %get-tuple-element.7), channel_id=1, source_target_pairs={{0,2},{2,0},{4,6},{6,4},{1,3},{3,1},{5,7},{7,5},{8,10},{10,8},{12,... | collective-permute-start | bytes 884744 | tf_op jit(solution)/shard_map/ppermute | solution.py:178
  116.0 14.8 %collective-permute-start.20 = (f32[9,32,256]{2,1,0:T(8,128)S(1)}, f32[9,32,256]{2,1,0:T(8,128)S(1)}, u32[]{:S(2)}, u32[]{:S(2)}) collective-permute-start(f32[9,32,256]{2,1,0:T(8,128)S(1)} %copy-done.5), channel_id=1, source_target_pairs={{0,4},{2,6},{4,0},{6,2},{1,5},{3,7},{5,1},{7,3},{8,12},{10,14},{12... | collective-permute-start | bytes 884744 | tf_op jit(solution)/shard_map/ppermute | solution.py:178
  117.5 15.1 %collective-permute-start.22 = (f32[9,32,256]{2,1,0:T(8,128)S(1)}, f32[9,32,256]{2,1,0:T(8,128)S(1)}, u32[]{:S(2)}, u32[]{:S(2)}) collective-permute-start(f32[9,32,256]{2,1,0:T(8,128)S(1)} %copy-done.4), channel_id=1, source_target_pairs={{0,2},{2,0},{4,6},{6,4},{1,3},{3,1},{5,7},{7,5},{8,10},{10,8},{12,... | collective-permute-start | bytes 884744 | tf_op jit(solution)/shard_map/ppermute | solution.py:178
  119.8 18.8 %collective-permute-start.19 = (f32[2,9,32,256]{3,2,1,0:T(8,128)S(1)}, f32[2,9,32,256]{3,2,1,0:T(8,128)S(1)}, u32[]{:S(2)}, u32[]{:S(2)}) collective-permute-start(f32[2,9,32,256]{3,2,1,0:T(8,128)S(1)} %pad_maximum_fusion.3), channel_id=1, source_target_pairs={{0,4},{2,6},{4,0},{6,2},{1,5},{3,7},{5,1},{7,3},{8,12},{10,14},{12... | collective-permute-start | bytes 1769480 | tf_op jit(solution)/shard_map/ppermute | solution.py:179
  130.8 12.6 %collective-permute-start.21 = (f32[2,9,32,256]{3,2,1,0:T(8,128)S(1)}, f32[2,9,32,256]{3,2,1,0:T(8,128)S(1)}, u32[]{:S(2)}, u32[]{:S(2)}) collective-permute-start(f32[2,9,32,256]{3,2,1,0:T(8,128)S(1)} %pad_maximum_fusion.4), channel_id=1, source_target_pairs={{0,2},{2,0},{4,6},{6,4},{1,3},{3,1},{5,7},{7,5},{8,10},{10,8},{12,... | collective-permute-start | bytes 1769480 | tf_op jit(solution)/shard_map/ppermute | solution.py:179
  132.6 16.9 %collective-permute-start.23 = (f32[2,9,32,256]{3,2,1,0:T(8,128)S(1)}, f32[2,9,32,256]{3,2,1,0:T(8,128)S(1)}, u32[]{:S(2)}, u32[]{:S(2)}) collective-permute-start(f32[2,9,32,256]{3,2,1,0:T(8,128)S(1)} %pad_maximum_fusion.5), channel_id=1, source_target_pairs={{0,4},{2,6},{4,0},{6,2},{1,5},{3,7},{5,1},{7,3},{8,12},{10,14},{12... | collective-permute-start | bytes 1769480 | tf_op jit(solution)/shard_map/ppermute | solution.py:179
  (17 other events, 164.0 us)
Sparse Core Ops, SparseCore 0:
  59.9 50.8 all-reduce.2

commit v2 on v1

v2 whole, which is shorter than its diff:
```python
import functools
import math

import jax
import jax.numpy as jnp
from jax import lax
from jax.experimental import pallas as pl
from jax.experimental.pallas import tpu as pltpu
from jax.sharding import PartitionSpec as P

F32, BF16 = jnp.float32, jnp.bfloat16


def split(x):
    hi = x.astype(BF16)
    return hi, (x - hi.astype(F32)).astype(BF16)


def padded_by_halo(shard, sides):
    for axis, dim in sides:
        count, length = lax.axis_size(axis), shard.shape[dim]
        up = [(i, (i + 1) % count) for i in range(count)]
        down = [(j, i) for i, j in up]
        before = lax.ppermute(lax.slice_in_dim(shard, length - 1, length, axis=dim), axis, up)
        after = lax.ppermute(lax.slice_in_dim(shard, 0, 1, axis=dim), axis, down)
        shard = jnp.concatenate([before, shard, after], axis=dim)
    return shard


def plain(volume, kernel, upstream):
    depth, height, width, channels = volume.shape
    cells = depth * height * width
    padded = padded_by_halo(jnp.stack([volume, upstream]), (("dev", 1), ("ha", 2), ("wa", 3)))

    def windows(which, sign):
        return jnp.stack(
            [
                padded[which, 1 + sign * a :, 1 + sign * b :, 1 + sign * c :][:depth, :height, :width].reshape(cells, channels)
                for a in (-1, 0, 1) for b in (-1, 0, 1) for c in (-1, 0, 1)
            ],
            axis=1,
        )

    dot = functools.partial(jnp.einsum, precision=lax.Precision.HIGHEST, preferred_element_type=F32)
    forward, backward = windows(0, 1), windows(1, -1)
    output = dot("ntc,cto->no", forward, kernel)
    volume_grad = dot("nto,cto->nc", backward, kernel)
    total = cells * lax.axis_size("dev") * lax.axis_size("ha") * lax.axis_size("wa")
    summed = lax.psum(dot("ntc,no->cto", forward, upstream.reshape(cells, channels)) * (1.0 / math.sqrt(total)), ("dev", "ha", "wa"))
    owned = channels // lax.axis_size("wa")
    kernel_grad = lax.dynamic_slice_in_dim(summed, lax.axis_index("wa") * owned, owned, 0)
    return output.reshape(volume.shape), volume_grad.reshape(volume.shape), kernel_grad


def conv_kernel(a, *refs):
    v_refs, u_refs, k_ref, out_ref, grad_ref = refs[:3], refs[3:6], refs[6], refs[-2], refs[-1]
    b = pl.program_id(0)

    @pl.when(b == 0)
    def _():
        out_ref[...] = refs[7][...] if a else jnp.zeros_like(out_ref)
        grad_ref[...] = refs[8][...] if a else jnp.zeros_like(grad_ref)

    cells, channels = out_ref.shape
    d, h = v_refs[0].shape[0] - 2, v_refs[0].shape[1] - 2
    out, grad = out_ref[...], grad_ref[...]
    for c in range(3):
        k_hi, k_lo = split(k_ref[c])
        v_hi, v_lo = split(v_refs[c][a : a + d, pl.ds(b, h)].reshape(cells, channels))
        u_hi, u_lo = split(u_refs[2 - c][2 - a : 2 - a + d, pl.ds(2 - b, h)].reshape(cells, channels))
        for left, right in ((v_hi, k_hi), (v_hi, k_lo), (v_lo, k_hi)):
            out += jnp.dot(left, right, preferred_element_type=F32)
        for left, right in ((u_hi, k_hi), (u_hi, k_lo), (u_lo, k_hi)):
            grad += lax.dot_general(left, right, (((1,), (1,)), ((), ())), preferred_element_type=F32)
    out_ref[...] = out
    grad_ref[...] = grad


def shifted_3(padded):
    width = padded.shape[2] - 2
    return [padded[:, :, c : c + width] for c in range(3)]


def conv_third(a, windows, taps, before=()):
    planes, rows, width, channels = windows[0].shape
    cells = (planes - 2) * (rows - 2) * width
    whole = pl.BlockSpec((planes, rows, width, channels), lambda i: (0,) * 4)
    result = pl.BlockSpec((cells, channels), lambda i: (0, 0))
    shape = jax.ShapeDtypeStruct((cells, channels), F32)
    return pl.pallas_call(
        functools.partial(conv_kernel, a),
        grid=(3,),
        in_specs=[whole] * 6 + [pl.BlockSpec((3, channels, channels), lambda i: (3 * a + i, 0, 0))] + [result] * len(before),
        out_specs=[result, result],
        out_shape=[shape, shape],
        compiler_params=pltpu.CompilerParams(vmem_limit_bytes=40 * 2**20),
        cost_estimate=pl.CostEstimate(flops=2 * 6 * 9 * cells * channels * channels, bytes_accessed=4 * 2**20, transcendentals=0),
        name=f"conv_{a}",
    )(*windows, taps, *before)


def packed(two, h, w):
    lane = lax.broadcasted_iota(jnp.int32, (64, 128), 1)
    total = jnp.zeros((64, 128), F32)
    for i, x in enumerate(two):
        left, right = x[:, :128], x[:, 128:]
        for j, tile in enumerate((jnp.where(w == 0, left, right), jnp.where(w == 0, right, left))):
            turned = pltpu.roll(tile, lax.rem(32 * (2 * i + j) + 128 - 32 * h, 128), 1)
            total = jnp.where(lane // 32 == 2 * i + j, turned, total)
    return total


def messages_kernel(*refs):
    h, w = lax.axis_index("ha"), lax.axis_index("wa")
    v_ref, u_ref, out_refs = refs[0], refs[1], refs[2:]
    for k, out_ref in enumerate(out_refs):
        chip = lax.rem(h + k, 4)
        out_ref[0:256] = u_ref[...]
        for t in range(2):
            out_ref[256:320, 128 * t : 128 * t + 128] = packed((v_ref[2 * t], v_ref[2 * t + 1]), chip, w)


def ends_kernel(*refs):
    h, w = lax.axis_index("ha"), lax.axis_index("wa")
    below_ref, above_ref, out_refs = refs[0], refs[1], refs[2:]
    for k, out_ref in enumerate(out_refs):
        out_ref[...] = packed((below_ref[0], above_ref[0]), lax.rem(h + k, 4), w)


def for_chips(body, shape, *arrays):
    vmem = pl.BlockSpec(memory_space=pltpu.VMEM)
    return pl.pallas_call(
        body,
        out_shape=[jax.ShapeDtypeStruct(shape, F32)] * 4,
        in_specs=[vmem] * len(arrays),
        out_specs=[vmem] * 4,
        name=body.__name__,
    )(*arrays)


def lay_out(shifted, plane, first, second):
    lane = lax.broadcasted_iota(jnp.int32, (32, 8, 128), 2)
    row = lax.broadcasted_iota(jnp.int32, (32, 8, 128), 1)
    first = jnp.where(lane < 32, first, 0.0)
    second = jnp.where(lane < 32, second, 0.0)
    down_1, down_2 = pltpu.roll(first, 1, 1), pltpu.roll(second, 1, 1)
    up_1, up_2 = pltpu.roll(first, 7, 1), pltpu.roll(second, 7, 1)
    for w, (before, here, after) in enumerate(
        (
            (jnp.where(row == 0, down_2, down_1), first, jnp.where(row == 7, up_2, up_1)),
            (jnp.where(row == 0, down_1, down_2), second, jnp.where(row == 7, up_1, up_2)),
        )
    ):
        joined = before + pltpu.roll(here, 32, 2) + pltpu.roll(after, 64, 2)
        shifted[w, plane, pl.ds(1, 32)] = joined
        shifted[w, plane, 0] = joined[31]
        shifted[w, plane, 33] = joined[0]


def plane_of(refs, z, offset):
    tile = 128 * (z // 2)
    plane = jnp.concatenate([ref[256:320, tile : tile + 128].reshape(8, 8, 128) for ref in refs], axis=0)
    return pltpu.roll(plane, (128 - 64 * (z % 2) - offset) % 128, 2)


def plane_grad_kernel(scale, planes, pieces, *refs):
    mine, other = refs[:4], refs[4:8]
    out_refs, shifted, u_cat = refs[-2 - pieces : -2], refs[-2], refs[-1]
    share = out_refs[0].shape[0]
    for z in range(4):
        lay_out(shifted, z + 1, plane_of(mine, z, 0), plane_of(other, z, 32))
    if planes != (1,):
        own_halo, other_halo = (ref[...].reshape(32, 8, 128) for ref in refs[8:10])
        for i, z in enumerate((0, 5)):
            lay_out(shifted, z, pltpu.roll(own_halo, (128 - 64 * i) % 128, 2), pltpu.roll(other_halo, 96 - 64 * i, 2))
    for i, ref in enumerate(mine + other):
        hi, lo = split(ref[0:256].T)
        u_cat[i, :, 0:256] = hi
        u_cat[i, :, 256:512] = hi
        u_cat[i, :, 512:768] = lo
    windows = [(a, b) for a in planes for b in range(3)]
    for start in range(0, len(windows), 2):
        group = windows[start : start + 2]
        total = jnp.zeros((256, 128 * len(group)), F32)
        for w in range(2):
            for k in range(4):
                cells = [shifted[w, a : a + 4, 8 * k + b : 8 * k + b + 8].reshape(256, 128) for a, b in group]
                hi, lo = split(jnp.concatenate(cells, axis=1))
                right = jnp.concatenate([hi, lo, hi], axis=0)
                total += jnp.dot(u_cat[4 * w + k], right, preferred_element_type=F32)
        turned = total.T * scale
        for i in range(len(group)):
            for c in range(3):
                tap = 3 * (start + i) + c
                out_refs[tap // share][tap % share] = turned[128 * i + 32 * c : 128 * i + 32 * c + 32]


def plane_grad(scale, planes, pieces, messages, halo=()):
    vmem = pl.BlockSpec(memory_space=pltpu.VMEM)
    shapes = [jax.ShapeDtypeStruct((9 * len(planes) // pieces, 32, 256), F32)] * pieces
    return pl.pallas_call(
        functools.partial(plane_grad_kernel, scale, planes, pieces),
        out_shape=shapes,
        in_specs=[vmem] * (8 + len(halo)),
        out_specs=[vmem] * len(shapes),
        scratch_shapes=[pltpu.VMEM((2, 6, 34, 8, 128), F32), pltpu.VMEM((8, 256, 768), BF16)],
        compiler_params=pltpu.CompilerParams(vmem_limit_bytes=40 * 2**20),
        cost_estimate=pl.CostEstimate(flops=2 * 3 * 9 * len(planes) * 32 * 2048 * 256, bytes_accessed=4 * 2**20, transcendentals=0),
        name=f"plane_grad_{len(planes)}",
    )(*messages, *halo)


SWAP = [(0, 1), (1, 0)]
UP = [(i, (i + 1) % 4) for i in range(4)]
DOWN = [((i + 1) % 4, i) for i in range(4)]


def pair(bit):
    return [(i, i ^ bit) for i in range(4)]


INWARDS, MIDDLE, OUTWARDS = [(0, 1), (3, 2)], [(1, 2), (2, 1)], [(1, 0), (2, 3)]


def together(*arrays):
    return lax.optimization_barrier(arrays)


def to(x, axis, where):
    return lax.ppermute(x, axis, where)


def shared(volume, kernel, upstream):
    h, w = lax.axis_index("ha"), lax.axis_index("wa")
    channels = volume.shape[-1]
    taps = kernel.transpose(1, 0, 2)
    scale = 1.0 / math.sqrt(256 * 32)

    z = lax.axis_index("dev")
    end = (z == 0) | (z == 3)
    x_bit, y_bit = lax.rem(h, 2), h // 2

    def around(messages):
        return [messages[0]] + [to(messages[4 - k], "ha", [((i + k) % 4, i) for i in range(4)]) for k in (1, 2, 3)]

    mine = around(for_chips(messages_kernel, (320, channels), volume.reshape(4, 64, channels), upstream.reshape(256, channels)))
    other = [to(mine[0], "wa", SWAP)]

    volume, upstream, _ = together(volume, upstream, other[0])
    below = to(jnp.stack([volume[3], upstream[3]]), "dev", UP)
    above = to(jnp.stack([volume[0], upstream[0]]), "dev", DOWN)
    ends = for_chips(ends_kernel, (64, 128), below.reshape(2, 64, channels), above.reshape(2, 64, channels))
    *arrived, _ = together(*mine[1:], ends[0])
    mine = mine[:1] + arrived
    other += [to(x, "wa", SWAP) for x in arrived]
    own_halo = around(ends)
    *arrived, _ = together(*mine, *other, *own_halo)
    mine, other = arrived[:4], arrived[4:8]
    own_halo = jnp.stack(own_halo)
    other_halo = to(own_halo, "wa", SWAP)

    (a0,) = plane_grad(scale, (1,), 1, mine + other)
    a1 = to(a0, "dev", INWARDS)
    b0, c0 = plane_grad(scale, (0, 2), 2, mine + other, (own_halo, other_halo))
    b1, c1 = to(b0, "dev", INWARDS), to(c0, "dev", INWARDS)
    a0, _ = together(a0 + a1, b0)
    a1 = to(a0, "dev", MIDDLE)

    def edge(row):
        return jnp.concatenate([below[:, row : row + 1], volume[:, row : row + 1], above[:, row : row + 1]], axis=0)

    low_edge, high_edge, _ = together(edge(0), edge(7), c0)
    behind, ahead = to(high_edge, "ha", UP), to(low_edge, "ha", DOWN)
    a1, b1, behind, ahead = together(a1, b1, behind, ahead)
    a0, b0 = a0 + a1, b0 + b1

    a1, b1 = to(a0, "dev", OUTWARDS), to(b0, "dev", MIDDLE)
    deep = jnp.concatenate([below, volume, above], axis=0)
    rows = jnp.concatenate([behind, deep, ahead], axis=1)
    v_rows = jnp.concatenate([rows[0:1], rows[2:7]], axis=0)
    u_own = [x[:256].reshape(4, 8, 8, channels) for x in mine]
    u_rows = jnp.concatenate([u_own[3][:, 7:8], u_own[0], u_own[1][:, 0:1]], axis=1)
    u_rows = jnp.concatenate([rows[1:2], u_rows, rows[7:8]], axis=0)
    both = jnp.concatenate([v_rows, u_rows], axis=0)
    sides = to(jnp.concatenate([both[:, :, 7:8], both[:, :, 0:1]], axis=2), "wa", SWAP)
    both = jnp.concatenate([sides[:, :, 0:1], both, sides[:, :, 1:2]], axis=2)
    windows = shifted_3(both[:6]) + shifted_3(both[6:])
    a1, b1, c1, *windows = together(a1, b1, c1, *windows)
    a0, b0, c0 = jnp.where(end, a1, a0), b0 + b1, c0 + c1

    def first_half(x):
        return to(x[:5], "ha", pair(1)), to(x[5:], "ha", pair(2))

    def joined(x, got):
        along_x, along_y = ([x[:5], got[0]], 2, x_bit), ([x[5:], got[1]], 1, y_bit)
        both = []
        for (own, other), axis, bit in (along_x, along_y):
            own, other = (jnp.expand_dims(t, (1, 2)) for t in (own, other))
            both.append(jnp.where(bit == 0, jnp.concatenate([own, other], axis), jnp.concatenate([other, own], axis)))
        return both

    def second_half(x):
        return to(x[0], "ha", pair(2)), to(x[1], "ha", pair(1))

    def placed(total, tap, x, far):
        for part, y in ((x[0], y_bit), (far[0], 1 - y_bit)):
            total = lax.dynamic_update_slice(total, part, (tap, y, 0, 0, 0))
        for part, x in ((x[1], x_bit), (far[1], 1 - x_bit)):
            total = lax.dynamic_update_slice(total, part, (tap + 5, 0, x, 0, 0))
        return total

    conv = conv_third(0, windows, taps)
    a_got = first_half(a0)
    a0, a1, a2, b1, c1, *conv = together(a0, *a_got, to(b0, "dev", OUTWARDS), to(c0, "dev", MIDDLE), *conv)
    b0, c0, a0 = jnp.where(end, b1, b0), c0 + c1, joined(a0, (a1, a2))

    a_far = second_half(a0)
    conv = conv_third(1, windows, taps, conv)
    b_got = first_half(b0)
    b0, b1, b2, c1, *conv = together(b0, *b_got, to(c0, "dev", OUTWARDS), *conv)
    c0, b0 = jnp.where(end, c1, c0), joined(b0, (b1, b2))

    b_far = second_half(b0)
    conv = conv_third(2, windows, taps, conv)
    c_got = first_half(c0)
    c0, c1, c2, *conv = together(c0, *c_got, *conv)
    c0 = joined(c0, (c1, c2))
    c_far = second_half(c0)

    kernel_grad = jnp.zeros((27, 2, 2, 32, channels), F32)
    kernel_grad = placed(kernel_grad, 9, a0, a_far)
    kernel_grad = placed(kernel_grad, 0, b0, b_far)
    kernel_grad = placed(kernel_grad, 18, c0, c_far)
    output, volume_grad = conv
    return output.reshape(volume.shape), volume_grad.reshape(volume.shape), kernel_grad.reshape(27, 128, channels).transpose(1, 0, 2)


def solution(mesh):
    sizes = tuple(mesh.shape[name] for name in ("dev", "ha", "wa"))
    placed = (P("dev", "ha", "wa", None), P(), P("dev", "ha", "wa", None))

    def per_device(volume, kernel, upstream):
        fits = sizes == (4, 4, 2) and volume.shape == (4, 8, 8, 256) and kernel.shape == (256, 27, 256)
        return (shared if fits else plain)(volume, kernel, upstream)

    return jax.shard_map(
        per_device,
        mesh=mesh,
        in_specs=placed,
        out_specs=(P("dev", "ha", "wa", None), P("dev", "ha", "wa", None), P("wa", None, None)),
        check_vma=False,
    )
```

time: 161 us -> 119 us (0.74); the launches traced: 158 us -> 118 us
  waiting for transfers between devices: 82.3 us -> 45.7 us
  starting transfers between devices: 24.1 us -> 44.2 us
  between operations: 14.5 us -> 1.36 us
  local copies, waits for them, and re-layouts: 17.7 us -> 6.64 us
  Pallas kernels: 12.9 us -> 18.2 us
  other arithmetic: 6.79 us -> 2.28 us
    psum x1 -> x0, waiting for transfers between devices: 30.1 us -> none  [sum_over_dev(): return lax.psum(x, 'dev')]
    ppermute x24 -> x37, starting transfers between devices: 24.1 us -> 44.2 us  [to(): return lax.ppermute(x, axis, where)]
    ppermute x24 -> x37, waiting for transfers between devices: 52.1 us -> 45.7 us  [to(): return lax.ppermute(x, axis, where)]
    ppermute x4 -> x0, local copies, waits for them, and re-layouts: 5.52 us -> none  [the longest x3 4.29 us: shared(): lax.ppermute(for_chip(4 - k), 'ha', [((i + k) % 4, i) for i in range(4)])]
    pallas_call x2 -> x7, Pallas kernels: 12.9 us -> 18.2 us  [the longest x3 8.14 us: conv_third(): pl.pallas_call(functools.partial(conv_kernel, a), grid=(3,), in_specs=[wh...]
    another operation x7 -> x3, other arithmetic: 5.01 us -> 0.79 us  [the longest x1 0.77 us: shared(): own_halo = jnp.stack(own_halo)]
    another operation x1 -> x0, local copies, waits for them, and re-layouts: 2.02 us -> none  [shifted_3(): return jnp.stack([padded[:, :, c:c + width] for c in range(3)])]
    slice x9 -> x18, local copies, waits for them, and re-layouts: 3.49 us -> 2.28 us  [the longest x1 0.95 us: shared(): above = to(jnp.stack([volume[0], upstream[0]]), 'dev', DOWN)]
  transfers between devices with their start and end apart: 25 -> 37, of which waited for: 14 -> 17; matrix products, arithmetic and copies ran while one was open for 11% -> 4% of each run, Pallas kernels for 5% -> 13%
where the time goes in v2:
time: 119 us; the launch traced here: 118 us
  waiting for transfers between devices  45.7 us (38%)
  starting transfers between devices  44.2 us (37%)
  Pallas kernels  18.2 us (15%)
  local copies, waits for them, and re-layouts  6.64 us (6%)
  other arithmetic  2.28 us (2%)
  between operations  1.36 us (1%)
    ppermute x37, waiting for transfers between devices, to(): return lax.ppermute(x, axis, where)  45.7 us
    ppermute x37, starting transfers between devices, to(): return lax.ppermute(x, axis, where)  44.2 us
    pallas_call x3, Pallas kernels, conv_third(): pl.pallas_call(functools.partial(conv_kernel, a), grid=(3,), in_specs=[wh...  8.14 us
    pallas_call x2, Pallas kernels, plane_grad(): pl.pallas_call(functools.partial(plane_grad_kernel, scale, planes, pieces...  5.83 us
    pallas_call x2, Pallas kernels, for_chips(): pl.pallas_call(body, out_shape=[jax.ShapeDtypeStruct(shape, F32)] * 4, in...  4.2 us
    unnamed x20, local copies, waits for them, and re-layouts  3.45 us
  transfers between devices with their start and end apart: 37, of which 17 were waited for; matrix products, arithmetic and copies ran while one was open for 4% of the time, Pallas kernels for 13%

profile of v2, /device:TPU:8, one launch (start us, length us, event | category | flops | bytes accessed | tf_op | source)
XLA Modules:
  0.0 118.3 jit_solution(8962113867939386816)
XLA Ops:
  0.6 2.4 %messages_kernel.1 = (f32[320,256]{1,0:T(8,128)}, f32[320,256]{1,0:T(8,128)}, f32[320,256]{1,0:T(8,128)}, f32[320,256]{1,0:T(8,128)}) custom-call(f32[4,64,256]{2,1,0:T(8,128)} %bitcast.40, f32[256,256]{1,0:T(8,128)} %bitcast.46), custom_call_target="tpu_custom_call" | custom-call | tf_op jit(solution)/shard_map/messages_kernel/pallas_call | solution.py:132
  3.0 2.4 %collective-permute-start = (f32[320,256]{1,0:T(8,128)}, f32[320,256]{1,0:T(8,128)S(1)}, u32[]{:S(2)}, u32[]{:S(2)}) collective-permute-start(f32[320,256]{1,0:T(8,128)} %get-tuple-element.67), channel_id=1, source_target_pairs={{2,0},{4,2},{6,4},{0,6},{3,1},{5,3},{7,5},{1,7},{10,8},{12,10},{14... | collective-permute-start | bytes 983048 | tf_op jit(solution)/shard_map/ppermute | solution.py:230
  9.7 3.7 %collective-permute-done.4 = f32[2,8,8,256]{3,2,1,0:T(8,128)S(1)} collective-permute-done((f32[2,8,8,256]{3,2,1,0:T(8,128)S(1)}, f32[2,8,8,256]{3,2,1,0:T(8,128)S(1)}, u32[]{:S(2)}, u32[]{:S(2)}) %collective-permute-start.4) | collective-permute-done | bytes 131104 | tf_op jit(solution)/shard_map/ppermute | solution.py:230
  13.4 2.9 %collective-permute-done.5 = f32[2,8,8,256]{3,2,1,0:T(8,128)S(1)} collective-permute-done((f32[2,8,8,256]{3,2,1,0:T(8,128)S(1)}, f32[2,8,8,256]{3,2,1,0:T(8,128)S(1)}, u32[]{:S(2)}, u32[]{:S(2)}) %collective-permute-start.5) | collective-permute-done | bytes 131104 | tf_op jit(solution)/shard_map/ppermute | solution.py:230
  18.8 2.3 %collective-permute-start.9 = (f32[64,128]{1,0:T(8,128)}, f32[64,128]{1,0:T(8,128)S(1)}, u32[]{:S(2)}, u32[]{:S(2)}) collective-permute-start(f32[64,128]{1,0:T(8,128)} %get-tuple-element.76), channel_id=1, source_target_pairs={{2,0},{4,2},{6,4},{0,6},{3,1},{5,3},{7,5},{1,7},{10,8},{12,10},{14... | collective-permute-start | bytes 98312 | tf_op jit(solution)/shard_map/ppermute | solution.py:230
  23.6 2.6 %collective-permute-start.11 = (f32[64,128]{1,0:T(8,128)}, f32[64,128]{1,0:T(8,128)S(1)}, u32[]{:S(2)}, u32[]{:S(2)}) collective-permute-start(f32[64,128]{1,0:T(8,128)} %get-tuple-element.78), channel_id=1, source_target_pairs={{6,0},{0,2},{2,4},{4,6},{7,1},{1,3},{3,5},{5,7},{14,8},{8,10},{10,... | collective-permute-start | bytes 98312 | tf_op jit(solution)/shard_map/ppermute | solution.py:230
  30.5 2.3 %plane_grad_1.1 = f32[9,32,256]{2,1,0:T(8,128)S(1)} custom-call(f32[320,256]{1,0:T(8,128)S(1)} %copy-done, f32[320,256]{1,0:T(8,128)S(1)} %collective-permute-done.refs_1_, f32[320,256]{1,0:T(8,128)S(1)} %collective-permute-done.1.refs_2_, f32[320,256]{1,0:T(8,128)S(1)} %collective-permute-done.2.refs_3_, f32[320,256]{1,0:T(8,128)S(1)} %collective-permute-done.3.refs_4_, ...), custom_call_target="tpu_custom_call" | custom-call | flops 905969664 | bytes 4194304 | tf_op jit(solution)/shard_map/plane_grad_1/pallas_call | solution.py:201
  34.1 3.5 %plane_grad_2.1 = (f32[9,32,256]{2,1,0:T(8,128)S(1)}, f32[9,32,256]{2,1,0:T(8,128)S(1)}) custom-call(f32[320,256]{1,0:T(8,128)S(1)} %copy-done, f32[320,256]{1,0:T(8,128)S(1)} %collective-permute-done.refs_1_, f32[320,256]{1,0:T(8,128)S(1)} %collective-permute-done.1.refs_2_, f32[320,256]{1,0:T(8,128)S(1)} %collective-permute-done.2.refs_3_, ...), custom_call_target="tpu_custom_call" | custom-call | flops 1811939328 | bytes 4194304 | tf_op jit(solution)/shard_map/plane_grad_2/pallas_call | solution.py:201
  39.1 5.4 %collective-permute-done.12 = f32[9,32,256]{2,1,0:T(8,128)S(1)} collective-permute-done((f32[9,32,256]{2,1,0:T(8,128)S(1)}, f32[9,32,256]{2,1,0:T(8,128)S(1)}, u32[]{:S(2)}, u32[]{:S(2)}) %collective-permute-start.12) | collective-permute-done | bytes 294944 | tf_op jit(solution)/shard_map/ppermute | solution.py:230
  44.5 3.5 %collective-permute-start.14 = (f32[9,32,256]{2,1,0:T(8,128)S(1)}, f32[9,32,256]{2,1,0:T(8,128)S(1)}, u32[]{:S(2)}, u32[]{:S(2)}) collective-permute-start(f32[9,32,256]{2,1,0:T(8,128)S(1)} %add.41), channel_id=1, source_target_pairs={{8,16},{16,8},{9,17},{17,9},{10,18},{18,10},{11,19},{19,11},{12,20... | collective-permute-start | bytes 884744 | tf_op jit(solution)/shard_map/ppermute | solution.py:230
  54.7 2.5 %collective-permute-start.18 = (f32[9,32,256]{2,1,0:T(8,128)S(1)}, f32[9,32,256]{2,1,0:T(8,128)S(1)}, u32[]{:S(2)}, u32[]{:S(2)}) collective-permute-start(f32[9,32,256]{2,1,0:T(8,128)S(1)} %add.42), channel_id=1, source_target_pairs={{8,0},{16,24},{9,1},{17,25},{10,2},{18,26},{11,3},{19,27},{12,4},{... | collective-permute-start | bytes 884744 | tf_op jit(solution)/shard_map/ppermute | solution.py:230
  57.2 2.3 %collective-permute-start.19 = (f32[9,32,256]{2,1,0:T(8,128)S(1)}, f32[9,32,256]{2,1,0:T(8,128)S(1)}, u32[]{:S(2)}, u32[]{:S(2)}) collective-permute-start(f32[9,32,256]{2,1,0:T(8,128)S(1)} %add.43), channel_id=1, source_target_pairs={{8,16},{16,8},{9,17},{17,9},{10,18},{18,10},{11,19},{19,11},{12,20... | collective-permute-start | bytes 884744 | tf_op jit(solution)/shard_map/ppermute | solution.py:230
  62.3 3.5 %collective-permute-done.19 = f32[9,32,256]{2,1,0:T(8,128)S(1)} collective-permute-done((f32[9,32,256]{2,1,0:T(8,128)S(1)}, f32[9,32,256]{2,1,0:T(8,128)S(1)}, u32[]{:S(2)}, u32[]{:S(2)}) %collective-permute-start.19) | collective-permute-done | bytes 294944 | tf_op jit(solution)/shard_map/ppermute | solution.py:230
  67.3 2.8 %collective-permute-start.25 = (f32[9,32,256]{2,1,0:T(8,128)S(1)}, f32[9,32,256]{2,1,0:T(8,128)S(1)}, u32[]{:S(2)}, u32[]{:S(2)}) collective-permute-start(f32[9,32,256]{2,1,0:T(8,128)S(1)} %add.45), channel_id=1, source_target_pairs={{8,16},{16,8},{9,17},{17,9},{10,18},{18,10},{11,19},{19,11},{12,20... | collective-permute-start | bytes 884744 | tf_op jit(solution)/shard_map/ppermute | solution.py:230
  71.8 2.5 %conv_0.1 = (f32[256,256]{1,0:T(8,128)S(1)}, f32[256,256]{1,0:T(8,128)S(1)}) custom-call(f32[6,10,8,256]{3,2,1,0:T(8,128)S(1)} %get-tuple-element.99.refs_0_, f32[6,10,8,256]{3,2,1,0:T(8,128)S(1)} %pad_maximum_fusion.5.refs_1_, f32[6,10,8,256]{3,2,1,0:T(8,128)S(1)} %get-tuple-element.101.refs_2_, f32[6,10,8,256]{3,2,1,0:T(8,128)S(1)} %get-tuple-element.102.refs_3_, ...), custom_call_target="tpu_custom_call" | custom-call | flops 1811939328 | bytes 4194304 | tf_op jit(solution)/shard_map/conv_0/pallas_call | solution.py:90
  74.3 2.9 %collective-permute-done.23 = f32[4,32,256]{2,1,0:T(8,128)S(1)} collective-permute-done((f32[4,32,256]{2,1,0:T(8,128)S(1)}, f32[4,32,256]{2,1,0:T(8,128)S(1)}, u32[]{:S(2)}, u32[]{:S(2)}) %collective-permute-start.23) | collective-permute-done | bytes 131104 | tf_op jit(solution)/shard_map/ppermute | solution.py:230
  82.4 2.4 %collective-permute-done.31 = f32[5,1,2,32,256]{4,3,0,2,1:T(8,128)S(1)} collective-permute-done((f32[5,1,2,32,256]{4,3,0,2,1:T(8,128)S(1)}, f32[5,1,2,32,256]{4,3,0,2,1:T(8,128)S(1)}, u32[]{:S(2)}, u32[]{:S(2)}) %collective-permute-start.31) | collective-permute-done | bytes 327712 | tf_op jit(solution)/shard_map/ppermute | solution.py:230
  85.9 2.5 %conv_1.1 = (f32[256,256]{1,0:T(8,128)S(1)}, f32[256,256]{1,0:T(8,128)S(1)}) custom-call(f32[6,10,8,256]{3,2,1,0:T(8,128)S(1)} %get-tuple-element.99.refs_0_, f32[6,10,8,256]{3,2,1,0:T(8,128)S(1)} %pad_maximum_fusion.5.refs_1_, f32[6,10,8,256]{3,2,1,0:T(8,128)S(1)} %get-tuple-element.101.refs_2_, f32[6,10,8,256]{3,2,1,0:T(8,128)S(1)} %get-tuple-element.102.refs_3_, ...), custom_call_target="tpu_custom_call" | custom-call | flops 1811939328 | bytes 4194304 | tf_op jit(solution)/shard_map/conv_1/pallas_call | solution.py:90
  88.4 4.2 %collective-permute-done.32 = f32[4,2,1,32,256]{4,3,0,2,1:T(8,128)S(1)} collective-permute-done((f32[4,2,1,32,256]{4,3,0,2,1:T(8,128)S(1)}, f32[4,2,1,32,256]{4,3,0,2,1:T(8,128)S(1)}, u32[]{:S(2)}, u32[]{:S(2)}) %collective-permute-start.32) | collective-permute-done | bytes 262176 | tf_op jit(solution)/shard_map/ppermute | solution.py:230
  93.1 2.5 %collective-permute-start.29 = (f32[5,32,256]{2,1,0:T(8,128)S(1)}, f32[5,32,256]{2,1,0:T(8,128)S(1)}, u32[]{:S(2)}, u32[]{:S(2)}) collective-permute-start(f32[5,32,256]{2,1,0:T(8,128)S(1)} %slice.189), channel_id=1, source_target_pairs={{0,2},{2,0},{4,6},{6,4},{1,3},{3,1},{5,7},{7,5},{8,10},{10,8},{12,... | collective-permute-start | bytes 491528 | tf_op jit(solution)/shard_map/ppermute | solution.py:230
  95.6 4.2 %collective-permute-done.33 = f32[5,1,2,32,256]{4,3,0,2,1:T(8,128)S(1)} collective-permute-done((f32[5,1,2,32,256]{4,3,0,2,1:T(8,128)S(1)}, f32[5,1,2,32,256]{4,3,0,2,1:T(8,128)S(1)}, u32[]{:S(2)}, u32[]{:S(2)}) %collective-permute-start.33) | collective-permute-done | bytes 327712 | tf_op jit(solution)/shard_map/ppermute | solution.py:230
  100.7 3.2 %conv_2.1 = (f32[256,256]{1,0:T(8,128)}, f32[256,256]{1,0:T(8,128)}) custom-call(f32[6,10,8,256]{3,2,1,0:T(8,128)S(1)} %get-tuple-element.99.refs_0_, f32[6,10,8,256]{3,2,1,0:T(8,128)S(1)} %pad_maximum_fusion.5.refs_1_, f32[6,10,8,256]{3,2,1,0:T(8,128)S(1)} %get-tuple-element.101.refs_2_, f32[6,10,8,256]{3,2,1,0:T(8,128)S(1)} %get-tuple-element.102.refs_3_, ...), custom_call_target="tpu_custom_call" | custom-call | flops 1811939328 | bytes 4194304 | tf_op jit(solution)/shard_map/conv_2/pallas_call | solution.py:90
  103.9 4.9 %collective-permute-done.34 = f32[4,2,1,32,256]{4,3,0,2,1:T(8,128)S(1)} collective-permute-done((f32[4,2,1,32,256]{4,3,0,2,1:T(8,128)S(1)}, f32[4,2,1,32,256]{4,3,0,2,1:T(8,128)S(1)}, u32[]{:S(2)}, u32[]{:S(2)}) %collective-permute-start.34) | collective-permute-done | bytes 262176 | tf_op jit(solution)/shard_map/ppermute | solution.py:230
  111.2 4.9 %collective-permute-done.35 = f32[5,1,2,32,256]{4,3,0,2,1:T(8,128)S(1)} collective-permute-done((f32[5,1,2,32,256]{4,3,0,2,1:T(8,128)S(1)}, f32[5,1,2,32,256]{4,3,0,2,1:T(8,128)S(1)}, u32[]{:S(2)}, u32[]{:S(2)}) %collective-permute-start.35) | collective-permute-done | bytes 327712 | tf_op jit(solution)/shard_map/ppermute | solution.py:230
  (140 shorter events, 40.5 us)
Async XLA Ops:
  3.0 18.1 %collective-permute-start = (f32[320,256]{1,0:T(8,128)}, f32[320,256]{1,0:T(8,128)S(1)}, u32[]{:S(2)}, u32[]{:S(2)}) collective-permute-start(f32[320,256]{1,0:T(8,128)} %get-tuple-element.67), channel_id=1, source_target_pairs={{2,0},{4,2},{6,4},{0,6},{3,1},{5,3},{7,5},{1,7},{10,8},{12,10},{14... | collective-permute-start | bytes 983048 | tf_op jit(solution)/shard_map/ppermute | solution.py:230
  5.5 17.1 %collective-permute-start.1 = (f32[320,256]{1,0:T(8,128)}, f32[320,256]{1,0:T(8,128)S(1)}, u32[]{:S(2)}, u32[]{:S(2)}) collective-permute-start(f32[320,256]{1,0:T(8,128)} %get-tuple-element.68), channel_id=1, source_target_pairs={{4,0},{6,2},{0,4},{2,6},{5,1},{7,3},{1,5},{3,7},{12,8},{14,10},{8,... | collective-permute-start | bytes 983048 | tf_op jit(solution)/shard_map/ppermute | solution.py:230
  6.0 16.6 %collective-permute-start.2 = (f32[320,256]{1,0:T(8,128)}, f32[320,256]{1,0:T(8,128)S(1)}, u32[]{:S(2)}, u32[]{:S(2)}) collective-permute-start(f32[320,256]{1,0:T(8,128)} %get-tuple-element.69), channel_id=1, source_target_pairs={{6,0},{0,2},{2,4},{4,6},{7,1},{1,3},{3,5},{5,7},{14,8},{8,10},{10,... | collective-permute-start | bytes 983048 | tf_op jit(solution)/shard_map/ppermute | solution.py:230
  9.2 7.1 %collective-permute-start.5 = (f32[2,8,8,256]{3,2,1,0:T(8,128)S(1)}, f32[2,8,8,256]{3,2,1,0:T(8,128)S(1)}, u32[]{:S(2)}, u32[]{:S(2)}) collective-permute-start(f32[2,8,8,256]{3,2,1,0:T(8,128)S(1)} %pad_maximum_fusion.9), channel_id=1, source_target_pairs={{8,0},{16,8},{24,16},{0,24},{9,1},{17,9},{25,17},{1,25},{10,2},{18... | collective-permute-start | bytes 393224 | tf_op jit(solution)/shard_map/ppermute | solution.py:230
  22.6 6.9 %collective-permute-start.7 = (f32[320,256]{1,0:T(8,128)S(1)}, f32[320,256]{1,0:T(8,128)S(1)}, u32[]{:S(2)}, u32[]{:S(2)}) collective-permute-start(f32[320,256]{1,0:T(8,128)S(1)} %collective-permute-done.1.refs_2_), channel_id=1, source_target_pairs={{0,1},{1,0},{2,3},{3,2},{4,5},{5,4},{6,7},{7,6},{8,9},{9,8},{10,11... | collective-permute-start | bytes 983048 | tf_op jit(solution)/shard_map/ppermute | solution.py:230
  32.8 11.7 %collective-permute-start.12 = (f32[9,32,256]{2,1,0:T(8,128)S(1)}, f32[9,32,256]{2,1,0:T(8,128)S(1)}, u32[]{:S(2)}, u32[]{:S(2)}) collective-permute-start(f32[9,32,256]{2,1,0:T(8,128)S(1)} %plane_grad_1.1), channel_id=1, source_target_pairs={{0,8},{24,16},{1,9},{25,17},{2,10},{26,18},{3,11},{27,19},{4,12},{... | collective-permute-start | bytes 884744 | tf_op jit(solution)/shard_map/ppermute | solution.py:230
  37.7 16.4 %collective-permute-start.15 = (f32[9,32,256]{2,1,0:T(8,128)S(1)}, f32[9,32,256]{2,1,0:T(8,128)S(1)}, u32[]{:S(2)}, u32[]{:S(2)}) collective-permute-start(f32[9,32,256]{2,1,0:T(8,128)S(1)} %get-tuple-element.87), channel_id=1, source_target_pairs={{0,8},{24,16},{1,9},{25,17},{2,10},{26,18},{3,11},{27,19},{4,12},{... | collective-permute-start | bytes 884744 | tf_op jit(solution)/shard_map/ppermute | solution.py:230
  44.5 10.1 %collective-permute-start.14 = (f32[9,32,256]{2,1,0:T(8,128)S(1)}, f32[9,32,256]{2,1,0:T(8,128)S(1)}, u32[]{:S(2)}, u32[]{:S(2)}) collective-permute-start(f32[9,32,256]{2,1,0:T(8,128)S(1)} %add.41), channel_id=1, source_target_pairs={{8,16},{16,8},{9,17},{17,9},{10,18},{18,10},{11,19},{19,11},{12,20... | collective-permute-start | bytes 884744 | tf_op jit(solution)/shard_map/ppermute | solution.py:230
  51.1 11.3 %collective-permute-start.20 = (f32[9,32,256]{2,1,0:T(8,128)S(1)}, f32[9,32,256]{2,1,0:T(8,128)S(1)}, u32[]{:S(2)}, u32[]{:S(2)}) collective-permute-start(f32[9,32,256]{2,1,0:T(8,128)S(1)} %get-tuple-element.89), channel_id=1, source_target_pairs={{0,8},{24,16},{1,9},{25,17},{2,10},{26,18},{3,11},{27,19},{4,12},{... | collective-permute-start | bytes 884744 | tf_op jit(solution)/shard_map/ppermute | solution.py:230
  54.7 7.7 %collective-permute-start.18 = (f32[9,32,256]{2,1,0:T(8,128)S(1)}, f32[9,32,256]{2,1,0:T(8,128)S(1)}, u32[]{:S(2)}, u32[]{:S(2)}) collective-permute-start(f32[9,32,256]{2,1,0:T(8,128)S(1)} %add.42), channel_id=1, source_target_pairs={{8,0},{16,24},{9,1},{17,25},{10,2},{18,26},{11,3},{19,27},{12,4},{... | collective-permute-start | bytes 884744 | tf_op jit(solution)/shard_map/ppermute | solution.py:230
  57.2 8.7 %collective-permute-start.19 = (f32[9,32,256]{2,1,0:T(8,128)S(1)}, f32[9,32,256]{2,1,0:T(8,128)S(1)}, u32[]{:S(2)}, u32[]{:S(2)}) collective-permute-start(f32[9,32,256]{2,1,0:T(8,128)S(1)} %add.43), channel_id=1, source_target_pairs={{8,16},{16,8},{9,17},{17,9},{10,18},{18,10},{11,19},{19,11},{12,20... | collective-permute-start | bytes 884744 | tf_op jit(solution)/shard_map/ppermute | solution.py:230
  65.9 11.3 %collective-permute-start.24 = (f32[9,32,256]{2,1,0:T(8,128)S(1)}, f32[9,32,256]{2,1,0:T(8,128)S(1)}, u32[]{:S(2)}, u32[]{:S(2)}) collective-permute-start(f32[9,32,256]{2,1,0:T(8,128)S(1)} %add.44), channel_id=1, source_target_pairs={{8,0},{16,24},{9,1},{17,25},{10,2},{18,26},{11,3},{19,27},{12,4},{... | collective-permute-start | bytes 884744 | tf_op jit(solution)/shard_map/ppermute | solution.py:230
  67.3 9.9 %collective-permute-start.25 = (f32[9,32,256]{2,1,0:T(8,128)S(1)}, f32[9,32,256]{2,1,0:T(8,128)S(1)}, u32[]{:S(2)}, u32[]{:S(2)}) collective-permute-start(f32[9,32,256]{2,1,0:T(8,128)S(1)} %add.45), channel_id=1, source_target_pairs={{8,16},{16,8},{9,17},{17,9},{10,18},{18,10},{11,19},{19,11},{12,20... | collective-permute-start | bytes 884744 | tf_op jit(solution)/shard_map/ppermute | solution.py:230
  70.1 7.0 %collective-permute-start.22 = (f32[5,32,256]{2,1,0:T(8,128)S(1)}, f32[5,32,256]{2,1,0:T(8,128)S(1)}, u32[]{:S(2)}, u32[]{:S(2)}) collective-permute-start(f32[5,32,256]{2,1,0:T(8,128)S(1)} %slice.185), channel_id=1, source_target_pairs={{0,2},{2,0},{4,6},{6,4},{1,3},{3,1},{5,7},{7,5},{8,10},{10,8},{12,... | collective-permute-start | bytes 491528 | tf_op jit(solution)/shard_map/ppermute | solution.py:230
  77.7 7.1 %collective-permute-start.31 = (f32[5,1,2,32,256]{4,3,0,2,1:T(8,128)S(1)}, f32[5,1,2,32,256]{4,3,0,2,1:T(8,128)S(1)}, u32[]{:S(2)}, u32[]{:S(2)}) collective-permute-start(f32[5,1,2,32,256]{4,3,0,2,1:T(8,128)S(1)} %get-tuple-element.138), channel_id=1, source_target_pairs={{0,4},{2,6},{4,0},{6,2},{1,5},{3,7},{5,1},{7,3},{8,12},{10,14},{12... | collective-permute-start | bytes 983048 | tf_op jit(solution)/shard_map/ppermute | solution.py:230
  78.1 10.3 %collective-permute-start.26 = (f32[5,32,256]{2,1,0:T(8,128)S(1)}, f32[5,32,256]{2,1,0:T(8,128)S(1)}, u32[]{:S(2)}, u32[]{:S(2)}) collective-permute-start(f32[5,32,256]{2,1,0:T(8,128)S(1)} %slice.187), channel_id=1, source_target_pairs={{0,2},{2,0},{4,6},{6,4},{1,3},{3,1},{5,7},{7,5},{8,10},{10,8},{12,... | collective-permute-start | bytes 491528 | tf_op jit(solution)/shard_map/ppermute | solution.py:230
  80.4 8.0 %collective-permute-start.27 = (f32[4,32,256]{2,1,0:T(8,128)S(1)}, f32[4,32,256]{2,1,0:T(8,128)S(1)}, u32[]{:S(2)}, u32[]{:S(2)}) collective-permute-start(f32[4,32,256]{2,1,0:T(8,128)S(1)} %slice.188), channel_id=1, source_target_pairs={{0,4},{2,6},{4,0},{6,2},{1,5},{3,7},{5,1},{7,3},{8,12},{10,14},{12... | collective-permute-start | bytes 393224 | tf_op jit(solution)/shard_map/ppermute | solution.py:230
  80.9 7.5 %collective-permute-start.28 = (f32[9,32,256]{2,1,0:T(8,128)S(1)}, f32[9,32,256]{2,1,0:T(8,128)S(1)}, u32[]{:S(2)}, u32[]{:S(2)}) collective-permute-start(f32[9,32,256]{2,1,0:T(8,128)S(1)} %add.46), channel_id=1, source_target_pairs={{8,0},{16,24},{9,1},{17,25},{10,2},{18,26},{11,3},{19,27},{12,4},{... | collective-permute-start | bytes 884744 | tf_op jit(solution)/shard_map/ppermute | solution.py:230
  84.9 7.7 %collective-permute-start.32 = (f32[4,2,1,32,256]{4,3,0,2,1:T(8,128)S(1)}, f32[4,2,1,32,256]{4,3,0,2,1:T(8,128)S(1)}, u32[]{:S(2)}, u32[]{:S(2)}) collective-permute-start(f32[4,2,1,32,256]{4,3,0,2,1:T(8,128)S(1)} %get-tuple-element.136), channel_id=1, source_target_pairs={{0,2},{2,0},{4,6},{6,4},{1,3},{3,1},{5,7},{7,5},{8,10},{10,8},{12,... | collective-permute-start | bytes 786440 | tf_op jit(solution)/shard_map/ppermute | solution.py:230
  92.7 7.1 %collective-permute-start.33 = (f32[5,1,2,32,256]{4,3,0,2,1:T(8,128)S(1)}, f32[5,1,2,32,256]{4,3,0,2,1:T(8,128)S(1)}, u32[]{:S(2)}, u32[]{:S(2)}) collective-permute-start(f32[5,1,2,32,256]{4,3,0,2,1:T(8,128)S(1)} %get-tuple-element.134), channel_id=1, source_target_pairs={{0,4},{2,6},{4,0},{6,2},{1,5},{3,7},{5,1},{7,3},{8,12},{10,14},{12... | collective-permute-start | bytes 983048 | tf_op jit(solution)/shard_map/ppermute | solution.py:230
  93.1 10.8 %collective-permute-start.29 = (f32[5,32,256]{2,1,0:T(8,128)S(1)}, f32[5,32,256]{2,1,0:T(8,128)S(1)}, u32[]{:S(2)}, u32[]{:S(2)}) collective-permute-start(f32[5,32,256]{2,1,0:T(8,128)S(1)} %slice.189), channel_id=1, source_target_pairs={{0,2},{2,0},{4,6},{6,4},{1,3},{3,1},{5,7},{7,5},{8,10},{10,8},{12,... | collective-permute-start | bytes 491528 | tf_op jit(solution)/shard_map/ppermute | solution.py:230
  95.6 8.3 %collective-permute-start.30 = (f32[4,32,256]{2,1,0:T(8,128)S(1)}, f32[4,32,256]{2,1,0:T(8,128)S(1)}, u32[]{:S(2)}, u32[]{:S(2)}) collective-permute-start(f32[4,32,256]{2,1,0:T(8,128)S(1)} %slice.190), channel_id=1, source_target_pairs={{0,4},{2,6},{4,0},{6,2},{1,5},{3,7},{5,1},{7,3},{8,12},{10,14},{12... | collective-permute-start | bytes 393224 | tf_op jit(solution)/shard_map/ppermute | solution.py:230
  99.9 8.9 %collective-permute-start.34 = (f32[4,2,1,32,256]{4,3,0,2,1:T(8,128)S(1)}, f32[4,2,1,32,256]{4,3,0,2,1:T(8,128)S(1)}, u32[]{:S(2)}, u32[]{:S(2)}) collective-permute-start(f32[4,2,1,32,256]{4,3,0,2,1:T(8,128)S(1)} %get-tuple-element.132), channel_id=1, source_target_pairs={{0,2},{2,0},{4,6},{6,4},{1,3},{3,1},{5,7},{7,5},{8,10},{10,8},{12,... | collective-permute-start | bytes 786440 | tf_op jit(solution)/shard_map/ppermute | solution.py:230
  109.0 7.1 %collective-permute-start.35 = (f32[5,1,2,32,256]{4,3,0,2,1:T(8,128)S(1)}, f32[5,1,2,32,256]{4,3,0,2,1:T(8,128)S(1)}, u32[]{:S(2)}, u32[]{:S(2)}) collective-permute-start(f32[5,1,2,32,256]{4,3,0,2,1:T(8,128)S(1)} %get-tuple-element.130), channel_id=1, source_target_pairs={{0,4},{2,6},{4,0},{6,2},{1,5},{3,7},{5,1},{7,3},{8,12},{10,14},{12... | collective-permute-start | bytes 983048 | tf_op jit(solution)/shard_map/ppermute | solution.py:230
  (23 other events, 165.3 us)

commit v3 on v2

--- a/solution.py
+++ b/solution.py
@@ -110,32 +110,23 @@
     return total
 
 
-def messages_kernel(*refs):
+def messages_kernel(below_ref, volume_ref, above_ref, *out_refs):
     h, w = lax.axis_index("ha"), lax.axis_index("wa")
-    v_ref, u_ref, out_refs = refs[0], refs[1], refs[2:]
+    planes = [below_ref[0], *(volume_ref[z] for z in range(4)), above_ref[0]]
     for k, out_ref in enumerate(out_refs):
-        chip = lax.rem(h + k, 4)
-        out_ref[0:256] = u_ref[...]
-        for t in range(2):
-            out_ref[256:320, 128 * t : 128 * t + 128] = packed((v_ref[2 * t], v_ref[2 * t + 1]), chip, w)
-
-
-def ends_kernel(*refs):
-    h, w = lax.axis_index("ha"), lax.axis_index("wa")
-    below_ref, above_ref, out_refs = refs[0], refs[1], refs[2:]
-    for k, out_ref in enumerate(out_refs):
-        out_ref[...] = packed((below_ref[0], above_ref[0]), lax.rem(h + k, 4), w)
-
-
-def for_chips(body, shape, *arrays):
+        for t in range(3):
+            out_ref[:, 128 * t : 128 * t + 128] = packed(planes[2 * t : 2 * t + 2], lax.rem(h + k, 4), w)
+
+
+def messages(below, volume, above):
     vmem = pl.BlockSpec(memory_space=pltpu.VMEM)
     return pl.pallas_call(
-        body,
-        out_shape=[jax.ShapeDtypeStruct(shape, F32)] * 4,
-        in_specs=[vmem] * len(arrays),
+        messages_kernel,
+        out_shape=[jax.ShapeDtypeStruct((64, 384), F32)] * 4,
+        in_specs=[vmem] * 3,
         out_specs=[vmem] * 4,
-        name=body.__name__,
-    )(*arrays)
+        name="messages",
+    )(below, volume, above)
 
 
 def lay_out(shifted, plane, first, second):
@@ -159,22 +150,17 @@
 
 def plane_of(refs, z, offset):
     tile = 128 * (z // 2)
-    plane = jnp.concatenate([ref[256:320, tile : tile + 128].reshape(8, 8, 128) for ref in refs], axis=0)
+    plane = jnp.concatenate([ref[:, tile : tile + 128].reshape(8, 8, 128) for ref in refs], axis=0)
     return pltpu.roll(plane, (128 - 64 * (z % 2) - offset) % 128, 2)
 
 
-def plane_grad_kernel(scale, planes, pieces, *refs):
-    mine, other = refs[:4], refs[4:8]
-    out_refs, shifted, u_cat = refs[-2 - pieces : -2], refs[-2], refs[-1]
+def plane_grad_kernel(scale, planes, *refs):
+    u_refs, mine, other, out_refs, shifted, u_cat = refs[:8], refs[8:12], refs[12:16], refs[16:-2], refs[-2], refs[-1]
     share = out_refs[0].shape[0]
-    for z in range(4):
-        lay_out(shifted, z + 1, plane_of(mine, z, 0), plane_of(other, z, 32))
-    if planes != (1,):
-        own_halo, other_halo = (ref[...].reshape(32, 8, 128) for ref in refs[8:10])
-        for i, z in enumerate((0, 5)):
-            lay_out(shifted, z, pltpu.roll(own_halo, (128 - 64 * i) % 128, 2), pltpu.roll(other_halo, 96 - 64 * i, 2))
-    for i, ref in enumerate(mine + other):
-        hi, lo = split(ref[0:256].T)
+    for z in range(1, 5) if planes == (1,) else range(6):
+        lay_out(shifted, z, plane_of(mine, z, 0), plane_of(other, z, 32))
+    for i, ref in enumerate(u_refs):
+        hi, lo = split(ref[...].T)
         u_cat[i, :, 0:256] = hi
         u_cat[i, :, 256:512] = hi
         u_cat[i, :, 512:768] = lo
@@ -195,19 +181,18 @@
                 out_refs[tap // share][tap % share] = turned[128 * i + 32 * c : 128 * i + 32 * c + 32]
 
 
-def plane_grad(scale, planes, pieces, messages, halo=()):
+def plane_grad(scale, planes, pieces, blocks):
     vmem = pl.BlockSpec(memory_space=pltpu.VMEM)
-    shapes = [jax.ShapeDtypeStruct((9 * len(planes) // pieces, 32, 256), F32)] * pieces
     return pl.pallas_call(
-        functools.partial(plane_grad_kernel, scale, planes, pieces),
-        out_shape=shapes,
-        in_specs=[vmem] * (8 + len(halo)),
-        out_specs=[vmem] * len(shapes),
+        functools.partial(plane_grad_kernel, scale, planes),
+        out_shape=[jax.ShapeDtypeStruct((9 * len(planes) // pieces, 32, 256), F32)] * pieces,
+        in_specs=[vmem] * 16,
+        out_specs=[vmem] * pieces,
         scratch_shapes=[pltpu.VMEM((2, 6, 34, 8, 128), F32), pltpu.VMEM((8, 256, 768), BF16)],
         compiler_params=pltpu.CompilerParams(vmem_limit_bytes=40 * 2**20),
         cost_estimate=pl.CostEstimate(flops=2 * 3 * 9 * len(planes) * 32 * 2048 * 256, bytes_accessed=4 * 2**20, transcendentals=0),
         name=f"plane_grad_{len(planes)}",
-    )(*messages, *halo)
+    )(*blocks)
 
 
 SWAP = [(0, 1), (1, 0)]
@@ -243,42 +228,39 @@
     def around(messages):
         return [messages[0]] + [to(messages[4 - k], "ha", [((i + k) % 4, i) for i in range(4)]) for k in (1, 2, 3)]
 
-    mine = around(for_chips(messages_kernel, (320, channels), volume.reshape(4, 64, channels), upstream.reshape(256, channels)))
-    other = [to(mine[0], "wa", SWAP)]
-
-    volume, upstream, _ = together(volume, upstream, other[0])
+    u_mine = around([upstream.reshape(256, channels)] * 4)
+    u_other = [to(u_mine[0], "wa", SWAP)]
+    volume, upstream, _ = together(volume, upstream, u_other[0])
     below = to(jnp.stack([volume[3], upstream[3]]), "dev", UP)
     above = to(jnp.stack([volume[0], upstream[0]]), "dev", DOWN)
-    ends = for_chips(ends_kernel, (64, 128), below.reshape(2, 64, channels), above.reshape(2, 64, channels))
-    *arrived, _ = together(*mine[1:], ends[0])
-    mine = mine[:1] + arrived
-    other += [to(x, "wa", SWAP) for x in arrived]
-    own_halo = around(ends)
-    *arrived, _ = together(*mine, *other, *own_halo)
-    mine, other = arrived[:4], arrived[4:8]
-    own_halo = jnp.stack(own_halo)
-    other_halo = to(own_halo, "wa", SWAP)
-
-    (a0,) = plane_grad(scale, (1,), 1, mine + other)
-    a1 = to(a0, "dev", INWARDS)
-    b0, c0 = plane_grad(scale, (0, 2), 2, mine + other, (own_halo, other_halo))
-    b1, c1 = to(b0, "dev", INWARDS), to(c0, "dev", INWARDS)
-    a0, _ = together(a0 + a1, b0)
-    a1 = to(a0, "dev", MIDDLE)
+    parts = messages(below.reshape(2, 64, channels), volume.reshape(4, 64, channels), above.reshape(2, 64, channels))
+    v_mine = around(parts)
+    *arrived, _ = together(*u_mine[1:], parts[0])
+    u_mine = u_mine[:1] + arrived
+    u_other += [to(x, "wa", SWAP) for x in arrived]
+    v_other = [to(x, "wa", SWAP) for x in v_mine]
+    blocks = together(*u_mine, *u_other, *v_mine, *v_other)
+
+    (a0,) = plane_grad(scale, (1,), 1, blocks)
 
     def edge(row):
         return jnp.concatenate([below[:, row : row + 1], volume[:, row : row + 1], above[:, row : row + 1]], axis=0)
 
-    low_edge, high_edge, _ = together(edge(0), edge(7), c0)
+    low_edge, high_edge, _ = together(edge(0), edge(7), a0)
     behind, ahead = to(high_edge, "ha", UP), to(low_edge, "ha", DOWN)
-    a1, b1, behind, ahead = together(a1, b1, behind, ahead)
+    a1 = to(a0, "dev", INWARDS)
+    b0, c0 = plane_grad(scale, (0, 2), 2, blocks)
+    b1, c1 = to(b0, "dev", INWARDS), to(c0, "dev", INWARDS)
+    a0, behind, ahead, _ = together(a0 + a1, behind, ahead, b0)
+    a1 = to(a0, "dev", MIDDLE)
+    a1, b1 = together(a1, b1)
     a0, b0 = a0 + a1, b0 + b1
 
     a1, b1 = to(a0, "dev", OUTWARDS), to(b0, "dev", MIDDLE)
     deep = jnp.concatenate([below, volume, above], axis=0)
     rows = jnp.concatenate([behind, deep, ahead], axis=1)
     v_rows = jnp.concatenate([rows[0:1], rows[2:7]], axis=0)
-    u_own = [x[:256].reshape(4, 8, 8, channels) for x in mine]
+    u_own = [x.reshape(4, 8, 8, channels) for x in u_mine]
     u_rows = jnp.concatenate([u_own[3][:, 7:8], u_own[0], u_own[1][:, 0:1]], axis=1)
     u_rows = jnp.concatenate([rows[1:2], u_rows, rows[7:8]], axis=0)
     both = jnp.concatenate([v_rows, u_rows], axis=0)
@@ -317,15 +299,17 @@
     a_far = second_half(a0)
     conv = conv_third(1, windows, taps, conv)
     b_got = first_half(b0)
-    b0, b1, b2, c1, *conv = together(b0, *b_got, to(c0, "dev", OUTWARDS), *conv)
+    b0, b1, b2, c1, *rest = together(b0, *b_got, to(c0, "dev", OUTWARDS), *a_far, *conv)
+    a_far, conv = rest[:2], rest[2:]
     c0, b0 = jnp.where(end, c1, c0), joined(b0, (b1, b2))
 
     b_far = second_half(b0)
     conv = conv_third(2, windows, taps, conv)
     c_got = first_half(c0)
-    c0, c1, c2, *conv = together(c0, *c_got, *conv)
+    c0, c1, c2, *rest = together(c0, *c_got, *b_far, *conv)
+    b_far, conv = rest[:2], rest[2:]
     c0 = joined(c0, (c1, c2))
-    c_far = second_half(c0)
+    c_far = together(*second_half(c0))
 
     kernel_grad = jnp.zeros((27, 2, 2, 32, channels), F32)
     kernel_grad = placed(kernel_grad, 9, a0, a_far)

time: 119 us -> 110 us (0.924)
  waiting for transfers between devices: 45.7 us -> 37.3 us
  local copies, waits for them, and re-layouts: 6.64 us -> 8.93 us
  Pallas kernels: 18.2 us -> 16.3 us
    ppermute x37 -> x40, waiting for transfers between devices: 45.7 us -> 37.3 us  [to(): return lax.ppermute(x, axis, where)]
    pallas_call x4 -> x3, Pallas kernels: 10 us -> 8.12 us  [the longest x2 5.94 us: plane_grad(): pl.pallas_call(functools.partial(plane_grad_kernel, scale, planes), out_s...]
    ppermute x37 -> x40, starting transfers between devices: 44.2 us -> 43.8 us  [to(): return lax.ppermute(x, axis, where)]
  transfers between devices with their start and end apart: 37 -> 40, of which waited for: 17 -> 19; matrix products, arithmetic and copies ran while one was open for 4% -> 5% of each run, Pallas kernels for 13% -> 13%
where the time goes in v3:
time: 110 us; the launch traced here: 109 us
  starting transfers between devices  43.8 us (40%)
  waiting for transfers between devices  37.3 us (34%)
  Pallas kernels  16.3 us (15%)
  local copies, waits for them, and re-layouts  8.93 us (8%)
  other arithmetic  1.57 us (1%)
  between operations  1.29 us (1%)
    ppermute x40, starting transfers between devices, to(): return lax.ppermute(x, axis, where)  43.8 us
    ppermute x40, waiting for transfers between devices, to(): return lax.ppermute(x, axis, where)  37.3 us
    pallas_call x3, Pallas kernels, conv_third(): pl.pallas_call(functools.partial(conv_kernel, a), grid=(3,), in_specs=[wh...  8.14 us
    pallas_call x2, Pallas kernels, plane_grad(): pl.pallas_call(functools.partial(plane_grad_kernel, scale, planes), out_s...  5.94 us
    unnamed x20, local copies, waits for them, and re-layouts  4.32 us
  transfers between devices with their start and end apart: 40, of which 19 were waited for; matrix products, arithmetic and copies ran while one was open for 5% of the time, Pallas kernels for 13%

profile of v3, /device:TPU:8, one launch (start us, length us, event | category | flops | bytes accessed | tf_op | source)
XLA Modules:
  0.0 109.1 jit_solution(469169294837744314)
XLA Ops:
  0.7 2.5 %collective-permute-start = (f32[256,256]{1,0:T(8,128)}, f32[256,256]{1,0:T(8,128)S(1)}, u32[]{:S(2)}, u32[]{:S(2)}) collective-permute-start(f32[256,256]{1,0:T(8,128)} %bitcast.36), channel_id=1, source_target_pairs={{2,0},{4,2},{6,4},{0,6},{3,1},{5,3},{7,5},{1,7},{10,8},{12,10},{14... | collective-permute-start | bytes 786440 | tf_op jit(solution)/shard_map/ppermute | solution.py:215
  4.2 1.6 %collective-permute-start.4 = (f32[2,8,8,256]{3,2,1,0:T(8,128)S(1)}, f32[2,8,8,256]{3,2,1,0:T(8,128)S(1)}, u32[]{:S(2)}, u32[]{:S(2)}) collective-permute-start(f32[2,8,8,256]{3,2,1,0:T(8,128)S(1)} %pad_maximum_fusion.8), channel_id=1, source_target_pairs={{0,8},{8,16},{16,24},{24,0},{1,9},{9,17},{17,25},{25,1},{2,10},{10... | collective-permute-start | bytes 393224 | tf_op jit(solution)/shard_map/ppermute | solution.py:215
  8.6 1.9 %collective-permute-done.4 = f32[2,8,8,256]{3,2,1,0:T(8,128)S(1)} collective-permute-done((f32[2,8,8,256]{3,2,1,0:T(8,128)S(1)}, f32[2,8,8,256]{3,2,1,0:T(8,128)S(1)}, u32[]{:S(2)}, u32[]{:S(2)}) %collective-permute-start.4) | collective-permute-done | bytes 131104 | tf_op jit(solution)/shard_map/ppermute | solution.py:215
  10.5 3.0 %collective-permute-done.5 = f32[2,8,8,256]{3,2,1,0:T(8,128)S(1)} collective-permute-done((f32[2,8,8,256]{3,2,1,0:T(8,128)S(1)}, f32[2,8,8,256]{3,2,1,0:T(8,128)S(1)}, u32[]{:S(2)}, u32[]{:S(2)}) %collective-permute-start.5) | collective-permute-done | bytes 131104 | tf_op jit(solution)/shard_map/ppermute | solution.py:215
  14.1 2.2 %messages.1 = (f32[64,384]{1,0:T(8,128)}, f32[64,384]{1,0:T(8,128)}, f32[64,384]{1,0:T(8,128)}, f32[64,384]{1,0:T(8,128)}) custom-call(f32[2,64,256]{2,1,0:T(8,128)} %bitcast.44, f32[4,64,256]{2,1,0:T(8,128)} %bitcast.43, f32[2,64,256]{2,1,0:T(8,128)} %bitcast.45), custom_call_target="tpu_custom_call" | custom-call | tf_op jit(solution)/shard_map/messages/pallas_call | solution.py:123
  16.3 1.6 %collective-permute-start.9 = (f32[64,384]{1,0:T(8,128)}, f32[64,384]{1,0:T(8,128)S(1)}, u32[]{:S(2)}, u32[]{:S(2)}) collective-permute-start(f32[64,384]{1,0:T(8,128)} %get-tuple-element.82), channel_id=1, source_target_pairs={{2,0},{4,2},{6,4},{0,6},{3,1},{5,3},{7,5},{1,7},{10,8},{12,10},{14... | collective-permute-start | bytes 294920 | tf_op jit(solution)/shard_map/ppermute | solution.py:215
  21.5 3.3 %collective-permute-done.10.refs_10_ = f32[64,384]{1,0:T(8,128)S(1)} collective-permute-done((f32[64,384]{1,0:T(8,128)}, f32[64,384]{1,0:T(8,128)S(1)}, u32[]{:S(2)}, u32[]{:S(2)}) %collective-permute-start.10) | collective-permute-done | bytes 98336 | tf_op jit(solution)/shard_map/ppermute | solution.py:215
  29.6 2.4 %plane_grad_1.1 = f32[9,32,256]{2,1,0:T(8,128)S(1)} custom-call(f32[256,256]{1,0:T(8,128)S(1)} %bitcast.39, f32[256,256]{1,0:T(8,128)S(1)} %collective-permute-done.refs_1_, f32[256,256]{1,0:T(8,128)S(1)} %collective-permute-done.1.refs_2_, f32[256,256]{1,0:T(8,128)S(1)} %collective-permute-done.2.refs_3_, f32[256,256]{1,0:T(8,128)S(1)} %collective-permute-done.3.refs_4_, ...), custom_call_target="tpu_custom_call" | custom-call | flops 905969664 | bytes 4194304 | tf_op jit(solution)/shard_map/plane_grad_1/pallas_call | solution.py:186
  33.6 2.8 %collective-permute-start.18 = (f32[8,1,8,256]{3,2,1,0:T(8,128)S(1)}, f32[8,1,8,256]{3,2,1,0:T(8,128)S(1)}, u32[]{:S(2)}, u32[]{:S(2)}) collective-permute-start(f32[8,1,8,256]{3,2,1,0:T(8,128)S(1)} %pad_maximum_fusion.13), channel_id=1, source_target_pairs={{2,0},{4,2},{6,4},{0,6},{3,1},{5,3},{7,5},{1,7},{10,8},{12,10},{14... | collective-permute-start | bytes 196616 | tf_op jit(solution)/shard_map/ppermute | solution.py:215
  36.4 3.6 %plane_grad_2.1 = (f32[9,32,256]{2,1,0:T(8,128)S(1)}, f32[9,32,256]{2,1,0:T(8,128)S(1)}) custom-call(f32[256,256]{1,0:T(8,128)S(1)} %bitcast.40, f32[256,256]{1,0:T(8,128)S(1)} %collective-permute-done.refs_1_, f32[256,256]{1,0:T(8,128)S(1)} %collective-permute-done.1.refs_2_, f32[256,256]{1,0:T(8,128)S(1)} %collective-permute-done.2.refs_3_, ...), custom_call_target="tpu_custom_call" | custom-call | flops 1811939328 | bytes 4194304 | tf_op jit(solution)/shard_map/plane_grad_2/pallas_call | solution.py:186
  43.0 2.9 %collective-permute-start.19 = (f32[9,32,256]{2,1,0:T(8,128)S(1)}, f32[9,32,256]{2,1,0:T(8,128)S(1)}, u32[]{:S(2)}, u32[]{:S(2)}) collective-permute-start(f32[9,32,256]{2,1,0:T(8,128)S(1)} %add.41), channel_id=1, source_target_pairs={{8,16},{16,8},{9,17},{17,9},{10,18},{18,10},{11,19},{19,11},{12,20... | collective-permute-start | bytes 884744 | tf_op jit(solution)/shard_map/ppermute | solution.py:215
  46.7 5.0 %collective-permute-done.20 = f32[9,32,256]{2,1,0:T(8,128)S(1)} collective-permute-done((f32[9,32,256]{2,1,0:T(8,128)S(1)}, f32[9,32,256]{2,1,0:T(8,128)S(1)}, u32[]{:S(2)}, u32[]{:S(2)}) %collective-permute-start.20) | collective-permute-done | bytes 294944 | tf_op jit(solution)/shard_map/ppermute | solution.py:215
  54.8 2.9 %collective-permute-start.22 = (f32[9,32,256]{2,1,0:T(8,128)S(1)}, f32[9,32,256]{2,1,0:T(8,128)S(1)}, u32[]{:S(2)}, u32[]{:S(2)}) collective-permute-start(f32[9,32,256]{2,1,0:T(8,128)S(1)} %add.43), channel_id=1, source_target_pairs={{8,16},{16,8},{9,17},{17,9},{10,18},{18,10},{11,19},{19,11},{12,20... | collective-permute-start | bytes 884744 | tf_op jit(solution)/shard_map/ppermute | solution.py:215
  59.9 4.2 %collective-permute-done.22 = f32[9,32,256]{2,1,0:T(8,128)S(1)} collective-permute-done((f32[9,32,256]{2,1,0:T(8,128)S(1)}, f32[9,32,256]{2,1,0:T(8,128)S(1)}, u32[]{:S(2)}, u32[]{:S(2)}) %collective-permute-start.22) | collective-permute-done | bytes 294944 | tf_op jit(solution)/shard_map/ppermute | solution.py:215
  65.5 2.9 %collective-permute-start.28 = (f32[9,32,256]{2,1,0:T(8,128)S(1)}, f32[9,32,256]{2,1,0:T(8,128)S(1)}, u32[]{:S(2)}, u32[]{:S(2)}) collective-permute-start(f32[9,32,256]{2,1,0:T(8,128)S(1)} %add.45), channel_id=1, source_target_pairs={{8,16},{16,8},{9,17},{17,9},{10,18},{18,10},{11,19},{19,11},{12,20... | collective-permute-start | bytes 884744 | tf_op jit(solution)/shard_map/ppermute | solution.py:215
  69.9 2.5 %conv_0.1 = (f32[256,256]{1,0:T(8,128)S(1)}, f32[256,256]{1,0:T(8,128)S(1)}) custom-call(f32[6,10,8,256]{3,2,1,0:T(8,128)S(1)} %get-tuple-element.113.refs_0_, f32[6,10,8,256]{3,2,1,0:T(8,128)S(1)} %pad_maximum_fusion.5.refs_1_, f32[6,10,8,256]{3,2,1,0:T(8,128)S(1)} %get-tuple-element.115.refs_2_, f32[6,10,8,256]{3,2,1,0:T(8,128)S(1)} %get-tuple-element.116.refs_3_, ...), custom_call_target="tpu_custom_call" | custom-call | flops 1811939328 | bytes 4194304 | tf_op jit(solution)/shard_map/conv_0/pallas_call | solution.py:90
  80.5 2.5 %conv_1.1 = (f32[256,256]{1,0:T(8,128)S(1)}, f32[256,256]{1,0:T(8,128)S(1)}) custom-call(f32[6,10,8,256]{3,2,1,0:T(8,128)S(1)} %get-tuple-element.113.refs_0_, f32[6,10,8,256]{3,2,1,0:T(8,128)S(1)} %pad_maximum_fusion.5.refs_1_, f32[6,10,8,256]{3,2,1,0:T(8,128)S(1)} %get-tuple-element.115.refs_2_, f32[6,10,8,256]{3,2,1,0:T(8,128)S(1)} %get-tuple-element.116.refs_3_, ...), custom_call_target="tpu_custom_call" | custom-call | flops 1811939328 | bytes 4194304 | tf_op jit(solution)/shard_map/conv_1/pallas_call | solution.py:90
  83.0 3.6 %collective-permute-done.30 = f32[4,32,256]{2,1,0:T(8,128)S(1)} collective-permute-done((f32[4,32,256]{2,1,0:T(8,128)S(1)}, f32[4,32,256]{2,1,0:T(8,128)S(1)}, u32[]{:S(2)}, u32[]{:S(2)}) %collective-permute-start.30) | collective-permute-done | bytes 131104 | tf_op jit(solution)/shard_map/ppermute | solution.py:215
  88.0 2.3 %collective-permute-start.37 = (f32[4,2,1,32,256]{4,3,0,2,1:T(8,128)S(1)}, f32[4,2,1,32,256]{4,3,0,2,1:T(8,128)S(1)}, u32[]{:S(2)}, u32[]{:S(2)}) collective-permute-start(f32[4,2,1,32,256]{4,3,0,2,1:T(8,128)S(1)} %maximum_select_fusion.4), channel_id=1, source_target_pairs={{0,2},{2,0},{4,6},{6,4},{1,3},{3,1},{5,7},{7,5},{8,10},{10,8},{12,... | collective-permute-start | bytes 786440 | tf_op jit(solution)/shard_map/ppermute | solution.py:215
  91.2 3.2 %conv_2.1 = (f32[256,256]{1,0:T(8,128)}, f32[256,256]{1,0:T(8,128)}) custom-call(f32[6,10,8,256]{3,2,1,0:T(8,128)S(1)} %get-tuple-element.113.refs_0_, f32[6,10,8,256]{3,2,1,0:T(8,128)S(1)} %pad_maximum_fusion.5.refs_1_, f32[6,10,8,256]{3,2,1,0:T(8,128)S(1)} %get-tuple-element.115.refs_2_, f32[6,10,8,256]{3,2,1,0:T(8,128)S(1)} %get-tuple-element.116.refs_3_, ...), custom_call_target="tpu_custom_call" | custom-call | flops 1811939328 | bytes 4194304 | tf_op jit(solution)/shard_map/conv_2/pallas_call | solution.py:90
  94.4 3.6 %collective-permute-done.35 = f32[4,32,256]{2,1,0:T(8,128)S(1)} collective-permute-done((f32[4,32,256]{2,1,0:T(8,128)S(1)}, f32[4,32,256]{2,1,0:T(8,128)S(1)}, u32[]{:S(2)}, u32[]{:S(2)}) %collective-permute-start.35) | collective-permute-done | bytes 131104 | tf_op jit(solution)/shard_map/ppermute | solution.py:215
  100.0 2.5 %collective-permute-start.39 = (f32[4,2,1,32,256]{4,3,0,2,1:T(8,128)S(1)}, f32[4,2,1,32,256]{4,3,0,2,1:T(8,128)S(1)}, u32[]{:S(2)}, u32[]{:S(2)}) collective-permute-start(f32[4,2,1,32,256]{4,3,0,2,1:T(8,128)S(1)} %maximum_select_fusion.5), channel_id=1, source_target_pairs={{0,2},{2,0},{4,6},{6,4},{1,3},{3,1},{5,7},{7,5},{8,10},{10,8},{12,... | collective-permute-start | bytes 786440 | tf_op jit(solution)/shard_map/ppermute | solution.py:215
  102.6 4.4 %collective-permute-done.39 = f32[4,2,1,32,256]{4,3,0,2,1:T(8,128)S(1)} collective-permute-done((f32[4,2,1,32,256]{4,3,0,2,1:T(8,128)S(1)}, f32[4,2,1,32,256]{4,3,0,2,1:T(8,128)S(1)}, u32[]{:S(2)}, u32[]{:S(2)}) %collective-permute-start.39) | collective-permute-done | bytes 262176 | tf_op jit(solution)/shard_map/ppermute | solution.py:215
  107.3 1.8 %copy-done.7 = f32[27,2,2,32,256]{4,3,2,1,0:T(8,128)} copy-done((f32[27,2,2,32,256]{4,3,2,1,0:T(8,128)}, f32[27,2,2,32,256]{4,3,2,1,0:T(8,128)S(1)}, u32[]{:S(2)}) %copy-start.7) | copy-done | bytes 3538968
  (143 shorter events, 38.7 us)
Async XLA Ops:
  0.7 17.7 %collective-permute-start = (f32[256,256]{1,0:T(8,128)}, f32[256,256]{1,0:T(8,128)S(1)}, u32[]{:S(2)}, u32[]{:S(2)}) collective-permute-start(f32[256,256]{1,0:T(8,128)} %bitcast.36), channel_id=1, source_target_pairs={{2,0},{4,2},{6,4},{0,6},{3,1},{5,3},{7,5},{1,7},{10,8},{12,10},{14... | collective-permute-start | bytes 786440 | tf_op jit(solution)/shard_map/ppermute | solution.py:215
  5.8 7.6 %collective-permute-start.5 = (f32[2,8,8,256]{3,2,1,0:T(8,128)S(1)}, f32[2,8,8,256]{3,2,1,0:T(8,128)S(1)}, u32[]{:S(2)}, u32[]{:S(2)}) collective-permute-start(f32[2,8,8,256]{3,2,1,0:T(8,128)S(1)} %pad_maximum_fusion.9), channel_id=1, source_target_pairs={{8,0},{16,8},{24,16},{0,24},{9,1},{17,9},{25,17},{1,25},{10,2},{18... | collective-permute-start | bytes 393224 | tf_op jit(solution)/shard_map/ppermute | solution.py:215
  6.3 13.6 %collective-permute-start.1 = (f32[256,256]{1,0:T(8,128)}, f32[256,256]{1,0:T(8,128)S(1)}, u32[]{:S(2)}, u32[]{:S(2)}) collective-permute-start(f32[256,256]{1,0:T(8,128)} %bitcast.37), channel_id=1, source_target_pairs={{4,0},{6,2},{0,4},{2,6},{5,1},{7,3},{1,5},{3,7},{12,8},{14,10},{8,... | collective-permute-start | bytes 786440 | tf_op jit(solution)/shard_map/ppermute | solution.py:215
  7.1 12.9 %collective-permute-start.2 = (f32[256,256]{1,0:T(8,128)}, f32[256,256]{1,0:T(8,128)S(1)}, u32[]{:S(2)}, u32[]{:S(2)}) collective-permute-start(f32[256,256]{1,0:T(8,128)} %bitcast.38), channel_id=1, source_target_pairs={{6,0},{0,2},{2,4},{4,6},{7,1},{1,3},{3,5},{5,7},{14,8},{8,10},{10,... | collective-permute-start | bytes 786440 | tf_op jit(solution)/shard_map/ppermute | solution.py:215
  20.0 7.8 %collective-permute-start.6 = (f32[256,256]{1,0:T(8,128)S(1)}, f32[256,256]{1,0:T(8,128)S(1)}, u32[]{:S(2)}, u32[]{:S(2)}) collective-permute-start(f32[256,256]{1,0:T(8,128)S(1)} %collective-permute-done.refs_1_), channel_id=1, source_target_pairs={{0,1},{1,0},{2,3},{3,2},{4,5},{5,4},{6,7},{7,6},{8,9},{9,8},{10,11... | collective-permute-start | bytes 786440 | tf_op jit(solution)/shard_map/ppermute | solution.py:215
  32.0 11.0 %collective-permute-start.16 = (f32[9,32,256]{2,1,0:T(8,128)S(1)}, f32[9,32,256]{2,1,0:T(8,128)S(1)}, u32[]{:S(2)}, u32[]{:S(2)}) collective-permute-start(f32[9,32,256]{2,1,0:T(8,128)S(1)} %plane_grad_1.1), channel_id=1, source_target_pairs={{0,8},{24,16},{1,9},{25,17},{2,10},{26,18},{3,11},{27,19},{4,12},{... | collective-permute-start | bytes 884744 | tf_op jit(solution)/shard_map/ppermute | solution.py:215
  33.4 9.6 %collective-permute-start.17 = (f32[8,1,8,256]{3,2,1,0:T(8,128)S(1)}, f32[8,1,8,256]{3,2,1,0:T(8,128)S(1)}, u32[]{:S(2)}, u32[]{:S(2)}) collective-permute-start(f32[8,1,8,256]{3,2,1,0:T(8,128)S(1)} %pad_maximum_fusion.14), channel_id=1, source_target_pairs={{0,2},{2,4},{4,6},{6,0},{1,3},{3,5},{5,7},{7,1},{8,10},{10,12},{12... | collective-permute-start | bytes 196616 | tf_op jit(solution)/shard_map/ppermute | solution.py:215
  33.6 9.4 %collective-permute-start.18 = (f32[8,1,8,256]{3,2,1,0:T(8,128)S(1)}, f32[8,1,8,256]{3,2,1,0:T(8,128)S(1)}, u32[]{:S(2)}, u32[]{:S(2)}) collective-permute-start(f32[8,1,8,256]{3,2,1,0:T(8,128)S(1)} %pad_maximum_fusion.13), channel_id=1, source_target_pairs={{2,0},{4,2},{6,4},{0,6},{3,1},{5,3},{7,5},{1,7},{10,8},{12,10},{14... | collective-permute-start | bytes 196616 | tf_op jit(solution)/shard_map/ppermute | solution.py:215
  39.9 11.8 %collective-permute-start.20 = (f32[9,32,256]{2,1,0:T(8,128)S(1)}, f32[9,32,256]{2,1,0:T(8,128)S(1)}, u32[]{:S(2)}, u32[]{:S(2)}) collective-permute-start(f32[9,32,256]{2,1,0:T(8,128)S(1)} %get-tuple-element.103), channel_id=1, source_target_pairs={{0,8},{24,16},{1,9},{25,17},{2,10},{26,18},{3,11},{27,19},{4,12},{... | collective-permute-start | bytes 884744 | tf_op jit(solution)/shard_map/ppermute | solution.py:215
  41.2 17.1 %collective-permute-start.23 = (f32[9,32,256]{2,1,0:T(8,128)S(1)}, f32[9,32,256]{2,1,0:T(8,128)S(1)}, u32[]{:S(2)}, u32[]{:S(2)}) collective-permute-start(f32[9,32,256]{2,1,0:T(8,128)S(1)} %get-tuple-element.107), channel_id=1, source_target_pairs={{0,8},{24,16},{1,9},{25,17},{2,10},{26,18},{3,11},{27,19},{4,12},{... | collective-permute-start | bytes 884744 | tf_op jit(solution)/shard_map/ppermute | solution.py:215
  43.0 10.1 %collective-permute-start.19 = (f32[9,32,256]{2,1,0:T(8,128)S(1)}, f32[9,32,256]{2,1,0:T(8,128)S(1)}, u32[]{:S(2)}, u32[]{:S(2)}) collective-permute-start(f32[9,32,256]{2,1,0:T(8,128)S(1)} %add.41), channel_id=1, source_target_pairs={{8,16},{16,8},{9,17},{17,9},{10,18},{18,10},{11,19},{19,11},{12,20... | collective-permute-start | bytes 884744 | tf_op jit(solution)/shard_map/ppermute | solution.py:215
  46.6 11.2 %collective-permute-start.24 = (f32[12,10,2,256]{3,2,1,0:T(2,128)S(1)}, f32[12,10,2,256]{3,2,1,0:T(2,128)S(1)}, u32[]{:S(2)}, u32[]{:S(2)}) collective-permute-start(f32[12,10,2,256]{3,2,1,0:T(2,128)S(1)} %pad_maximum_fusion.7), channel_id=1, source_target_pairs={{0,1},{1,0},{2,3},{3,2},{4,5},{5,4},{6,7},{7,6},{8,9},{9,8},{10,11... | collective-permute-start | bytes 737288 | tf_op jit(solution)/shard_map/ppermute | solution.py:215
  54.8 9.2 %collective-permute-start.22 = (f32[9,32,256]{2,1,0:T(8,128)S(1)}, f32[9,32,256]{2,1,0:T(8,128)S(1)}, u32[]{:S(2)}, u32[]{:S(2)}) collective-permute-start(f32[9,32,256]{2,1,0:T(8,128)S(1)} %add.43), channel_id=1, source_target_pairs={{8,16},{16,8},{9,17},{17,9},{10,18},{18,10},{11,19},{19,11},{12,20... | collective-permute-start | bytes 884744 | tf_op jit(solution)/shard_map/ppermute | solution.py:215
  64.1 9.8 %collective-permute-start.27 = (f32[9,32,256]{2,1,0:T(8,128)S(1)}, f32[9,32,256]{2,1,0:T(8,128)S(1)}, u32[]{:S(2)}, u32[]{:S(2)}) collective-permute-start(f32[9,32,256]{2,1,0:T(8,128)S(1)} %add.44), channel_id=1, source_target_pairs={{8,0},{16,24},{9,1},{17,25},{10,2},{18,26},{11,3},{19,27},{12,4},{... | collective-permute-start | bytes 884744 | tf_op jit(solution)/shard_map/ppermute | solution.py:215
  65.5 8.6 %collective-permute-start.28 = (f32[9,32,256]{2,1,0:T(8,128)S(1)}, f32[9,32,256]{2,1,0:T(8,128)S(1)}, u32[]{:S(2)}, u32[]{:S(2)}) collective-permute-start(f32[9,32,256]{2,1,0:T(8,128)S(1)} %add.45), channel_id=1, source_target_pairs={{8,16},{16,8},{9,17},{17,9},{10,18},{18,10},{11,19},{19,11},{12,20... | collective-permute-start | bytes 884744 | tf_op jit(solution)/shard_map/ppermute | solution.py:215
  74.2 12.4 %collective-permute-start.31 = (f32[9,32,256]{2,1,0:T(8,128)S(1)}, f32[9,32,256]{2,1,0:T(8,128)S(1)}, u32[]{:S(2)}, u32[]{:S(2)}) collective-permute-start(f32[9,32,256]{2,1,0:T(8,128)S(1)} %add.46), channel_id=1, source_target_pairs={{8,0},{16,24},{9,1},{17,25},{10,2},{18,26},{11,3},{19,27},{12,4},{... | collective-permute-start | bytes 884744 | tf_op jit(solution)/shard_map/ppermute | solution.py:215
  76.2 10.4 %collective-permute-start.32 = (f32[5,1,2,32,256]{4,3,0,2,1:T(8,128)S(1)}, f32[5,1,2,32,256]{4,3,0,2,1:T(8,128)S(1)}, u32[]{:S(2)}, u32[]{:S(2)}) collective-permute-start(f32[5,1,2,32,256]{4,3,0,2,1:T(8,128)S(1)} %get-tuple-element.154), channel_id=1, source_target_pairs={{0,4},{2,6},{4,0},{6,2},{1,5},{3,7},{5,1},{7,3},{8,12},{10,14},{12... | collective-permute-start | bytes 983048 | tf_op jit(solution)/shard_map/ppermute | solution.py:215
  77.0 9.6 %collective-permute-start.33 = (f32[4,2,1,32,256]{4,3,0,2,1:T(8,128)S(1)}, f32[4,2,1,32,256]{4,3,0,2,1:T(8,128)S(1)}, u32[]{:S(2)}, u32[]{:S(2)}) collective-permute-start(f32[4,2,1,32,256]{4,3,0,2,1:T(8,128)S(1)} %maximum_select_fusion.3), channel_id=1, source_target_pairs={{0,2},{2,0},{4,6},{6,4},{1,3},{3,1},{5,7},{7,5},{8,10},{10,8},{12,... | collective-permute-start | bytes 786440 | tf_op jit(solution)/shard_map/ppermute | solution.py:215
  78.2 8.4 %collective-permute-start.29 = (f32[5,32,256]{2,1,0:T(8,128)S(1)}, f32[5,32,256]{2,1,0:T(8,128)S(1)}, u32[]{:S(2)}, u32[]{:S(2)}) collective-permute-start(f32[5,32,256]{2,1,0:T(8,128)S(1)} %slice.175), channel_id=1, source_target_pairs={{0,2},{2,0},{4,6},{6,4},{1,3},{3,1},{5,7},{7,5},{8,10},{10,8},{12,... | collective-permute-start | bytes 491528 | tf_op jit(solution)/shard_map/ppermute | solution.py:215
  86.8 12.4 %collective-permute-start.36 = (f32[5,1,2,32,256]{4,3,0,2,1:T(8,128)S(1)}, f32[5,1,2,32,256]{4,3,0,2,1:T(8,128)S(1)}, u32[]{:S(2)}, u32[]{:S(2)}) collective-permute-start(f32[5,1,2,32,256]{4,3,0,2,1:T(8,128)S(1)} %get-tuple-element.152), channel_id=1, source_target_pairs={{0,4},{2,6},{4,0},{6,2},{1,5},{3,7},{5,1},{7,3},{8,12},{10,14},{12... | collective-permute-start | bytes 983048 | tf_op jit(solution)/shard_map/ppermute | solution.py:215
  88.0 11.2 %collective-permute-start.37 = (f32[4,2,1,32,256]{4,3,0,2,1:T(8,128)S(1)}, f32[4,2,1,32,256]{4,3,0,2,1:T(8,128)S(1)}, u32[]{:S(2)}, u32[]{:S(2)}) collective-permute-start(f32[4,2,1,32,256]{4,3,0,2,1:T(8,128)S(1)} %maximum_select_fusion.4), channel_id=1, source_target_pairs={{0,2},{2,0},{4,6},{6,4},{1,3},{3,1},{5,7},{7,5},{8,10},{10,8},{12,... | collective-permute-start | bytes 786440 | tf_op jit(solution)/shard_map/ppermute | solution.py:215
  90.4 8.8 %collective-permute-start.34 = (f32[5,32,256]{2,1,0:T(8,128)S(1)}, f32[5,32,256]{2,1,0:T(8,128)S(1)}, u32[]{:S(2)}, u32[]{:S(2)}) collective-permute-start(f32[5,32,256]{2,1,0:T(8,128)S(1)} %slice.177), channel_id=1, source_target_pairs={{0,2},{2,0},{4,6},{6,4},{1,3},{3,1},{5,7},{7,5},{8,10},{10,8},{12,... | collective-permute-start | bytes 491528 | tf_op jit(solution)/shard_map/ppermute | solution.py:215
  90.5 7.5 %collective-permute-start.35 = (f32[4,32,256]{2,1,0:T(8,128)S(1)}, f32[4,32,256]{2,1,0:T(8,128)S(1)}, u32[]{:S(2)}, u32[]{:S(2)}) collective-permute-start(f32[4,32,256]{2,1,0:T(8,128)S(1)} %slice.178), channel_id=1, source_target_pairs={{0,4},{2,6},{4,0},{6,2},{1,5},{3,7},{5,1},{7,3},{8,12},{10,14},{12... | collective-permute-start | bytes 393224 | tf_op jit(solution)/shard_map/ppermute | solution.py:215
  99.5 7.5 %collective-permute-start.38 = (f32[5,1,2,32,256]{4,3,0,2,1:T(8,128)S(1)}, f32[5,1,2,32,256]{4,3,0,2,1:T(8,128)S(1)}, u32[]{:S(2)}, u32[]{:S(2)}) collective-permute-start(f32[5,1,2,32,256]{4,3,0,2,1:T(8,128)S(1)} %get-tuple-element.150), channel_id=1, source_target_pairs={{0,4},{2,6},{4,0},{6,2},{1,5},{3,7},{5,1},{7,3},{8,12},{10,14},{12... | collective-permute-start | bytes 983048 | tf_op jit(solution)/shard_map/ppermute | solution.py:215
  (26 other events, 163.5 us)

commit v4 on v3

--- a/solution.py
+++ b/solution.py
@@ -99,23 +99,22 @@
     )(*windows, taps, *before)
 
 
-def packed(two, h, w):
-    lane = lax.broadcasted_iota(jnp.int32, (64, 128), 1)
-    total = jnp.zeros((64, 128), F32)
-    for i, x in enumerate(two):
-        left, right = x[:, :128], x[:, 128:]
-        for j, tile in enumerate((jnp.where(w == 0, left, right), jnp.where(w == 0, right, left))):
-            turned = pltpu.roll(tile, lax.rem(32 * (2 * i + j) + 128 - 32 * h, 128), 1)
-            total = jnp.where(lane // 32 == 2 * i + j, turned, total)
-    return total
-
-
 def messages_kernel(below_ref, volume_ref, above_ref, *out_refs):
     h, w = lax.axis_index("ha"), lax.axis_index("wa")
-    planes = [below_ref[0], *(volume_ref[z] for z in range(4)), above_ref[0]]
-    for k, out_ref in enumerate(out_refs):
-        for t in range(3):
-            out_ref[:, 128 * t : 128 * t + 128] = packed(planes[2 * t : 2 * t + 2], lax.rem(h + k, 4), w)
+    lane = lax.broadcasted_iota(jnp.int32, (64, 128), 1) // 32
+    for t in range(3):
+        tiles = []
+        for z in (2 * t, 2 * t + 1):
+            x = below_ref[0] if z == 0 else above_ref[0] if z == 5 else volume_ref[z - 1]
+            left, right = x[:, :128], x[:, 128:]
+            for tile in (jnp.where(w == 0, left, right), jnp.where(w == 0, right, left)):
+                tiles.append(pltpu.roll(tile, lax.rem(128 - 32 * h, 128), 1))
+        for k, out_ref in enumerate(out_refs):
+            total = tiles[0] if k == 0 else pltpu.roll(tiles[0], 128 - 32 * k, 1)
+            for j in range(1, 4):
+                shift = 32 * (j - k) % 128
+                total = jnp.where(lane == j, pltpu.roll(tiles[j], shift, 1) if shift else tiles[j], total)
+            out_ref[:, 128 * t : 128 * t + 128] = total
 
 
 def messages(below, volume, above):
@@ -125,6 +124,7 @@
         out_shape=[jax.ShapeDtypeStruct((64, 384), F32)] * 4,
         in_specs=[vmem] * 3,
         out_specs=[vmem] * 4,
+        compiler_params=pltpu.CompilerParams(vmem_limit_bytes=4 * 2**20),
         name="messages",
     )(below, volume, above)
 
@@ -230,7 +230,7 @@
 
     u_mine = around([upstream.reshape(256, channels)] * 4)
     u_other = [to(u_mine[0], "wa", SWAP)]
-    volume, upstream, _ = together(volume, upstream, u_other[0])
+    volume, upstream, u_other[0] = together(volume, upstream, u_other[0])
     below = to(jnp.stack([volume[3], upstream[3]]), "dev", UP)
     above = to(jnp.stack([volume[0], upstream[0]]), "dev", DOWN)
     parts = messages(below.reshape(2, 64, channels), volume.reshape(4, 64, channels), above.reshape(2, 64, channels))
@@ -239,24 +239,26 @@
     u_mine = u_mine[:1] + arrived
     u_other += [to(x, "wa", SWAP) for x in arrived]
     v_other = [to(x, "wa", SWAP) for x in v_mine]
-    blocks = together(*u_mine, *u_other, *v_mine, *v_other)
+    blocks = [*u_mine, *u_other, *v_mine, *v_other]
 
     (a0,) = plane_grad(scale, (1,), 1, blocks)
 
-    def edge(row):
-        return jnp.concatenate([below[:, row : row + 1], volume[:, row : row + 1], above[:, row : row + 1]], axis=0)
-
-    low_edge, high_edge, _ = together(edge(0), edge(7), a0)
-    behind, ahead = to(high_edge, "ha", UP), to(low_edge, "ha", DOWN)
     a1 = to(a0, "dev", INWARDS)
     b0, c0 = plane_grad(scale, (0, 2), 2, blocks)
     b1, c1 = to(b0, "dev", INWARDS), to(c0, "dev", INWARDS)
-    a0, behind, ahead, _ = together(a0 + a1, behind, ahead, b0)
+    a0, b0 = together(a0 + a1, b0)
     a1 = to(a0, "dev", MIDDLE)
     a1, b1 = together(a1, b1)
     a0, b0 = a0 + a1, b0 + b1
 
+    def edge(row):
+        return jnp.concatenate([below[:, row : row + 1], volume[:, row : row + 1], above[:, row : row + 1]], axis=0)
+
+    low_edge, high_edge, b0 = together(edge(0), edge(7), b0)
+    behind, ahead = to(high_edge, "ha", UP), to(low_edge, "ha", DOWN)
     a1, b1 = to(a0, "dev", OUTWARDS), to(b0, "dev", MIDDLE)
+    a1, b1, c1, behind, ahead = together(a1, b1, c1, behind, ahead)
+    a0, b0, c0 = jnp.where(end, a1, a0), b0 + b1, c0 + c1
     deep = jnp.concatenate([below, volume, above], axis=0)
     rows = jnp.concatenate([behind, deep, ahead], axis=1)
     v_rows = jnp.concatenate([rows[0:1], rows[2:7]], axis=0)
@@ -267,14 +269,12 @@
     sides = to(jnp.concatenate([both[:, :, 7:8], both[:, :, 0:1]], axis=2), "wa", SWAP)
     both = jnp.concatenate([sides[:, :, 0:1], both, sides[:, :, 1:2]], axis=2)
     windows = shifted_3(both[:6]) + shifted_3(both[6:])
-    a1, b1, c1, *windows = together(a1, b1, c1, *windows)
-    a0, b0, c0 = jnp.where(end, a1, a0), b0 + b1, c0 + c1
 
     def first_half(x):
-        return to(x[:5], "ha", pair(1)), to(x[5:], "ha", pair(2))
+        return to(x[:, :16], "ha", pair(1)), to(x[:, 16:], "ha", pair(2))
 
     def joined(x, got):
-        along_x, along_y = ([x[:5], got[0]], 2, x_bit), ([x[5:], got[1]], 1, y_bit)
+        along_x, along_y = ([x[:, :16], got[0]], 2, x_bit), ([x[:, 16:], got[1]], 1, y_bit)
         both = []
         for (own, other), axis, bit in (along_x, along_y):
             own, other = (jnp.expand_dims(t, (1, 2)) for t in (own, other))
@@ -288,28 +288,28 @@
         for part, y in ((x[0], y_bit), (far[0], 1 - y_bit)):
             total = lax.dynamic_update_slice(total, part, (tap, y, 0, 0, 0))
         for part, x in ((x[1], x_bit), (far[1], 1 - x_bit)):
-            total = lax.dynamic_update_slice(total, part, (tap + 5, 0, x, 0, 0))
+            total = lax.dynamic_update_slice(total, part, (tap, 0, x, 16, 0))
         return total
 
+    a_got = first_half(a0)
+    a2, a3, b1, c1, *windows = together(*a_got, to(b0, "dev", OUTWARDS), to(c0, "dev", MIDDLE), *windows)
+    b0, c0, a0 = jnp.where(end, b1, b0), c0 + c1, joined(a0, a_got)
+
+    a_far = second_half(a0)
+    b_got = first_half(b0)
     conv = conv_third(0, windows, taps)
-    a_got = first_half(a0)
-    a0, a1, a2, b1, c1, *conv = together(a0, *a_got, to(b0, "dev", OUTWARDS), to(c0, "dev", MIDDLE), *conv)
-    b0, c0, a0 = jnp.where(end, b1, b0), c0 + c1, joined(a0, (a1, a2))
-
-    a_far = second_half(a0)
+    c1, b2, b3, *rest = together(to(c0, "dev", OUTWARDS), *b_got, *a_far, *conv)
+    a_far, conv = rest[:2], rest[2:]
+    c0, b0 = jnp.where(end, c1, c0), joined(b0, (b2, b3))
+
+    b_far = second_half(b0)
+    c_got = first_half(c0)
     conv = conv_third(1, windows, taps, conv)
-    b_got = first_half(b0)
-    b0, b1, b2, c1, *rest = together(b0, *b_got, to(c0, "dev", OUTWARDS), *a_far, *conv)
-    a_far, conv = rest[:2], rest[2:]
-    c0, b0 = jnp.where(end, c1, c0), joined(b0, (b1, b2))
-
-    b_far = second_half(b0)
-    conv = conv_third(2, windows, taps, conv)
-    c_got = first_half(c0)
-    c0, c1, c2, *rest = together(c0, *c_got, *b_far, *conv)
+    c1, c2, *rest = together(*c_got, *b_far, *conv)
     b_far, conv = rest[:2], rest[2:]
     c0 = joined(c0, (c1, c2))
     c_far = together(*second_half(c0))
+    conv = conv_third(2, windows, taps, conv)
 
     kernel_grad = jnp.zeros((27, 2, 2, 32, channels), F32)
     kernel_grad = placed(kernel_grad, 9, a0, a_far)

time: 110 us -> 106 us (0.964)
  waiting for transfers between devices: 37.3 us -> 41.3 us
  starting transfers between devices: 43.8 us -> 40 us
  local copies, waits for them, and re-layouts: 8.93 us -> 6.9 us
  Pallas kernels: 16.3 us -> 14.7 us
    ppermute x40, waiting for transfers between devices: 37.3 us -> 41.3 us  [to(): return lax.ppermute(x, axis, where)]
    ppermute x40, starting transfers between devices: 43.8 us -> 40 us  [to(): return lax.ppermute(x, axis, where)]
    pallas_call x1, Pallas kernels: 2.18 us -> 0.6 us  [messages(): pl.pallas_call(messages_kernel, out_shape=[jax.ShapeDtypeStruct((64, 384)...]
    unnamed x20 -> x14, local copies, waits for them, and re-layouts: 4.32 us -> 3.71 us
  transfers between devices with their start and end apart: 40 -> 40, of which waited for: 19 -> 18; matrix products, arithmetic and copies ran while one was open for 5% -> 4% of each run, Pallas kernels for 13% -> 12%
where the time goes in v4:
time: 106 us
  waiting for transfers between devices  41.3 us (39%)
  starting transfers between devices  40 us (38%)
  Pallas kernels  14.7 us (14%)
  local copies, waits for them, and re-layouts  6.9 us (7%)
  other arithmetic  1.52 us (1%)
  between operations  1.22 us (1%)
    ppermute x40, waiting for transfers between devices, to(): return lax.ppermute(x, axis, where)  41.3 us
    ppermute x40, starting transfers between devices, to(): return lax.ppermute(x, axis, where)  40 us
    pallas_call x3, Pallas kernels, conv_third(): pl.pallas_call(functools.partial(conv_kernel, a), grid=(3,), in_specs=[wh...  8.13 us
    pallas_call x2, Pallas kernels, plane_grad(): pl.pallas_call(functools.partial(plane_grad_kernel, scale, planes), out_s...  5.95 us
    unnamed x14, local copies, waits for them, and re-layouts  3.71 us
  transfers between devices with their start and end apart: 40, of which 18 were waited for; matrix products, arithmetic and copies ran while one was open for 4% of the time, Pallas kernels for 12%

profile of v4, /device:TPU:8, one launch (start us, length us, event | category | flops | bytes accessed | tf_op | source)
XLA Modules:
  0.0 105.6 jit_solution(5903246052111376949)
XLA Ops:
  0.7 2.5 %collective-permute-start = (f32[256,256]{1,0:T(8,128)}, f32[256,256]{1,0:T(8,128)S(1)}, u32[]{:S(2)}, u32[]{:S(2)}) collective-permute-start(f32[256,256]{1,0:T(8,128)} %bitcast.39), channel_id=1, source_target_pairs={{2,0},{4,2},{6,4},{0,6},{3,1},{5,3},{7,5},{1,7},{10,8},{12,10},{14... | collective-permute-start | bytes 786440 | tf_op jit(solution)/shard_map/ppermute | solution.py:215
  7.4 3.3 %collective-permute-done.4 = f32[2,8,8,256]{3,2,1,0:T(8,128)S(1)} collective-permute-done((f32[2,8,8,256]{3,2,1,0:T(8,128)S(1)}, f32[2,8,8,256]{3,2,1,0:T(8,128)S(1)}, u32[]{:S(2)}, u32[]{:S(2)}) %collective-permute-start.4) | collective-permute-done | bytes 131104 | tf_op jit(solution)/shard_map/ppermute | solution.py:215
  10.7 3.0 %collective-permute-done.5 = f32[2,8,8,256]{3,2,1,0:T(8,128)S(1)} collective-permute-done((f32[2,8,8,256]{3,2,1,0:T(8,128)S(1)}, f32[2,8,8,256]{3,2,1,0:T(8,128)S(1)}, u32[]{:S(2)}, u32[]{:S(2)}) %collective-permute-start.5) | collective-permute-done | bytes 131104 | tf_op jit(solution)/shard_map/ppermute | solution.py:215
  20.5 2.9 %collective-permute-done.10.refs_10_ = f32[64,384]{1,0:T(8,128)S(1)} collective-permute-done((f32[64,384]{1,0:T(8,128)S(1)}, f32[64,384]{1,0:T(8,128)S(1)}, u32[]{:S(2)}, u32[]{:S(2)}) %collective-permute-start.10) | collective-permute-done | bytes 98336 | tf_op jit(solution)/shard_map/ppermute | solution.py:215
  26.6 2.4 %plane_grad_1.1 = f32[9,32,256]{2,1,0:T(8,128)S(1)} custom-call(f32[256,256]{1,0:T(8,128)S(1)} %bitcast.42, f32[256,256]{1,0:T(8,128)S(1)} %collective-permute-done.refs_1_, f32[256,256]{1,0:T(8,128)S(1)} %collective-permute-done.1.refs_2_, f32[256,256]{1,0:T(8,128)S(1)} %collective-permute-done.2.refs_3_, f32[256,256]{1,0:T(8,128)S(1)} %collective-permute-done.3.refs_4_, ...), custom_call_target="tpu_custom_call" | custom-call | flops 905969664 | bytes 4194304 | tf_op jit(solution)/shard_map/plane_grad_1/pallas_call | solution.py:186
  30.3 3.6 %plane_grad_2.1 = (f32[9,32,256]{2,1,0:T(8,128)S(1)}, f32[9,32,256]{2,1,0:T(8,128)S(1)}) custom-call(f32[256,256]{1,0:T(8,128)S(1)} %bitcast.43, f32[256,256]{1,0:T(8,128)S(1)} %collective-permute-done.refs_1_, f32[256,256]{1,0:T(8,128)S(1)} %collective-permute-done.1.refs_2_, f32[256,256]{1,0:T(8,128)S(1)} %collective-permute-done.2.refs_3_, ...), custom_call_target="tpu_custom_call" | custom-call | flops 1811939328 | bytes 4194304 | tf_op jit(solution)/shard_map/plane_grad_2/pallas_call | solution.py:186
  35.3 5.4 %collective-permute-done.16 = f32[9,32,256]{2,1,0:T(8,128)S(1)} collective-permute-done((f32[9,32,256]{2,1,0:T(8,128)S(1)}, f32[9,32,256]{2,1,0:T(8,128)S(1)}, u32[]{:S(2)}, u32[]{:S(2)}) %collective-permute-start.16) | collective-permute-done | bytes 294944 | tf_op jit(solution)/shard_map/ppermute | solution.py:215
  40.8 1.9 %collective-permute-start.17 = (f32[9,32,256]{2,1,0:T(8,128)S(1)}, f32[9,32,256]{2,1,0:T(8,128)S(1)}, u32[]{:S(2)}, u32[]{:S(2)}) collective-permute-start(f32[9,32,256]{2,1,0:T(8,128)S(1)} %add.41), channel_id=1, source_target_pairs={{8,16},{16,8},{9,17},{17,9},{10,18},{18,10},{11,19},{19,11},{12,20... | collective-permute-start | bytes 884744 | tf_op jit(solution)/shard_map/ppermute | solution.py:215
  44.1 2.6 %collective-permute-done.18 = f32[9,32,256]{2,1,0:T(8,128)S(1)} collective-permute-done((f32[9,32,256]{2,1,0:T(8,128)S(1)}, f32[9,32,256]{2,1,0:T(8,128)S(1)}, u32[]{:S(2)}, u32[]{:S(2)}) %collective-permute-start.18) | collective-permute-done | bytes 294944 | tf_op jit(solution)/shard_map/ppermute | solution.py:215
  46.7 3.3 %collective-permute-done.17 = f32[9,32,256]{2,1,0:T(8,128)S(1)} collective-permute-done((f32[9,32,256]{2,1,0:T(8,128)S(1)}, f32[9,32,256]{2,1,0:T(8,128)S(1)}, u32[]{:S(2)}, u32[]{:S(2)}) %collective-permute-start.17) | collective-permute-done | bytes 294944 | tf_op jit(solution)/shard_map/ppermute | solution.py:215
  51.5 2.2 %collective-permute-start.20 = (f32[9,32,256]{2,1,0:T(8,128)S(1)}, f32[9,32,256]{2,1,0:T(8,128)S(1)}, u32[]{:S(2)}, u32[]{:S(2)}) collective-permute-start(f32[9,32,256]{2,1,0:T(8,128)S(1)} %add.43), channel_id=1, source_target_pairs={{8,16},{16,8},{9,17},{17,9},{10,18},{18,10},{11,19},{19,11},{12,20... | collective-permute-start | bytes 884744 | tf_op jit(solution)/shard_map/ppermute | solution.py:215
  54.0 2.7 %collective-permute-start.23 = (f32[8,1,8,256]{3,2,1,0:T(8,128)S(1)}, f32[8,1,8,256]{3,2,1,0:T(8,128)S(1)}, u32[]{:S(2)}, u32[]{:S(2)}) collective-permute-start(f32[8,1,8,256]{3,2,1,0:T(8,128)S(1)} %pad_maximum_fusion.13), channel_id=1, source_target_pairs={{2,0},{4,2},{6,4},{0,6},{3,1},{5,3},{7,5},{1,7},{10,8},{12,10},{14... | collective-permute-start | bytes 196616 | tf_op jit(solution)/shard_map/ppermute | solution.py:215
  56.7 2.2 %collective-permute-done.22 = f32[8,1,8,256]{3,2,1,0:T(8,128)S(1)} collective-permute-done((f32[8,1,8,256]{3,2,1,0:T(8,128)S(1)}, f32[8,1,8,256]{3,2,1,0:T(8,128)S(1)}, u32[]{:S(2)}, u32[]{:S(2)}) %collective-permute-start.22) | collective-permute-done | bytes 65568 | tf_op jit(solution)/shard_map/ppermute | solution.py:215
  60.2 1.9 %collective-permute-start.24 = (f32[9,16,256]{2,1,0:T(8,128)S(1)}, f32[9,16,256]{2,1,0:T(8,128)S(1)}, u32[]{:S(2)}, u32[]{:S(2)}) collective-permute-start(f32[9,16,256]{2,1,0:T(8,128)S(1)} %get-tuple-element.142), channel_id=1, source_target_pairs={{0,2},{2,0},{4,6},{6,4},{1,3},{3,1},{5,7},{7,5},{8,10},{10,8},{12,... | collective-permute-start | bytes 442376 | tf_op jit(solution)/shard_map/ppermute | solution.py:215
  64.7 3.6 %collective-permute-start.27 = (f32[9,32,256]{2,1,0:T(8,128)S(1)}, f32[9,32,256]{2,1,0:T(8,128)S(1)}, u32[]{:S(2)}, u32[]{:S(2)}) collective-permute-start(f32[9,32,256]{2,1,0:T(8,128)S(1)} %add.45), channel_id=1, source_target_pairs={{8,16},{16,8},{9,17},{17,9},{10,18},{18,10},{11,19},{19,11},{12,20... | collective-permute-start | bytes 884744 | tf_op jit(solution)/shard_map/ppermute | solution.py:215
  71.0 2.2 %collective-permute-done.27 = f32[9,32,256]{2,1,0:T(8,128)S(1)} collective-permute-done((f32[9,32,256]{2,1,0:T(8,128)S(1)}, f32[9,32,256]{2,1,0:T(8,128)S(1)}, u32[]{:S(2)}, u32[]{:S(2)}) %collective-permute-start.27) | collective-permute-done | bytes 294944 | tf_op jit(solution)/shard_map/ppermute | solution.py:215
  76.1 2.5 %conv_0.1 = (f32[256,256]{1,0:T(8,128)S(1)}, f32[256,256]{1,0:T(8,128)S(1)}) custom-call(f32[6,10,8,256]{3,2,1,0:T(8,128)S(1)} %get-tuple-element.80.refs_0_, f32[6,10,8,256]{3,2,1,0:T(8,128)S(1)} %pad_maximum_fusion.5.refs_1_, f32[6,10,8,256]{3,2,1,0:T(8,128)S(1)} %get-tuple-element.82.refs_2_, f32[6,10,8,256]{3,2,1,0:T(8,128)S(1)} %get-tuple-element.83.refs_3_, ...), custom_call_target="tpu_custom_call" | custom-call | flops 1811939328 | bytes 4194304 | tf_op jit(solution)/shard_map/conv_0/pallas_call | solution.py:90
  78.6 3.9 %collective-permute-done.30 = f32[9,16,256]{2,1,0:T(8,128)S(1)} collective-permute-done((f32[9,16,256]{2,1,0:T(8,128)S(1)}, f32[9,16,256]{2,1,0:T(8,128)S(1)}, u32[]{:S(2)}, u32[]{:S(2)}) %collective-permute-start.30) | collective-permute-done | bytes 147488 | tf_op jit(solution)/shard_map/ppermute | solution.py:215
  84.8 1.8 %collective-permute-start.34 = (f32[9,16,256]{2,1,0:T(8,128)S(1)}, f32[9,16,256]{2,1,0:T(8,128)S(1)}, u32[]{:S(2)}, u32[]{:S(2)}) collective-permute-start(f32[9,16,256]{2,1,0:T(8,128)S(1)} %get-tuple-element.134), channel_id=1, source_target_pairs={{0,2},{2,0},{4,6},{6,4},{1,3},{3,1},{5,7},{7,5},{8,10},{10,8},{12,... | collective-permute-start | bytes 442376 | tf_op jit(solution)/shard_map/ppermute | solution.py:215
  87.0 2.5 %conv_1.1 = (f32[256,256]{1,0:T(8,128)S(1)}, f32[256,256]{1,0:T(8,128)S(1)}) custom-call(f32[6,10,8,256]{3,2,1,0:T(8,128)S(1)} %get-tuple-element.80.refs_0_, f32[6,10,8,256]{3,2,1,0:T(8,128)S(1)} %pad_maximum_fusion.5.refs_1_, f32[6,10,8,256]{3,2,1,0:T(8,128)S(1)} %get-tuple-element.82.refs_2_, f32[6,10,8,256]{3,2,1,0:T(8,128)S(1)} %get-tuple-element.83.refs_3_, ...), custom_call_target="tpu_custom_call" | custom-call | flops 1811939328 | bytes 4194304 | tf_op jit(solution)/shard_map/conv_1/pallas_call | solution.py:90
  89.5 6.2 %collective-permute-done.34 = f32[9,16,256]{2,1,0:T(8,128)S(1)} collective-permute-done((f32[9,16,256]{2,1,0:T(8,128)S(1)}, f32[9,16,256]{2,1,0:T(8,128)S(1)}, u32[]{:S(2)}, u32[]{:S(2)}) %collective-permute-start.34) | collective-permute-done | bytes 147488 | tf_op jit(solution)/shard_map/ppermute | solution.py:215
  96.9 3.2 %conv_2.1 = (f32[256,256]{1,0:T(8,128)}, f32[256,256]{1,0:T(8,128)}) custom-call(f32[6,10,8,256]{3,2,1,0:T(8,128)S(1)} %get-tuple-element.80.refs_0_, f32[6,10,8,256]{3,2,1,0:T(8,128)S(1)} %pad_maximum_fusion.5.refs_1_, f32[6,10,8,256]{3,2,1,0:T(8,128)S(1)} %get-tuple-element.82.refs_2_, f32[6,10,8,256]{3,2,1,0:T(8,128)S(1)} %get-tuple-element.83.refs_3_, ...), custom_call_target="tpu_custom_call" | custom-call | flops 1811939328 | bytes 4194304 | tf_op jit(solution)/shard_map/conv_2/pallas_call | solution.py:90
  100.2 2.9 %collective-permute-done.38 = f32[9,1,2,16,256]{4,3,0,2,1:T(8,128)S(1)} collective-permute-done((f32[9,1,2,16,256]{4,3,0,2,1:T(8,128)S(1)}, f32[9,1,2,16,256]{4,3,0,2,1:T(8,128)S(1)}, u32[]{:S(2)}, u32[]{:S(2)}) %collective-permute-start.38) | collective-permute-done | bytes 294944 | tf_op jit(solution)/shard_map/ppermute | solution.py:215
  103.8 1.8 %copy-done.4 = f32[27,2,2,32,256]{4,3,2,1,0:T(8,128)} copy-done((f32[27,2,2,32,256]{4,3,2,1,0:T(8,128)}, f32[27,2,2,32,256]{4,3,2,1,0:T(8,128)S(1)}, u32[]{:S(2)}) %copy-start.4) | copy-done | bytes 3538968
  (128 shorter events, 34.0 us)
Async XLA Ops:
  0.7 16.7 %collective-permute-start = (f32[256,256]{1,0:T(8,128)}, f32[256,256]{1,0:T(8,128)S(1)}, u32[]{:S(2)}, u32[]{:S(2)}) collective-permute-start(f32[256,256]{1,0:T(8,128)} %bitcast.39), channel_id=1, source_target_pairs={{2,0},{4,2},{6,4},{0,6},{3,1},{5,3},{7,5},{1,7},{10,8},{12,10},{14... | collective-permute-start | bytes 786440 | tf_op jit(solution)/shard_map/ppermute | solution.py:215
  3.2 15.6 %collective-permute-start.1 = (f32[256,256]{1,0:T(8,128)}, f32[256,256]{1,0:T(8,128)S(1)}, u32[]{:S(2)}, u32[]{:S(2)}) collective-permute-start(f32[256,256]{1,0:T(8,128)} %bitcast.40), channel_id=1, source_target_pairs={{4,0},{6,2},{0,4},{2,6},{5,1},{7,3},{1,5},{3,7},{12,8},{14,10},{8,... | collective-permute-start | bytes 786440 | tf_op jit(solution)/shard_map/ppermute | solution.py:215
  6.3 7.4 %collective-permute-start.5 = (f32[2,8,8,256]{3,2,1,0:T(8,128)S(1)}, f32[2,8,8,256]{3,2,1,0:T(8,128)S(1)}, u32[]{:S(2)}, u32[]{:S(2)}) collective-permute-start(f32[2,8,8,256]{3,2,1,0:T(8,128)S(1)} %pad_maximum_fusion.9), channel_id=1, source_target_pairs={{8,0},{16,8},{24,16},{0,24},{9,1},{17,9},{25,17},{1,25},{10,2},{18... | collective-permute-start | bytes 393224 | tf_op jit(solution)/shard_map/ppermute | solution.py:215
  6.8 13.2 %collective-permute-start.2 = (f32[256,256]{1,0:T(8,128)}, f32[256,256]{1,0:T(8,128)S(1)}, u32[]{:S(2)}, u32[]{:S(2)}) collective-permute-start(f32[256,256]{1,0:T(8,128)} %bitcast.41), channel_id=1, source_target_pairs={{6,0},{0,2},{2,4},{4,6},{7,1},{1,3},{3,5},{5,7},{14,8},{8,10},{10,... | collective-permute-start | bytes 786440 | tf_op jit(solution)/shard_map/ppermute | solution.py:215
  29.0 11.8 %collective-permute-start.16 = (f32[9,32,256]{2,1,0:T(8,128)S(1)}, f32[9,32,256]{2,1,0:T(8,128)S(1)}, u32[]{:S(2)}, u32[]{:S(2)}) collective-permute-start(f32[9,32,256]{2,1,0:T(8,128)S(1)} %plane_grad_1.1), channel_id=1, source_target_pairs={{0,8},{24,16},{1,9},{25,17},{2,10},{26,18},{3,11},{27,19},{4,12},{... | collective-permute-start | bytes 884744 | tf_op jit(solution)/shard_map/ppermute | solution.py:215
  33.9 12.8 %collective-permute-start.18 = (f32[9,32,256]{2,1,0:T(8,128)S(1)}, f32[9,32,256]{2,1,0:T(8,128)S(1)}, u32[]{:S(2)}, u32[]{:S(2)}) collective-permute-start(f32[9,32,256]{2,1,0:T(8,128)S(1)} %get-tuple-element.69), channel_id=1, source_target_pairs={{0,8},{24,16},{1,9},{25,17},{2,10},{26,18},{3,11},{27,19},{4,12},{... | collective-permute-start | bytes 884744 | tf_op jit(solution)/shard_map/ppermute | solution.py:215
  40.8 9.3 %collective-permute-start.17 = (f32[9,32,256]{2,1,0:T(8,128)S(1)}, f32[9,32,256]{2,1,0:T(8,128)S(1)}, u32[]{:S(2)}, u32[]{:S(2)}) collective-permute-start(f32[9,32,256]{2,1,0:T(8,128)S(1)} %add.41), channel_id=1, source_target_pairs={{8,16},{16,8},{9,17},{17,9},{10,18},{18,10},{11,19},{19,11},{12,20... | collective-permute-start | bytes 884744 | tf_op jit(solution)/shard_map/ppermute | solution.py:215
  42.8 13.9 %collective-permute-start.21 = (f32[9,32,256]{2,1,0:T(8,128)S(1)}, f32[9,32,256]{2,1,0:T(8,128)S(1)}, u32[]{:S(2)}, u32[]{:S(2)}) collective-permute-start(f32[9,32,256]{2,1,0:T(8,128)S(1)} %get-tuple-element.72), channel_id=1, source_target_pairs={{0,8},{24,16},{1,9},{25,17},{2,10},{26,18},{3,11},{27,19},{4,12},{... | collective-permute-start | bytes 884744 | tf_op jit(solution)/shard_map/ppermute | solution.py:215
  50.1 9.0 %collective-permute-start.19 = (f32[9,32,256]{2,1,0:T(8,128)S(1)}, f32[9,32,256]{2,1,0:T(8,128)S(1)}, u32[]{:S(2)}, u32[]{:S(2)}) collective-permute-start(f32[9,32,256]{2,1,0:T(8,128)S(1)} %add.42), channel_id=1, source_target_pairs={{8,0},{16,24},{9,1},{17,25},{10,2},{18,26},{11,3},{19,27},{12,4},{... | collective-permute-start | bytes 884744 | tf_op jit(solution)/shard_map/ppermute | solution.py:215
  51.5 8.6 %collective-permute-start.20 = (f32[9,32,256]{2,1,0:T(8,128)S(1)}, f32[9,32,256]{2,1,0:T(8,128)S(1)}, u32[]{:S(2)}, u32[]{:S(2)}) collective-permute-start(f32[9,32,256]{2,1,0:T(8,128)S(1)} %add.43), channel_id=1, source_target_pairs={{8,16},{16,8},{9,17},{17,9},{10,18},{18,10},{11,19},{19,11},{12,20... | collective-permute-start | bytes 884744 | tf_op jit(solution)/shard_map/ppermute | solution.py:215
  60.2 8.9 %collective-permute-start.24 = (f32[9,16,256]{2,1,0:T(8,128)S(1)}, f32[9,16,256]{2,1,0:T(8,128)S(1)}, u32[]{:S(2)}, u32[]{:S(2)}) collective-permute-start(f32[9,16,256]{2,1,0:T(8,128)S(1)} %get-tuple-element.142), channel_id=1, source_target_pairs={{0,2},{2,0},{4,6},{6,4},{1,3},{3,1},{5,7},{7,5},{8,10},{10,8},{12,... | collective-permute-start | bytes 442376 | tf_op jit(solution)/shard_map/ppermute | solution.py:215
  62.1 8.0 %collective-permute-start.25 = (f32[9,16,256]{2,1,0:T(8,128)S(1)}, f32[9,16,256]{2,1,0:T(8,128)S(1)}, u32[]{:S(2)}, u32[]{:S(2)}) collective-permute-start(f32[9,16,256]{2,1,0:T(8,128)S(1)} %get-tuple-element.141), channel_id=1, source_target_pairs={{0,4},{2,6},{4,0},{6,2},{1,5},{3,7},{5,1},{7,3},{8,12},{10,14},{12... | collective-permute-start | bytes 442376 | tf_op jit(solution)/shard_map/ppermute | solution.py:215
  63.3 7.7 %collective-permute-start.26 = (f32[9,32,256]{2,1,0:T(8,128)S(1)}, f32[9,32,256]{2,1,0:T(8,128)S(1)}, u32[]{:S(2)}, u32[]{:S(2)}) collective-permute-start(f32[9,32,256]{2,1,0:T(8,128)S(1)} %add.44), channel_id=1, source_target_pairs={{8,0},{16,24},{9,1},{17,25},{10,2},{18,26},{11,3},{19,27},{12,4},{... | collective-permute-start | bytes 884744 | tf_op jit(solution)/shard_map/ppermute | solution.py:215
  64.7 8.6 %collective-permute-start.27 = (f32[9,32,256]{2,1,0:T(8,128)S(1)}, f32[9,32,256]{2,1,0:T(8,128)S(1)}, u32[]{:S(2)}, u32[]{:S(2)}) collective-permute-start(f32[9,32,256]{2,1,0:T(8,128)S(1)} %add.45), channel_id=1, source_target_pairs={{8,16},{16,8},{9,17},{17,9},{10,18},{18,10},{11,19},{19,11},{12,20... | collective-permute-start | bytes 884744 | tf_op jit(solution)/shard_map/ppermute | solution.py:215
  69.6 12.9 %collective-permute-start.32 = (f32[9,1,2,16,256]{4,3,0,2,1:T(8,128)S(1)}, f32[9,1,2,16,256]{4,3,0,2,1:T(8,128)S(1)}, u32[]{:S(2)}, u32[]{:S(2)}) collective-permute-start(f32[9,1,2,16,256]{4,3,0,2,1:T(8,128)S(1)} %get-tuple-element.114), channel_id=1, source_target_pairs={{0,4},{2,6},{4,0},{6,2},{1,5},{3,7},{5,1},{7,3},{8,12},{10,14},{12... | collective-permute-start | bytes 884744 | tf_op jit(solution)/shard_map/ppermute | solution.py:215
  70.1 12.4 %collective-permute-start.33 = (f32[9,2,1,16,256]{4,3,0,2,1:T(8,128)S(1)}, f32[9,2,1,16,256]{4,3,0,2,1:T(8,128)S(1)}, u32[]{:S(2)}, u32[]{:S(2)}) collective-permute-start(f32[9,2,1,16,256]{4,3,0,2,1:T(8,128)S(1)} %maximum_select_fusion.1), channel_id=1, source_target_pairs={{0,2},{2,0},{4,6},{6,4},{1,3},{3,1},{5,7},{7,5},{8,10},{10,8},{12,... | collective-permute-start | bytes 884744 | tf_op jit(solution)/shard_map/ppermute | solution.py:215
  73.3 9.1 %collective-permute-start.29 = (f32[9,32,256]{2,1,0:T(8,128)S(1)}, f32[9,32,256]{2,1,0:T(8,128)S(1)}, u32[]{:S(2)}, u32[]{:S(2)}) collective-permute-start(f32[9,32,256]{2,1,0:T(8,128)S(1)} %add.46), channel_id=1, source_target_pairs={{8,0},{16,24},{9,1},{17,25},{10,2},{18,26},{11,3},{19,27},{12,4},{... | collective-permute-start | bytes 884744 | tf_op jit(solution)/shard_map/ppermute | solution.py:215
  74.9 7.5 %collective-permute-start.30 = (f32[9,16,256]{2,1,0:T(8,128)S(1)}, f32[9,16,256]{2,1,0:T(8,128)S(1)}, u32[]{:S(2)}, u32[]{:S(2)}) collective-permute-start(f32[9,16,256]{2,1,0:T(8,128)S(1)} %get-tuple-element.138), channel_id=1, source_target_pairs={{0,2},{2,0},{4,6},{6,4},{1,3},{3,1},{5,7},{7,5},{8,10},{10,8},{12,... | collective-permute-start | bytes 442376 | tf_op jit(solution)/shard_map/ppermute | solution.py:215
  75.1 7.4 %collective-permute-start.31 = (f32[9,16,256]{2,1,0:T(8,128)S(1)}, f32[9,16,256]{2,1,0:T(8,128)S(1)}, u32[]{:S(2)}, u32[]{:S(2)}) collective-permute-start(f32[9,16,256]{2,1,0:T(8,128)S(1)} %get-tuple-element.137), channel_id=1, source_target_pairs={{0,4},{2,6},{4,0},{6,2},{1,5},{3,7},{5,1},{7,3},{8,12},{10,14},{12... | collective-permute-start | bytes 442376 | tf_op jit(solution)/shard_map/ppermute | solution.py:215
  82.7 13.0 %collective-permute-start.36 = (f32[9,1,2,16,256]{4,3,0,2,1:T(8,128)S(1)}, f32[9,1,2,16,256]{4,3,0,2,1:T(8,128)S(1)}, u32[]{:S(2)}, u32[]{:S(2)}) collective-permute-start(f32[9,1,2,16,256]{4,3,0,2,1:T(8,128)S(1)} %get-tuple-element.112), channel_id=1, source_target_pairs={{0,4},{2,6},{4,0},{6,2},{1,5},{3,7},{5,1},{7,3},{8,12},{10,14},{12... | collective-permute-start | bytes 884744 | tf_op jit(solution)/shard_map/ppermute | solution.py:215
  84.4 11.3 %collective-permute-start.37 = (f32[9,2,1,16,256]{4,3,0,2,1:T(8,128)S(1)}, f32[9,2,1,16,256]{4,3,0,2,1:T(8,128)S(1)}, u32[]{:S(2)}, u32[]{:S(2)}) collective-permute-start(f32[9,2,1,16,256]{4,3,0,2,1:T(8,128)S(1)} %maximum_select_fusion.3), channel_id=1, source_target_pairs={{0,2},{2,0},{4,6},{6,4},{1,3},{3,1},{5,7},{7,5},{8,10},{10,8},{12,... | collective-permute-start | bytes 884744 | tf_op jit(solution)/shard_map/ppermute | solution.py:215
  84.8 10.8 %collective-permute-start.34 = (f32[9,16,256]{2,1,0:T(8,128)S(1)}, f32[9,16,256]{2,1,0:T(8,128)S(1)}, u32[]{:S(2)}, u32[]{:S(2)}) collective-permute-start(f32[9,16,256]{2,1,0:T(8,128)S(1)} %get-tuple-element.134), channel_id=1, source_target_pairs={{0,2},{2,0},{4,6},{6,4},{1,3},{3,1},{5,7},{7,5},{8,10},{10,8},{12,... | collective-permute-start | bytes 442376 | tf_op jit(solution)/shard_map/ppermute | solution.py:215
  86.6 9.0 %collective-permute-start.35 = (f32[9,16,256]{2,1,0:T(8,128)S(1)}, f32[9,16,256]{2,1,0:T(8,128)S(1)}, u32[]{:S(2)}, u32[]{:S(2)}) collective-permute-start(f32[9,16,256]{2,1,0:T(8,128)S(1)} %get-tuple-element.133), channel_id=1, source_target_pairs={{0,4},{2,6},{4,0},{6,2},{1,5},{3,7},{5,1},{7,3},{8,12},{10,14},{12... | collective-permute-start | bytes 442376 | tf_op jit(solution)/shard_map/ppermute | solution.py:215
  95.9 7.2 %collective-permute-start.38 = (f32[9,1,2,16,256]{4,3,0,2,1:T(8,128)S(1)}, f32[9,1,2,16,256]{4,3,0,2,1:T(8,128)S(1)}, u32[]{:S(2)}, u32[]{:S(2)}) collective-permute-start(f32[9,1,2,16,256]{4,3,0,2,1:T(8,128)S(1)} %get-tuple-element.110), channel_id=1, source_target_pairs={{0,4},{2,6},{4,0},{6,2},{1,5},{3,7},{5,1},{7,3},{8,12},{10,14},{12... | collective-permute-start | bytes 884744 | tf_op jit(solution)/shard_map/ppermute | solution.py:215
  (23 other events, 149.9 us)

commit v5 on v4

--- a/solution.py
+++ b/solution.py
@@ -195,6 +195,37 @@
     )(*blocks)
 
 
+def placed_kernel(firsts, *refs):
+    pieces, out_ref, sems = refs[: 4 * len(firsts)], refs[-2], refs[-1]
+    h = lax.axis_index("ha")
+    copies = []
+    for i, ref in enumerate(pieces):
+        last = i % 2
+        near, far = (2, 1) if last else (1, 2)
+        for j in range(2):
+            chip = h ^ (near * j + (far if i % 4 >= 2 else 0))
+            rows = pl.ds(pl.multiple_of(32 * chip + 16 * last, 16), 16)
+            copies.append(pltpu.make_async_copy(ref.at[j], out_ref.at[pl.ds(firsts[i // 4], ref.shape[1]), rows], sems.at[len(copies)]))
+            copies[-1].start()
+    for copy in copies:
+        copy.wait()
+
+
+def placed(firsts, pieces, total=None):
+    vmem, hbm = pl.BlockSpec(memory_space=pltpu.VMEM), pl.BlockSpec(memory_space=pltpu.HBM)
+    more = [] if total is None else [total]
+    return pl.pallas_call(
+        functools.partial(placed_kernel, firsts),
+        out_shape=jax.ShapeDtypeStruct((27, 128, 256), F32),
+        in_specs=[vmem] * len(pieces) + [hbm] * len(more),
+        out_specs=hbm,
+        scratch_shapes=[pltpu.SemaphoreType.DMA((2 * len(pieces),))],
+        input_output_aliases={len(pieces): 0} if more else {},
+        compiler_params=pltpu.CompilerParams(vmem_limit_bytes=4 * 2**20),
+        name=f"placed_{len(firsts)}",
+    )(*pieces, *more)
+
+
 SWAP = [(0, 1), (1, 0)]
 UP = [(i, (i + 1) % 4) for i in range(4)]
 DOWN = [((i + 1) % 4, i) for i in range(4)]
@@ -223,7 +254,6 @@
 
     z = lax.axis_index("dev")
     end = (z == 0) | (z == 3)
-    x_bit, y_bit = lax.rem(h, 2), h // 2
 
     def around(messages):
         return [messages[0]] + [to(messages[4 - k], "ha", [((i + k) % 4, i) for i in range(4)]) for k in (1, 2, 3)]
@@ -274,22 +304,10 @@
         return to(x[:, :16], "ha", pair(1)), to(x[:, 16:], "ha", pair(2))
 
     def joined(x, got):
-        along_x, along_y = ([x[:, :16], got[0]], 2, x_bit), ([x[:, 16:], got[1]], 1, y_bit)
-        both = []
-        for (own, other), axis, bit in (along_x, along_y):
-            own, other = (jnp.expand_dims(t, (1, 2)) for t in (own, other))
-            both.append(jnp.where(bit == 0, jnp.concatenate([own, other], axis), jnp.concatenate([other, own], axis)))
-        return both
+        return jnp.stack([x[:, :16], got[0]]), jnp.stack([x[:, 16:], got[1]])
 
     def second_half(x):
         return to(x[0], "ha", pair(2)), to(x[1], "ha", pair(1))
-
-    def placed(total, tap, x, far):
-        for part, y in ((x[0], y_bit), (far[0], 1 - y_bit)):
-            total = lax.dynamic_update_slice(total, part, (tap, y, 0, 0, 0))
-        for part, x in ((x[1], x_bit), (far[1], 1 - x_bit)):
-            total = lax.dynamic_update_slice(total, part, (tap, 0, x, 16, 0))
-        return total
 
     a_got = first_half(a0)
     a2, a3, b1, c1, *windows = together(*a_got, to(b0, "dev", OUTWARDS), to(c0, "dev", MIDDLE), *windows)
@@ -311,12 +329,10 @@
     c_far = together(*second_half(c0))
     conv = conv_third(2, windows, taps, conv)
 
-    kernel_grad = jnp.zeros((27, 2, 2, 32, channels), F32)
-    kernel_grad = placed(kernel_grad, 9, a0, a_far)
-    kernel_grad = placed(kernel_grad, 0, b0, b_far)
-    kernel_grad = placed(kernel_grad, 18, c0, c_far)
+    kernel_grad = placed((9, 0), (*a0, *a_far, *b0, *b_far))
+    kernel_grad = placed((18,), (*c0, *c_far), kernel_grad)
     output, volume_grad = conv
-    return output.reshape(volume.shape), volume_grad.reshape(volume.shape), kernel_grad.reshape(27, 128, channels).transpose(1, 0, 2)
+    return output.reshape(volume.shape), volume_grad.reshape(volume.shape), kernel_grad.transpose(1, 0, 2)
 
 
 def solution(mesh):

time: 106 us -> 104 us (0.981)
  waiting for transfers between devices: 41.3 us -> 35.1 us
  starting transfers between devices: 40 us -> 44.4 us
  local copies, waits for them, and re-layouts: 6.9 us -> 4.26 us
  Pallas kernels: 14.7 us -> 17.3 us
    ppermute x40, waiting for transfers between devices: 41.3 us -> 35.1 us  [to(): return lax.ppermute(x, axis, where)]
    ppermute x40, starting transfers between devices: 40 us -> 44.4 us  [to(): return lax.ppermute(x, axis, where)]
    pallas_call x0 -> x2, Pallas kernels: none -> 2.6 us  [placed(): pl.pallas_call(functools.partial(placed_kernel, firsts), out_shape=jax.Sh...]
    unnamed x14 -> x12, local copies, waits for them, and re-layouts: 3.71 us -> 1.92 us
  transfers between devices with their start and end apart: 40 -> 40, of which waited for: 18 -> 17; matrix products, arithmetic and copies ran while one was open for 4% -> 3% of each run, Pallas kernels for 12% -> 13%
where the time goes in v5:
time: 104 us
  starting transfers between devices  44.4 us (43%)
  waiting for transfers between devices  35.1 us (34%)
  Pallas kernels  17.3 us (17%)
  local copies, waits for them, and re-layouts  4.26 us (4%)
  between operations  1.3 us (1%)
  other arithmetic  1.29 us (1%)
    ppermute x40, starting transfers between devices, to(): return lax.ppermute(x, axis, where)  44.4 us
    ppermute x40, waiting for transfers between devices, to(): return lax.ppermute(x, axis, where)  35.1 us
    pallas_call x3, Pallas kernels, conv_third(): pl.pallas_call(functools.partial(conv_kernel, a), grid=(3,), in_specs=[wh...  8.14 us
    pallas_call x2, Pallas kernels, plane_grad(): pl.pallas_call(functools.partial(plane_grad_kernel, scale, planes), out_s...  5.95 us
    pallas_call x2, Pallas kernels, placed(): pl.pallas_call(functools.partial(placed_kernel, firsts), out_shape=jax.Sh...  2.6 us
  transfers between devices with their start and end apart: 40, of which 17 were waited for; matrix products, arithmetic and copies ran while one was open for 3% of the time, Pallas kernels for 13%

profile of v5, /device:TPU:8, one launch (start us, length us, event | category | flops | bytes accessed | tf_op | source)
XLA Modules:
  0.0 103.7 jit_solution(13273756104267978458)
XLA Ops:
  4.8 1.6 %collective-permute-start.4 = (f32[2,8,8,256]{3,2,1,0:T(8,128)S(1)}, f32[2,8,8,256]{3,2,1,0:T(8,128)S(1)}, u32[]{:S(2)}, u32[]{:S(2)}) collective-permute-start(f32[2,8,8,256]{3,2,1,0:T(8,128)S(1)} %pad_maximum_fusion.14), channel_id=1, source_target_pairs={{0,8},{8,16},{16,24},{24,0},{1,9},{9,17},{17,25},{25,1},{2,10},{10... | collective-permute-start | bytes 393224 | tf_op jit(solution)/shard_map/ppermute | solution.py:246
  8.3 2.5 %collective-permute-done.4 = f32[2,8,8,256]{3,2,1,0:T(8,128)S(1)} collective-permute-done((f32[2,8,8,256]{3,2,1,0:T(8,128)S(1)}, f32[2,8,8,256]{3,2,1,0:T(8,128)S(1)}, u32[]{:S(2)}, u32[]{:S(2)}) %collective-permute-start.4) | collective-permute-done | bytes 131104 | tf_op jit(solution)/shard_map/ppermute | solution.py:246
  10.8 3.0 %collective-permute-done.5 = f32[2,8,8,256]{3,2,1,0:T(8,128)S(1)} collective-permute-done((f32[2,8,8,256]{3,2,1,0:T(8,128)S(1)}, f32[2,8,8,256]{3,2,1,0:T(8,128)S(1)}, u32[]{:S(2)}, u32[]{:S(2)}) %collective-permute-start.5) | collective-permute-done | bytes 131104 | tf_op jit(solution)/shard_map/ppermute | solution.py:246
  17.9 2.2 %collective-permute-done.9.refs_9_ = f32[64,384]{1,0:T(8,128)S(1)} collective-permute-done((f32[64,384]{1,0:T(8,128)S(1)}, f32[64,384]{1,0:T(8,128)S(1)}, u32[]{:S(2)}, u32[]{:S(2)}) %collective-permute-start.9) | collective-permute-done | bytes 98336 | tf_op jit(solution)/shard_map/ppermute | solution.py:246
  20.6 2.8 %collective-permute-done.10.refs_10_ = f32[64,384]{1,0:T(8,128)S(1)} collective-permute-done((f32[64,384]{1,0:T(8,128)S(1)}, f32[64,384]{1,0:T(8,128)S(1)}, u32[]{:S(2)}, u32[]{:S(2)}) %collective-permute-start.10) | collective-permute-done | bytes 98336 | tf_op jit(solution)/shard_map/ppermute | solution.py:246
  26.6 2.4 %plane_grad_1.1 = f32[9,32,256]{2,1,0:T(8,128)S(1)} custom-call(f32[256,256]{1,0:T(8,128)S(1)} %bitcast.40, f32[256,256]{1,0:T(8,128)S(1)} %collective-permute-done.refs_1_, f32[256,256]{1,0:T(8,128)S(1)} %collective-permute-done.1.refs_2_, f32[256,256]{1,0:T(8,128)S(1)} %collective-permute-done.2.refs_3_, f32[256,256]{1,0:T(8,128)S(1)} %collective-permute-done.3.refs_4_, ...), custom_call_target="tpu_custom_call" | custom-call | flops 905969664 | bytes 4194304 | tf_op jit(solution)/shard_map/plane_grad_1/pallas_call | solution.py:186
  30.3 3.6 %plane_grad_2.1 = (f32[9,32,256]{2,1,0:T(8,128)S(1)}, f32[9,32,256]{2,1,0:T(8,128)S(1)}) custom-call(f32[256,256]{1,0:T(8,128)S(1)} %bitcast.41, f32[256,256]{1,0:T(8,128)S(1)} %collective-permute-done.refs_1_, f32[256,256]{1,0:T(8,128)S(1)} %collective-permute-done.1.refs_2_, f32[256,256]{1,0:T(8,128)S(1)} %collective-permute-done.2.refs_3_, ...), custom_call_target="tpu_custom_call" | custom-call | flops 1811939328 | bytes 4194304 | tf_op jit(solution)/shard_map/plane_grad_2/pallas_call | solution.py:186
  35.3 5.4 %collective-permute-done.16 = f32[9,32,256]{2,1,0:T(8,128)S(1)} collective-permute-done((f32[9,32,256]{2,1,0:T(8,128)S(1)}, f32[9,32,256]{2,1,0:T(8,128)S(1)}, u32[]{:S(2)}, u32[]{:S(2)}) %collective-permute-start.16) | collective-permute-done | bytes 294944 | tf_op jit(solution)/shard_map/ppermute | solution.py:246
  40.7 2.2 %collective-permute-start.17 = (f32[9,32,256]{2,1,0:T(8,128)S(1)}, f32[9,32,256]{2,1,0:T(8,128)S(1)}, u32[]{:S(2)}, u32[]{:S(2)}) collective-permute-start(f32[9,32,256]{2,1,0:T(8,128)S(1)} %add.18), channel_id=1, source_target_pairs={{8,16},{16,8},{9,17},{17,9},{10,18},{18,10},{11,19},{19,11},{12,20... | collective-permute-start | bytes 884744 | tf_op jit(solution)/shard_map/ppermute | solution.py:246
  44.3 2.3 %collective-permute-done.18 = f32[9,32,256]{2,1,0:T(8,128)S(1)} collective-permute-done((f32[9,32,256]{2,1,0:T(8,128)S(1)}, f32[9,32,256]{2,1,0:T(8,128)S(1)}, u32[]{:S(2)}, u32[]{:S(2)}) %collective-permute-start.18) | collective-permute-done | bytes 294944 | tf_op jit(solution)/shard_map/ppermute | solution.py:246
  46.6 3.4 %collective-permute-done.17 = f32[9,32,256]{2,1,0:T(8,128)S(1)} collective-permute-done((f32[9,32,256]{2,1,0:T(8,128)S(1)}, f32[9,32,256]{2,1,0:T(8,128)S(1)}, u32[]{:S(2)}, u32[]{:S(2)}) %collective-permute-start.17) | collective-permute-done | bytes 294944 | tf_op jit(solution)/shard_map/ppermute | solution.py:246
  50.1 2.3 %collective-permute-start.20 = (f32[9,32,256]{2,1,0:T(8,128)S(1)}, f32[9,32,256]{2,1,0:T(8,128)S(1)}, u32[]{:S(2)}, u32[]{:S(2)}) collective-permute-start(f32[9,32,256]{2,1,0:T(8,128)S(1)} %add.20), channel_id=1, source_target_pairs={{8,16},{16,8},{9,17},{17,9},{10,18},{18,10},{11,19},{19,11},{12,20... | collective-permute-start | bytes 884744 | tf_op jit(solution)/shard_map/ppermute | solution.py:246
  53.9 2.8 %collective-permute-start.23 = (f32[8,1,8,256]{3,2,1,0:T(8,128)S(1)}, f32[8,1,8,256]{3,2,1,0:T(8,128)S(1)}, u32[]{:S(2)}, u32[]{:S(2)}) collective-permute-start(f32[8,1,8,256]{3,2,1,0:T(8,128)S(1)} %pad_maximum_fusion.19), channel_id=1, source_target_pairs={{2,0},{4,2},{6,4},{0,6},{3,1},{5,3},{7,5},{1,7},{10,8},{12,10},{14... | collective-permute-start | bytes 196616 | tf_op jit(solution)/shard_map/ppermute | solution.py:246
  56.7 2.3 %collective-permute-done.22 = f32[8,1,8,256]{3,2,1,0:T(8,128)S(1)} collective-permute-done((f32[8,1,8,256]{3,2,1,0:T(8,128)S(1)}, f32[8,1,8,256]{3,2,1,0:T(8,128)S(1)}, u32[]{:S(2)}, u32[]{:S(2)}) %collective-permute-start.22) | collective-permute-done | bytes 65568 | tf_op jit(solution)/shard_map/ppermute | solution.py:246
  60.5 2.3 %collective-permute-start.24 = (f32[9,16,256]{2,1,0:T(8,128)S(1)}, f32[9,16,256]{2,1,0:T(8,128)S(1)}, u32[]{:S(2)}, u32[]{:S(2)}) collective-permute-start(f32[9,16,256]{2,1,0:T(8,128)S(1)} %get-tuple-element.136), channel_id=1, source_target_pairs={{0,2},{2,0},{4,6},{6,4},{1,3},{3,1},{5,7},{7,5},{8,10},{10,8},{12,... | collective-permute-start | bytes 442376 | tf_op jit(solution)/shard_map/ppermute | solution.py:246
  62.8 1.8 %collective-permute-start.26 = (f32[9,32,256]{2,1,0:T(8,128)S(1)}, f32[9,32,256]{2,1,0:T(8,128)S(1)}, u32[]{:S(2)}, u32[]{:S(2)}) collective-permute-start(f32[9,32,256]{2,1,0:T(8,128)S(1)} %add.21), channel_id=1, source_target_pairs={{8,0},{16,24},{9,1},{17,25},{10,2},{18,26},{11,3},{19,27},{12,4},{... | collective-permute-start | bytes 884744 | tf_op jit(solution)/shard_map/ppermute | solution.py:246
  64.7 3.4 %collective-permute-start.27 = (f32[9,32,256]{2,1,0:T(8,128)S(1)}, f32[9,32,256]{2,1,0:T(8,128)S(1)}, u32[]{:S(2)}, u32[]{:S(2)}) collective-permute-start(f32[9,32,256]{2,1,0:T(8,128)S(1)} %add.22), channel_id=1, source_target_pairs={{8,16},{16,8},{9,17},{17,9},{10,18},{18,10},{11,19},{19,11},{12,20... | collective-permute-start | bytes 884744 | tf_op jit(solution)/shard_map/ppermute | solution.py:246
  69.4 1.9 %collective-permute-start.33 = (f32[2,9,16,256]{3,2,1,0:T(8,128)S(1)}, f32[2,9,16,256]{3,2,1,0:T(8,128)S(1)}, u32[]{:S(2)}, u32[]{:S(2)}) collective-permute-start(f32[2,9,16,256]{3,2,1,0:T(8,128)S(1)} %pad_maximum_fusion.8.refs_1_), channel_id=1, source_target_pairs={{0,2},{2,0},{4,6},{6,4},{1,3},{3,1},{5,7},{7,5},{8,10},{10,8},{12,... | collective-permute-start | bytes 884744 | tf_op jit(solution)/shard_map/ppermute | solution.py:246
  77.0 2.5 %conv_0.1 = (f32[256,256]{1,0:T(8,128)S(1)}, f32[256,256]{1,0:T(8,128)S(1)}) custom-call(f32[6,10,8,256]{3,2,1,0:T(8,128)S(1)} %get-tuple-element.80.refs_0_, f32[6,10,8,256]{3,2,1,0:T(8,128)S(1)} %pad_maximum_fusion.5.refs_1_, f32[6,10,8,256]{3,2,1,0:T(8,128)S(1)} %get-tuple-element.82.refs_2_, f32[6,10,8,256]{3,2,1,0:T(8,128)S(1)} %get-tuple-element.83.refs_3_, ...), custom_call_target="tpu_custom_call" | custom-call | flops 1811939328 | bytes 4194304 | tf_op jit(solution)/shard_map/conv_0/pallas_call | solution.py:90
  79.5 2.1 %collective-permute-done.31 = f32[9,16,256]{2,1,0:T(8,128)S(1)} collective-permute-done((f32[9,16,256]{2,1,0:T(8,128)S(1)}, f32[9,16,256]{2,1,0:T(8,128)S(1)}, u32[]{:S(2)}, u32[]{:S(2)}) %collective-permute-start.31) | collective-permute-done | bytes 147488 | tf_op jit(solution)/shard_map/ppermute | solution.py:246
  81.9 1.8 %collective-permute-start.37 = (f32[2,9,16,256]{3,2,1,0:T(8,128)S(1)}, f32[2,9,16,256]{3,2,1,0:T(8,128)S(1)}, u32[]{:S(2)}, u32[]{:S(2)}) collective-permute-start(f32[2,9,16,256]{3,2,1,0:T(8,128)S(1)} %pad_maximum_fusion.10.refs_5_), channel_id=1, source_target_pairs={{0,2},{2,0},{4,6},{6,4},{1,3},{3,1},{5,7},{7,5},{8,10},{10,8},{12,... | collective-permute-start | bytes 884744 | tf_op jit(solution)/shard_map/ppermute | solution.py:246
  86.2 2.4 %conv_1.1 = (f32[256,256]{1,0:T(8,128)S(1)}, f32[256,256]{1,0:T(8,128)S(1)}) custom-call(f32[6,10,8,256]{3,2,1,0:T(8,128)S(1)} %get-tuple-element.80.refs_0_, f32[6,10,8,256]{3,2,1,0:T(8,128)S(1)} %pad_maximum_fusion.5.refs_1_, f32[6,10,8,256]{3,2,1,0:T(8,128)S(1)} %get-tuple-element.82.refs_2_, f32[6,10,8,256]{3,2,1,0:T(8,128)S(1)} %get-tuple-element.83.refs_3_, ...), custom_call_target="tpu_custom_call" | custom-call | flops 1811939328 | bytes 4194304 | tf_op jit(solution)/shard_map/conv_1/pallas_call | solution.py:90
  88.7 6.3 %collective-permute-done.35 = f32[9,16,256]{2,1,0:T(8,128)S(1)} collective-permute-done((f32[9,16,256]{2,1,0:T(8,128)S(1)}, f32[9,16,256]{2,1,0:T(8,128)S(1)}, u32[]{:S(2)}, u32[]{:S(2)}) %collective-permute-start.35) | collective-permute-done | bytes 147488 | tf_op jit(solution)/shard_map/ppermute | solution.py:246
  98.5 3.2 %conv_2.1 = (f32[256,256]{1,0:T(8,128)}, f32[256,256]{1,0:T(8,128)}) custom-call(f32[6,10,8,256]{3,2,1,0:T(8,128)S(1)} %get-tuple-element.80.refs_0_, f32[6,10,8,256]{3,2,1,0:T(8,128)S(1)} %pad_maximum_fusion.5.refs_1_, f32[6,10,8,256]{3,2,1,0:T(8,128)S(1)} %get-tuple-element.82.refs_2_, f32[6,10,8,256]{3,2,1,0:T(8,128)S(1)} %get-tuple-element.83.refs_3_, ...), custom_call_target="tpu_custom_call" | custom-call | flops 1811939328 | bytes 4194304 | tf_op jit(solution)/shard_map/conv_2/pallas_call | solution.py:90
  (117 shorter events, 36.0 us)
Async XLA Ops:
  0.7 16.6 %collective-permute-start.2 = (f32[256,256]{1,0:T(8,128)}, f32[256,256]{1,0:T(8,128)S(1)}, u32[]{:S(2)}, u32[]{:S(2)}) collective-permute-start(f32[256,256]{1,0:T(8,128)} %bitcast.37), channel_id=1, source_target_pairs={{6,0},{0,2},{2,4},{4,6},{7,1},{1,3},{3,5},{5,7},{14,8},{8,10},{10,... | collective-permute-start | bytes 786440 | tf_op jit(solution)/shard_map/ppermute | solution.py:246
  2.3 15.6 %collective-permute-start.1 = (f32[256,256]{1,0:T(8,128)}, f32[256,256]{1,0:T(8,128)S(1)}, u32[]{:S(2)}, u32[]{:S(2)}) collective-permute-start(f32[256,256]{1,0:T(8,128)} %bitcast.38), channel_id=1, source_target_pairs={{4,0},{6,2},{0,4},{2,6},{5,1},{7,3},{1,5},{3,7},{12,8},{14,10},{8,... | collective-permute-start | bytes 786440 | tf_op jit(solution)/shard_map/ppermute | solution.py:246
  6.4 7.4 %collective-permute-start.5 = (f32[2,8,8,256]{3,2,1,0:T(8,128)S(1)}, f32[2,8,8,256]{3,2,1,0:T(8,128)S(1)}, u32[]{:S(2)}, u32[]{:S(2)}) collective-permute-start(f32[2,8,8,256]{3,2,1,0:T(8,128)S(1)} %pad_maximum_fusion.15), channel_id=1, source_target_pairs={{8,0},{16,8},{24,16},{0,24},{9,1},{17,9},{25,17},{1,25},{10,2},{18... | collective-permute-start | bytes 393224 | tf_op jit(solution)/shard_map/ppermute | solution.py:246
  6.9 13.2 %collective-permute-start = (f32[256,256]{1,0:T(8,128)}, f32[256,256]{1,0:T(8,128)S(1)}, u32[]{:S(2)}, u32[]{:S(2)}) collective-permute-start(f32[256,256]{1,0:T(8,128)} %bitcast.39), channel_id=1, source_target_pairs={{2,0},{4,2},{6,4},{0,6},{3,1},{5,3},{7,5},{1,7},{10,8},{12,10},{14... | collective-permute-start | bytes 786440 | tf_op jit(solution)/shard_map/ppermute | solution.py:246
  16.8 6.6 %collective-permute-start.10 = (f32[64,384]{1,0:T(8,128)S(1)}, f32[64,384]{1,0:T(8,128)S(1)}, u32[]{:S(2)}, u32[]{:S(2)}) collective-permute-start(f32[64,384]{1,0:T(8,128)S(1)} %get-tuple-element.64), channel_id=1, source_target_pairs={{4,0},{6,2},{0,4},{2,6},{5,1},{7,3},{1,5},{3,7},{12,8},{14,10},{8,... | collective-permute-start | bytes 294920 | tf_op jit(solution)/shard_map/ppermute | solution.py:246
  29.0 11.8 %collective-permute-start.16 = (f32[9,32,256]{2,1,0:T(8,128)S(1)}, f32[9,32,256]{2,1,0:T(8,128)S(1)}, u32[]{:S(2)}, u32[]{:S(2)}) collective-permute-start(f32[9,32,256]{2,1,0:T(8,128)S(1)} %plane_grad_1.1), channel_id=1, source_target_pairs={{0,8},{24,16},{1,9},{25,17},{2,10},{26,18},{3,11},{27,19},{4,12},{... | collective-permute-start | bytes 884744 | tf_op jit(solution)/shard_map/ppermute | solution.py:246
  33.9 12.7 %collective-permute-start.18 = (f32[9,32,256]{2,1,0:T(8,128)S(1)}, f32[9,32,256]{2,1,0:T(8,128)S(1)}, u32[]{:S(2)}, u32[]{:S(2)}) collective-permute-start(f32[9,32,256]{2,1,0:T(8,128)S(1)} %get-tuple-element.69), channel_id=1, source_target_pairs={{0,8},{24,16},{1,9},{25,17},{2,10},{26,18},{3,11},{27,19},{4,12},{... | collective-permute-start | bytes 884744 | tf_op jit(solution)/shard_map/ppermute | solution.py:246
  40.7 9.3 %collective-permute-start.17 = (f32[9,32,256]{2,1,0:T(8,128)S(1)}, f32[9,32,256]{2,1,0:T(8,128)S(1)}, u32[]{:S(2)}, u32[]{:S(2)}) collective-permute-start(f32[9,32,256]{2,1,0:T(8,128)S(1)} %add.18), channel_id=1, source_target_pairs={{8,16},{16,8},{9,17},{17,9},{10,18},{18,10},{11,19},{19,11},{12,20... | collective-permute-start | bytes 884744 | tf_op jit(solution)/shard_map/ppermute | solution.py:246
  43.0 13.7 %collective-permute-start.21 = (f32[9,32,256]{2,1,0:T(8,128)S(1)}, f32[9,32,256]{2,1,0:T(8,128)S(1)}, u32[]{:S(2)}, u32[]{:S(2)}) collective-permute-start(f32[9,32,256]{2,1,0:T(8,128)S(1)} %get-tuple-element.72), channel_id=1, source_target_pairs={{0,8},{24,16},{1,9},{25,17},{2,10},{26,18},{3,11},{27,19},{4,12},{... | collective-permute-start | bytes 884744 | tf_op jit(solution)/shard_map/ppermute | solution.py:246
  50.1 9.0 %collective-permute-start.20 = (f32[9,32,256]{2,1,0:T(8,128)S(1)}, f32[9,32,256]{2,1,0:T(8,128)S(1)}, u32[]{:S(2)}, u32[]{:S(2)}) collective-permute-start(f32[9,32,256]{2,1,0:T(8,128)S(1)} %add.20), channel_id=1, source_target_pairs={{8,16},{16,8},{9,17},{17,9},{10,18},{18,10},{11,19},{19,11},{12,20... | collective-permute-start | bytes 884744 | tf_op jit(solution)/shard_map/ppermute | solution.py:246
  52.4 6.8 %collective-permute-start.19 = (f32[9,32,256]{2,1,0:T(8,128)S(1)}, f32[9,32,256]{2,1,0:T(8,128)S(1)}, u32[]{:S(2)}, u32[]{:S(2)}) collective-permute-start(f32[9,32,256]{2,1,0:T(8,128)S(1)} %add.19), channel_id=1, source_target_pairs={{8,0},{16,24},{9,1},{17,25},{10,2},{18,26},{11,3},{19,27},{12,4},{... | collective-permute-start | bytes 884744 | tf_op jit(solution)/shard_map/ppermute | solution.py:246
  59.4 10.0 %collective-permute-start.25 = (f32[9,16,256]{2,1,0:T(8,128)S(1)}, f32[9,16,256]{2,1,0:T(8,128)S(1)}, u32[]{:S(2)}, u32[]{:S(2)}) collective-permute-start(f32[9,16,256]{2,1,0:T(8,128)S(1)} %get-tuple-element.135), channel_id=1, source_target_pairs={{0,4},{2,6},{4,0},{6,2},{1,5},{3,7},{5,1},{7,3},{8,12},{10,14},{12... | collective-permute-start | bytes 442376 | tf_op jit(solution)/shard_map/ppermute | solution.py:246
  60.5 8.4 %collective-permute-start.24 = (f32[9,16,256]{2,1,0:T(8,128)S(1)}, f32[9,16,256]{2,1,0:T(8,128)S(1)}, u32[]{:S(2)}, u32[]{:S(2)}) collective-permute-start(f32[9,16,256]{2,1,0:T(8,128)S(1)} %get-tuple-element.136), channel_id=1, source_target_pairs={{0,2},{2,0},{4,6},{6,4},{1,3},{3,1},{5,7},{7,5},{8,10},{10,8},{12,... | collective-permute-start | bytes 442376 | tf_op jit(solution)/shard_map/ppermute | solution.py:246
  62.8 9.0 %collective-permute-start.26 = (f32[9,32,256]{2,1,0:T(8,128)S(1)}, f32[9,32,256]{2,1,0:T(8,128)S(1)}, u32[]{:S(2)}, u32[]{:S(2)}) collective-permute-start(f32[9,32,256]{2,1,0:T(8,128)S(1)} %add.21), channel_id=1, source_target_pairs={{8,0},{16,24},{9,1},{17,25},{10,2},{18,26},{11,3},{19,27},{12,4},{... | collective-permute-start | bytes 884744 | tf_op jit(solution)/shard_map/ppermute | solution.py:246
  64.7 8.6 %collective-permute-start.27 = (f32[9,32,256]{2,1,0:T(8,128)S(1)}, f32[9,32,256]{2,1,0:T(8,128)S(1)}, u32[]{:S(2)}, u32[]{:S(2)}) collective-permute-start(f32[9,32,256]{2,1,0:T(8,128)S(1)} %add.22), channel_id=1, source_target_pairs={{8,16},{16,8},{9,17},{17,9},{10,18},{18,10},{11,19},{19,11},{12,20... | collective-permute-start | bytes 884744 | tf_op jit(solution)/shard_map/ppermute | solution.py:246
  68.9 10.6 %collective-permute-start.32 = (f32[2,9,16,256]{3,2,1,0:T(8,128)S(1)}, f32[2,9,16,256]{3,2,1,0:T(8,128)S(1)}, u32[]{:S(2)}, u32[]{:S(2)}) collective-permute-start(f32[2,9,16,256]{3,2,1,0:T(8,128)S(1)} %pad_maximum_fusion.7.refs_0_), channel_id=1, source_target_pairs={{0,4},{2,6},{4,0},{6,2},{1,5},{3,7},{5,1},{7,3},{8,12},{10,14},{12... | collective-permute-start | bytes 884744 | tf_op jit(solution)/shard_map/ppermute | solution.py:246
  69.4 10.1 %collective-permute-start.33 = (f32[2,9,16,256]{3,2,1,0:T(8,128)S(1)}, f32[2,9,16,256]{3,2,1,0:T(8,128)S(1)}, u32[]{:S(2)}, u32[]{:S(2)}) collective-permute-start(f32[2,9,16,256]{3,2,1,0:T(8,128)S(1)} %pad_maximum_fusion.8.refs_1_), channel_id=1, source_target_pairs={{0,2},{2,0},{4,6},{6,4},{1,3},{3,1},{5,7},{7,5},{8,10},{10,8},{12,... | collective-permute-start | bytes 884744 | tf_op jit(solution)/shard_map/ppermute | solution.py:246
  73.4 8.4 %collective-permute-start.29 = (f32[9,32,256]{2,1,0:T(8,128)S(1)}, f32[9,32,256]{2,1,0:T(8,128)S(1)}, u32[]{:S(2)}, u32[]{:S(2)}) collective-permute-start(f32[9,32,256]{2,1,0:T(8,128)S(1)} %add.23), channel_id=1, source_target_pairs={{8,0},{16,24},{9,1},{17,25},{10,2},{18,26},{11,3},{19,27},{12,4},{... | collective-permute-start | bytes 884744 | tf_op jit(solution)/shard_map/ppermute | solution.py:246
  81.9 13.1 %collective-permute-start.37 = (f32[2,9,16,256]{3,2,1,0:T(8,128)S(1)}, f32[2,9,16,256]{3,2,1,0:T(8,128)S(1)}, u32[]{:S(2)}, u32[]{:S(2)}) collective-permute-start(f32[2,9,16,256]{3,2,1,0:T(8,128)S(1)} %pad_maximum_fusion.10.refs_5_), channel_id=1, source_target_pairs={{0,2},{2,0},{4,6},{6,4},{1,3},{3,1},{5,7},{7,5},{8,10},{10,8},{12,... | collective-permute-start | bytes 884744 | tf_op jit(solution)/shard_map/ppermute | solution.py:246
  83.7 11.3 %collective-permute-start.36 = (f32[2,9,16,256]{3,2,1,0:T(8,128)S(1)}, f32[2,9,16,256]{3,2,1,0:T(8,128)S(1)}, u32[]{:S(2)}, u32[]{:S(2)}) collective-permute-start(f32[2,9,16,256]{3,2,1,0:T(8,128)S(1)} %pad_maximum_fusion.9.refs_4_), channel_id=1, source_target_pairs={{0,4},{2,6},{4,0},{6,2},{1,5},{3,7},{5,1},{7,3},{8,12},{10,14},{12... | collective-permute-start | bytes 884744 | tf_op jit(solution)/shard_map/ppermute | solution.py:246
  84.5 10.5 %collective-permute-start.35 = (f32[9,16,256]{2,1,0:T(8,128)S(1)}, f32[9,16,256]{2,1,0:T(8,128)S(1)}, u32[]{:S(2)}, u32[]{:S(2)}) collective-permute-start(f32[9,16,256]{2,1,0:T(8,128)S(1)} %get-tuple-element.127), channel_id=1, source_target_pairs={{0,4},{2,6},{4,0},{6,2},{1,5},{3,7},{5,1},{7,3},{8,12},{10,14},{12... | collective-permute-start | bytes 442376 | tf_op jit(solution)/shard_map/ppermute | solution.py:246
  85.9 9.0 %collective-permute-start.34 = (f32[9,16,256]{2,1,0:T(8,128)S(1)}, f32[9,16,256]{2,1,0:T(8,128)S(1)}, u32[]{:S(2)}, u32[]{:S(2)}) collective-permute-start(f32[9,16,256]{2,1,0:T(8,128)S(1)} %get-tuple-element.128), channel_id=1, source_target_pairs={{0,2},{2,0},{4,6},{6,4},{1,3},{3,1},{5,7},{7,5},{8,10},{10,8},{12,... | collective-permute-start | bytes 442376 | tf_op jit(solution)/shard_map/ppermute | solution.py:246
  95.0 7.2 %collective-permute-start.39 = (f32[2,9,16,256]{3,2,1,0:T(8,128)S(1)}, f32[2,9,16,256]{3,2,1,0:T(8,128)S(1)}, u32[]{:S(2)}, u32[]{:S(2)}) collective-permute-start(f32[2,9,16,256]{3,2,1,0:T(8,128)S(1)} %pad_maximum_fusion.12.refs_1_), channel_id=1, source_target_pairs={{0,2},{2,0},{4,6},{6,4},{1,3},{3,1},{5,7},{7,5},{8,10},{10,8},{12,... | collective-permute-start | bytes 884744 | tf_op jit(solution)/shard_map/ppermute | solution.py:246
  95.4 7.0 %collective-permute-start.38 = (f32[2,9,16,256]{3,2,1,0:T(8,128)S(1)}, f32[2,9,16,256]{3,2,1,0:T(8,128)S(1)}, u32[]{:S(2)}, u32[]{:S(2)}) collective-permute-start(f32[2,9,16,256]{3,2,1,0:T(8,128)S(1)} %pad_maximum_fusion.11.refs_0_), channel_id=1, source_target_pairs={{0,4},{2,6},{4,0},{6,2},{1,5},{3,7},{5,1},{7,3},{8,12},{10,14},{12... | collective-permute-start | bytes 884744 | tf_op jit(solution)/shard_map/ppermute | solution.py:246
  (22 other events, 152.0 us)

commit v6 on v5

--- a/solution.py
+++ b/solution.py
@@ -99,13 +99,21 @@
     )(*windows, taps, *before)
 
 
-def messages_kernel(below_ref, volume_ref, above_ref, *out_refs):
+def messages_kernel(*refs):
     h, w = lax.axis_index("ha"), lax.axis_index("wa")
     lane = lax.broadcasted_iota(jnp.int32, (64, 128), 1) // 32
-    for t in range(3):
+    out_refs = refs[-4:]
+    own = len(refs) == 7
+    if own:
+        refs[2][...] = refs[1][...]
+        pairs = [(refs[0][0], refs[0][1]), (refs[0][2], refs[0][3])]
+    else:
+        pairs = [(refs[0][0], refs[1][0])]
+        for out_ref, there_ref in zip(out_refs, refs[2:6]):
+            out_ref[:, :256] = there_ref[...]
+    for t, pair_of_planes in enumerate(pairs, 0 if own else 2):
         tiles = []
-        for z in (2 * t, 2 * t + 1):
-            x = below_ref[0] if z == 0 else above_ref[0] if z == 5 else volume_ref[z - 1]
+        for x in pair_of_planes:
             left, right = x[:, :128], x[:, 128:]
             for tile in (jnp.where(w == 0, left, right), jnp.where(w == 0, right, left)):
                 tiles.append(pltpu.roll(tile, lax.rem(128 - 32 * h, 128), 1))
@@ -117,16 +125,19 @@
             out_ref[:, 128 * t : 128 * t + 128] = total
 
 
-def messages(below, volume, above):
+def messages(lanes, *arrays):
     vmem = pl.BlockSpec(memory_space=pltpu.VMEM)
+    shapes = [jax.ShapeDtypeStruct((64, lanes), F32)] * 4
+    if lanes == 256:
+        shapes = [jax.ShapeDtypeStruct(arrays[1].shape, F32), *shapes]
     return pl.pallas_call(
         messages_kernel,
-        out_shape=[jax.ShapeDtypeStruct((64, 384), F32)] * 4,
-        in_specs=[vmem] * 3,
-        out_specs=[vmem] * 4,
+        out_shape=shapes,
+        in_specs=[vmem] * len(arrays),
+        out_specs=[vmem] * len(shapes),
         compiler_params=pltpu.CompilerParams(vmem_limit_bytes=4 * 2**20),
-        name="messages",
-    )(below, volume, above)
+        name=f"messages_{lanes}",
+    )(*arrays)
 
 
 def lay_out(shifted, plane, first, second):
@@ -149,6 +160,7 @@
 
 
 def plane_of(refs, z, offset):
+    z = (1, 2, 3, 4, 0, 5).index(z)
     tile = 128 * (z // 2)
     plane = jnp.concatenate([ref[:, tile : tile + 128].reshape(8, 8, 128) for ref in refs], axis=0)
     return pltpu.roll(plane, (128 - 64 * (z % 2) - offset) % 128, 2)
@@ -260,16 +272,17 @@
 
     u_mine = around([upstream.reshape(256, channels)] * 4)
     u_other = [to(u_mine[0], "wa", SWAP)]
+    own, *parts = messages(256, volume.reshape(4, 64, channels), u_mine[0])
     volume, upstream, u_other[0] = together(volume, upstream, u_other[0])
     below = to(jnp.stack([volume[3], upstream[3]]), "dev", UP)
     above = to(jnp.stack([volume[0], upstream[0]]), "dev", DOWN)
-    parts = messages(below.reshape(2, 64, channels), volume.reshape(4, 64, channels), above.reshape(2, 64, channels))
+    parts = messages(384, below.reshape(2, 64, channels), above.reshape(2, 64, channels), *parts)
     v_mine = around(parts)
     *arrived, _ = together(*u_mine[1:], parts[0])
     u_mine = u_mine[:1] + arrived
     u_other += [to(x, "wa", SWAP) for x in arrived]
     v_other = [to(x, "wa", SWAP) for x in v_mine]
-    blocks = [*u_mine, *u_other, *v_mine, *v_other]
+    blocks = [own, *u_mine[1:], *u_other, *v_mine, *v_other]
 
     (a0,) = plane_grad(scale, (1,), 1, blocks)
 
@@ -325,7 +338,7 @@
     conv = conv_third(1, windows, taps, conv)
     c1, c2, *rest = together(*c_got, *b_far, *conv)
     b_far, conv = rest[:2], rest[2:]
-    c0 = joined(c0, (c1, c2))
+    c0 = joined(c0, c_got)
     c_far = together(*second_half(c0))
     conv = conv_third(2, windows, taps, conv)
 

time: 104 us -> 101 us (0.971)
  waiting for transfers between devices: 35.1 us -> 30.6 us
  starting transfers between devices: 44.4 us -> 45.6 us
    ppermute x40, waiting for transfers between devices: 35.1 us -> 30.6 us  [to(): return lax.ppermute(x, axis, where)]
    ppermute x40, starting transfers between devices: 44.4 us -> 45.6 us  [to(): return lax.ppermute(x, axis, where)]
  transfers between devices with their start and end apart: 40 -> 40, of which waited for: 17 -> 16; matrix products, arithmetic and copies ran while one was open for 3% -> 3% of each run, Pallas kernels for 13% -> 14%
where the time goes in v6:
time: 101 us; the launch traced here: 100 us
  starting transfers between devices  45.6 us (45%)
  waiting for transfers between devices  30.6 us (30%)
  Pallas kernels  17.3 us (17%)
  local copies, waits for them, and re-layouts  4.26 us (4%)
  other arithmetic  1.3 us (1%)
  between operations  1.28 us (1%)
    ppermute x40, starting transfers between devices, to(): return lax.ppermute(x, axis, where)  45.6 us
    ppermute x40, waiting for transfers between devices, to(): return lax.ppermute(x, axis, where)  30.6 us
    pallas_call x3, Pallas kernels, conv_third(): pl.pallas_call(functools.partial(conv_kernel, a), grid=(3,), in_specs=[wh...  8.14 us
    pallas_call x2, Pallas kernels, plane_grad(): pl.pallas_call(functools.partial(plane_grad_kernel, scale, planes), out_s...  5.89 us
    pallas_call x2, Pallas kernels, placed(): pl.pallas_call(functools.partial(placed_kernel, firsts), out_shape=jax.Sh...  2.6 us
  transfers between devices with their start and end apart: 40, of which 16 were waited for; matrix products, arithmetic and copies ran while one was open for 3% of the time, Pallas kernels for 14%

profile of v6, /device:TPU:8, one launch (start us, length us, event | category | flops | bytes accessed | tf_op | source)
XLA Modules:
  0.0 100.4 jit_solution(14526154338047920650)
XLA Ops:
  4.8 1.6 %collective-permute-start.4 = (f32[2,8,8,256]{3,2,1,0:T(8,128)S(1)}, f32[2,8,8,256]{3,2,1,0:T(8,128)S(1)}, u32[]{:S(2)}, u32[]{:S(2)}) collective-permute-start(f32[2,8,8,256]{3,2,1,0:T(8,128)S(1)} %pad_maximum_fusion.14), channel_id=1, source_target_pairs={{0,8},{8,16},{16,24},{24,0},{1,9},{9,17},{17,25},{25,1},{2,10},{10... | collective-permute-start | bytes 393224 | tf_op jit(solution)/shard_map/ppermute | solution.py:258
  10.8 3.0 %collective-permute-done.5 = f32[2,8,8,256]{3,2,1,0:T(8,128)S(1)} collective-permute-done((f32[2,8,8,256]{3,2,1,0:T(8,128)S(1)}, f32[2,8,8,256]{3,2,1,0:T(8,128)S(1)}, u32[]{:S(2)}, u32[]{:S(2)}) %collective-permute-start.5) | collective-permute-done | bytes 131104 | tf_op jit(solution)/shard_map/ppermute | solution.py:258
  16.6 2.2 %collective-permute-done.9.refs_9_ = f32[64,384]{1,0:T(8,128)S(1)} collective-permute-done((f32[64,384]{1,0:T(8,128)S(1)}, f32[64,384]{1,0:T(8,128)S(1)}, u32[]{:S(2)}, u32[]{:S(2)}) %collective-permute-start.9) | collective-permute-done | bytes 98336 | tf_op jit(solution)/shard_map/ppermute | solution.py:258
  19.3 2.8 %collective-permute-done.10.refs_10_ = f32[64,384]{1,0:T(8,128)S(1)} collective-permute-done((f32[64,384]{1,0:T(8,128)S(1)}, f32[64,384]{1,0:T(8,128)S(1)}, u32[]{:S(2)}, u32[]{:S(2)}) %collective-permute-start.10) | collective-permute-done | bytes 98336 | tf_op jit(solution)/shard_map/ppermute | solution.py:258
  24.3 2.3 %plane_grad_1.1 = f32[9,32,256]{2,1,0:T(8,128)S(1)} custom-call(f32[256,256]{1,0:T(8,128)S(1)} %get-tuple-element.59.refs_0_, f32[256,256]{1,0:T(8,128)S(1)} %collective-permute-done.refs_1_, f32[256,256]{1,0:T(8,128)S(1)} %collective-permute-done.1.refs_2_, f32[256,256]{1,0:T(8,128)S(1)} %collective-permute-done.2.refs_3_, ...), custom_call_target="tpu_custom_call" | custom-call | flops 905969664 | bytes 4194304 | tf_op jit(solution)/shard_map/plane_grad_1/pallas_call | solution.py:198
  28.0 3.5 %plane_grad_2.1 = (f32[9,32,256]{2,1,0:T(8,128)S(1)}, f32[9,32,256]{2,1,0:T(8,128)S(1)}) custom-call(f32[256,256]{1,0:T(8,128)S(1)} %get-tuple-element.59.refs_0_, f32[256,256]{1,0:T(8,128)S(1)} %collective-permute-done.refs_1_, f32[256,256]{1,0:T(8,128)S(1)} %collective-permute-done.1.refs_2_, f32[256,256]{1,0:T(8,128)S(1)} %collective-permute-done.2.refs_3_, ...), custom_call_target="tpu_custom_call" | custom-call | flops 1811939328 | bytes 4194304 | tf_op jit(solution)/shard_map/plane_grad_2/pallas_call | solution.py:198
  33.0 5.4 %collective-permute-done.16 = f32[9,32,256]{2,1,0:T(8,128)S(1)} collective-permute-done((f32[9,32,256]{2,1,0:T(8,128)S(1)}, f32[9,32,256]{2,1,0:T(8,128)S(1)}, u32[]{:S(2)}, u32[]{:S(2)}) %collective-permute-start.16) | collective-permute-done | bytes 294944 | tf_op jit(solution)/shard_map/ppermute | solution.py:258
  38.5 2.5 %collective-permute-start.17 = (f32[9,32,256]{2,1,0:T(8,128)S(1)}, f32[9,32,256]{2,1,0:T(8,128)S(1)}, u32[]{:S(2)}, u32[]{:S(2)}) collective-permute-start(f32[9,32,256]{2,1,0:T(8,128)S(1)} %add.18), channel_id=1, source_target_pairs={{8,16},{16,8},{9,17},{17,9},{10,18},{18,10},{11,19},{19,11},{12,20... | collective-permute-start | bytes 884744 | tf_op jit(solution)/shard_map/ppermute | solution.py:258
  42.3 1.8 %collective-permute-done.18 = f32[9,32,256]{2,1,0:T(8,128)S(1)} collective-permute-done((f32[9,32,256]{2,1,0:T(8,128)S(1)}, f32[9,32,256]{2,1,0:T(8,128)S(1)}, u32[]{:S(2)}, u32[]{:S(2)}) %collective-permute-start.18) | collective-permute-done | bytes 294944 | tf_op jit(solution)/shard_map/ppermute | solution.py:258
  44.1 3.7 %collective-permute-done.17 = f32[9,32,256]{2,1,0:T(8,128)S(1)} collective-permute-done((f32[9,32,256]{2,1,0:T(8,128)S(1)}, f32[9,32,256]{2,1,0:T(8,128)S(1)}, u32[]{:S(2)}, u32[]{:S(2)}) %collective-permute-start.17) | collective-permute-done | bytes 294944 | tf_op jit(solution)/shard_map/ppermute | solution.py:258
  47.9 2.5 %collective-permute-start.20 = (f32[9,32,256]{2,1,0:T(8,128)S(1)}, f32[9,32,256]{2,1,0:T(8,128)S(1)}, u32[]{:S(2)}, u32[]{:S(2)}) collective-permute-start(f32[9,32,256]{2,1,0:T(8,128)S(1)} %add.20), channel_id=1, source_target_pairs={{8,16},{16,8},{9,17},{17,9},{10,18},{18,10},{11,19},{19,11},{12,20... | collective-permute-start | bytes 884744 | tf_op jit(solution)/shard_map/ppermute | solution.py:258
  52.8 1.9 %collective-permute-start.23 = (f32[8,1,8,256]{3,2,1,0:T(8,128)S(1)}, f32[8,1,8,256]{3,2,1,0:T(8,128)S(1)}, u32[]{:S(2)}, u32[]{:S(2)}) collective-permute-start(f32[8,1,8,256]{3,2,1,0:T(8,128)S(1)} %pad_maximum_fusion.19), channel_id=1, source_target_pairs={{2,0},{4,2},{6,4},{0,6},{3,1},{5,3},{7,5},{1,7},{10,8},{12,10},{14... | collective-permute-start | bytes 196616 | tf_op jit(solution)/shard_map/ppermute | solution.py:258
  54.7 2.3 %collective-permute-done.22 = f32[8,1,8,256]{3,2,1,0:T(8,128)S(1)} collective-permute-done((f32[8,1,8,256]{3,2,1,0:T(8,128)S(1)}, f32[8,1,8,256]{3,2,1,0:T(8,128)S(1)}, u32[]{:S(2)}, u32[]{:S(2)}) %collective-permute-start.22) | collective-permute-done | bytes 65568 | tf_op jit(solution)/shard_map/ppermute | solution.py:258
  58.7 2.1 %collective-permute-start.24 = (f32[9,16,256]{2,1,0:T(8,128)S(1)}, f32[9,16,256]{2,1,0:T(8,128)S(1)}, u32[]{:S(2)}, u32[]{:S(2)}) collective-permute-start(f32[9,16,256]{2,1,0:T(8,128)S(1)} %get-tuple-element.142), channel_id=1, source_target_pairs={{0,2},{2,0},{4,6},{6,4},{1,3},{3,1},{5,7},{7,5},{8,10},{10,8},{12,... | collective-permute-start | bytes 442376 | tf_op jit(solution)/shard_map/ppermute | solution.py:258
  62.1 3.6 %collective-permute-start.27 = (f32[9,32,256]{2,1,0:T(8,128)S(1)}, f32[9,32,256]{2,1,0:T(8,128)S(1)}, u32[]{:S(2)}, u32[]{:S(2)}) collective-permute-start(f32[9,32,256]{2,1,0:T(8,128)S(1)} %add.22), channel_id=1, source_target_pairs={{8,16},{16,8},{9,17},{17,9},{10,18},{18,10},{11,19},{19,11},{12,20... | collective-permute-start | bytes 884744 | tf_op jit(solution)/shard_map/ppermute | solution.py:258
  67.1 2.0 %collective-permute-start.33 = (f32[2,9,16,256]{3,2,1,0:T(8,128)S(1)}, f32[2,9,16,256]{3,2,1,0:T(8,128)S(1)}, u32[]{:S(2)}, u32[]{:S(2)}) collective-permute-start(f32[2,9,16,256]{3,2,1,0:T(8,128)S(1)} %pad_maximum_fusion.8.refs_1_), channel_id=1, source_target_pairs={{0,2},{2,0},{4,6},{6,4},{1,3},{3,1},{5,7},{7,5},{8,10},{10,8},{12,... | collective-permute-start | bytes 884744 | tf_op jit(solution)/shard_map/ppermute | solution.py:258
  72.4 1.6 %collective-permute-start.31 = (f32[9,16,256]{2,1,0:T(8,128)S(1)}, f32[9,16,256]{2,1,0:T(8,128)S(1)}, u32[]{:S(2)}, u32[]{:S(2)}) collective-permute-start(f32[9,16,256]{2,1,0:T(8,128)S(1)} %get-tuple-element.137), channel_id=1, source_target_pairs={{0,4},{2,6},{4,0},{6,2},{1,5},{3,7},{5,1},{7,3},{8,12},{10,14},{12... | collective-permute-start | bytes 442376 | tf_op jit(solution)/shard_map/ppermute | solution.py:258
  75.0 2.5 %conv_0.1 = (f32[256,256]{1,0:T(8,128)S(1)}, f32[256,256]{1,0:T(8,128)S(1)}) custom-call(f32[6,10,8,256]{3,2,1,0:T(8,128)S(1)} %get-tuple-element.88.refs_0_, f32[6,10,8,256]{3,2,1,0:T(8,128)S(1)} %pad_maximum_fusion.5.refs_1_, f32[6,10,8,256]{3,2,1,0:T(8,128)S(1)} %get-tuple-element.90.refs_2_, f32[6,10,8,256]{3,2,1,0:T(8,128)S(1)} %get-tuple-element.91.refs_3_, ...), custom_call_target="tpu_custom_call" | custom-call | flops 1811939328 | bytes 4194304 | tf_op jit(solution)/shard_map/conv_0/pallas_call | solution.py:90
  77.5 1.8 %collective-permute-done.31 = f32[9,16,256]{2,1,0:T(8,128)S(1)} collective-permute-done((f32[9,16,256]{2,1,0:T(8,128)S(1)}, f32[9,16,256]{2,1,0:T(8,128)S(1)}, u32[]{:S(2)}, u32[]{:S(2)}) %collective-permute-start.31) | collective-permute-done | bytes 147488 | tf_op jit(solution)/shard_map/ppermute | solution.py:258
  79.7 1.6 %collective-permute-start.35 = (f32[9,16,256]{2,1,0:T(8,128)S(1)}, f32[9,16,256]{2,1,0:T(8,128)S(1)}, u32[]{:S(2)}, u32[]{:S(2)}) collective-permute-start(f32[9,16,256]{2,1,0:T(8,128)S(1)} %get-tuple-element.133), channel_id=1, source_target_pairs={{0,4},{2,6},{4,0},{6,2},{1,5},{3,7},{5,1},{7,3},{8,12},{10,14},{12... | collective-permute-start | bytes 442376 | tf_op jit(solution)/shard_map/ppermute | solution.py:258
  84.0 4.1 %collective-permute-done.34 = f32[9,16,256]{2,1,0:T(8,128)S(1)} collective-permute-done((f32[9,16,256]{2,1,0:T(8,128)S(1)}, f32[9,16,256]{2,1,0:T(8,128)S(1)}, u32[]{:S(2)}, u32[]{:S(2)}) %collective-permute-start.34) | collective-permute-done | bytes 147488 | tf_op jit(solution)/shard_map/ppermute | solution.py:258
  88.7 1.8 %collective-permute-start.39 = (f32[2,9,16,256]{3,2,1,0:T(8,128)S(1)}, f32[2,9,16,256]{3,2,1,0:T(8,128)S(1)}, u32[]{:S(2)}, u32[]{:S(2)}) collective-permute-start(f32[2,9,16,256]{3,2,1,0:T(8,128)S(1)} %pad_maximum_fusion.12.refs_1_), channel_id=1, source_target_pairs={{0,2},{2,0},{4,6},{6,4},{1,3},{3,1},{5,7},{7,5},{8,10},{10,8},{12,... | collective-permute-start | bytes 884744 | tf_op jit(solution)/shard_map/ppermute | solution.py:258
  90.5 2.5 %conv_1.1 = (f32[256,256]{1,0:T(8,128)S(1)}, f32[256,256]{1,0:T(8,128)S(1)}) custom-call(f32[6,10,8,256]{3,2,1,0:T(8,128)S(1)} %get-tuple-element.88.refs_0_, f32[6,10,8,256]{3,2,1,0:T(8,128)S(1)} %pad_maximum_fusion.5.refs_1_, f32[6,10,8,256]{3,2,1,0:T(8,128)S(1)} %get-tuple-element.90.refs_2_, f32[6,10,8,256]{3,2,1,0:T(8,128)S(1)} %get-tuple-element.91.refs_3_, ...), custom_call_target="tpu_custom_call" | custom-call | flops 1811939328 | bytes 4194304 | tf_op jit(solution)/shard_map/conv_1/pallas_call | solution.py:90
  95.9 3.2 %conv_2.1 = (f32[256,256]{1,0:T(8,128)}, f32[256,256]{1,0:T(8,128)}) custom-call(f32[6,10,8,256]{3,2,1,0:T(8,128)S(1)} %get-tuple-element.88.refs_0_, f32[6,10,8,256]{3,2,1,0:T(8,128)S(1)} %pad_maximum_fusion.5.refs_1_, f32[6,10,8,256]{3,2,1,0:T(8,128)S(1)} %get-tuple-element.90.refs_2_, f32[6,10,8,256]{3,2,1,0:T(8,128)S(1)} %get-tuple-element.91.refs_3_, ...), custom_call_target="tpu_custom_call" | custom-call | flops 1811939328 | bytes 4194304 | tf_op jit(solution)/shard_map/conv_2/pallas_call | solution.py:90
  (118 shorter events, 36.9 us)
Async XLA Ops:
  0.7 15.3 %collective-permute-start.2 = (f32[256,256]{1,0:T(8,128)}, f32[256,256]{1,0:T(8,128)S(1)}, u32[]{:S(2)}, u32[]{:S(2)}) collective-permute-start(f32[256,256]{1,0:T(8,128)} %bitcast.37), channel_id=1, source_target_pairs={{6,0},{0,2},{2,4},{4,6},{7,1},{1,3},{3,5},{5,7},{14,8},{8,10},{10,... | collective-permute-start | bytes 786440 | tf_op jit(solution)/shard_map/ppermute | solution.py:258
  2.3 14.3 %collective-permute-start.1 = (f32[256,256]{1,0:T(8,128)}, f32[256,256]{1,0:T(8,128)S(1)}, u32[]{:S(2)}, u32[]{:S(2)}) collective-permute-start(f32[256,256]{1,0:T(8,128)} %bitcast.38), channel_id=1, source_target_pairs={{4,0},{6,2},{0,4},{2,6},{5,1},{7,3},{1,5},{3,7},{12,8},{14,10},{8,... | collective-permute-start | bytes 786440 | tf_op jit(solution)/shard_map/ppermute | solution.py:258
  6.4 7.4 %collective-permute-start.5 = (f32[2,8,8,256]{3,2,1,0:T(8,128)S(1)}, f32[2,8,8,256]{3,2,1,0:T(8,128)S(1)}, u32[]{:S(2)}, u32[]{:S(2)}) collective-permute-start(f32[2,8,8,256]{3,2,1,0:T(8,128)S(1)} %pad_maximum_fusion.15), channel_id=1, source_target_pairs={{8,0},{16,8},{24,16},{0,24},{9,1},{17,9},{25,17},{1,25},{10,2},{18... | collective-permute-start | bytes 393224 | tf_op jit(solution)/shard_map/ppermute | solution.py:258
  6.9 11.9 %collective-permute-start = (f32[256,256]{1,0:T(8,128)}, f32[256,256]{1,0:T(8,128)S(1)}, u32[]{:S(2)}, u32[]{:S(2)}) collective-permute-start(f32[256,256]{1,0:T(8,128)} %bitcast.39), channel_id=1, source_target_pairs={{2,0},{4,2},{6,4},{0,6},{3,1},{5,3},{7,5},{1,7},{10,8},{12,10},{14... | collective-permute-start | bytes 786440 | tf_op jit(solution)/shard_map/ppermute | solution.py:258
  26.7 11.7 %collective-permute-start.16 = (f32[9,32,256]{2,1,0:T(8,128)S(1)}, f32[9,32,256]{2,1,0:T(8,128)S(1)}, u32[]{:S(2)}, u32[]{:S(2)}) collective-permute-start(f32[9,32,256]{2,1,0:T(8,128)S(1)} %plane_grad_1.1), channel_id=1, source_target_pairs={{0,8},{24,16},{1,9},{25,17},{2,10},{26,18},{3,11},{27,19},{4,12},{... | collective-permute-start | bytes 884744 | tf_op jit(solution)/shard_map/ppermute | solution.py:258
  31.5 12.6 %collective-permute-start.18 = (f32[9,32,256]{2,1,0:T(8,128)S(1)}, f32[9,32,256]{2,1,0:T(8,128)S(1)}, u32[]{:S(2)}, u32[]{:S(2)}) collective-permute-start(f32[9,32,256]{2,1,0:T(8,128)S(1)} %get-tuple-element.77), channel_id=1, source_target_pairs={{0,8},{24,16},{1,9},{25,17},{2,10},{26,18},{3,11},{27,19},{4,12},{... | collective-permute-start | bytes 884744 | tf_op jit(solution)/shard_map/ppermute | solution.py:258
  38.5 9.3 %collective-permute-start.17 = (f32[9,32,256]{2,1,0:T(8,128)S(1)}, f32[9,32,256]{2,1,0:T(8,128)S(1)}, u32[]{:S(2)}, u32[]{:S(2)}) collective-permute-start(f32[9,32,256]{2,1,0:T(8,128)S(1)} %add.18), channel_id=1, source_target_pairs={{8,16},{16,8},{9,17},{17,9},{10,18},{18,10},{11,19},{19,11},{12,20... | collective-permute-start | bytes 884744 | tf_op jit(solution)/shard_map/ppermute | solution.py:258
  41.0 13.7 %collective-permute-start.21 = (f32[9,32,256]{2,1,0:T(8,128)S(1)}, f32[9,32,256]{2,1,0:T(8,128)S(1)}, u32[]{:S(2)}, u32[]{:S(2)}) collective-permute-start(f32[9,32,256]{2,1,0:T(8,128)S(1)} %get-tuple-element.80), channel_id=1, source_target_pairs={{0,8},{24,16},{1,9},{25,17},{2,10},{26,18},{3,11},{27,19},{4,12},{... | collective-permute-start | bytes 884744 | tf_op jit(solution)/shard_map/ppermute | solution.py:258
  47.9 9.2 %collective-permute-start.20 = (f32[9,32,256]{2,1,0:T(8,128)S(1)}, f32[9,32,256]{2,1,0:T(8,128)S(1)}, u32[]{:S(2)}, u32[]{:S(2)}) collective-permute-start(f32[9,32,256]{2,1,0:T(8,128)S(1)} %add.20), channel_id=1, source_target_pairs={{8,16},{16,8},{9,17},{17,9},{10,18},{18,10},{11,19},{19,11},{12,20... | collective-permute-start | bytes 884744 | tf_op jit(solution)/shard_map/ppermute | solution.py:258
  50.4 6.7 %collective-permute-start.19 = (f32[9,32,256]{2,1,0:T(8,128)S(1)}, f32[9,32,256]{2,1,0:T(8,128)S(1)}, u32[]{:S(2)}, u32[]{:S(2)}) collective-permute-start(f32[9,32,256]{2,1,0:T(8,128)S(1)} %add.19), channel_id=1, source_target_pairs={{8,0},{16,24},{9,1},{17,25},{10,2},{18,26},{11,3},{19,27},{12,4},{... | collective-permute-start | bytes 884744 | tf_op jit(solution)/shard_map/ppermute | solution.py:258
  57.3 9.8 %collective-permute-start.25 = (f32[9,16,256]{2,1,0:T(8,128)S(1)}, f32[9,16,256]{2,1,0:T(8,128)S(1)}, u32[]{:S(2)}, u32[]{:S(2)}) collective-permute-start(f32[9,16,256]{2,1,0:T(8,128)S(1)} %get-tuple-element.141), channel_id=1, source_target_pairs={{0,4},{2,6},{4,0},{6,2},{1,5},{3,7},{5,1},{7,3},{8,12},{10,14},{12... | collective-permute-start | bytes 442376 | tf_op jit(solution)/shard_map/ppermute | solution.py:258
  58.7 7.9 %collective-permute-start.24 = (f32[9,16,256]{2,1,0:T(8,128)S(1)}, f32[9,16,256]{2,1,0:T(8,128)S(1)}, u32[]{:S(2)}, u32[]{:S(2)}) collective-permute-start(f32[9,16,256]{2,1,0:T(8,128)S(1)} %get-tuple-element.142), channel_id=1, source_target_pairs={{0,2},{2,0},{4,6},{6,4},{1,3},{3,1},{5,7},{7,5},{8,10},{10,8},{12,... | collective-permute-start | bytes 442376 | tf_op jit(solution)/shard_map/ppermute | solution.py:258
  60.8 8.8 %collective-permute-start.26 = (f32[9,32,256]{2,1,0:T(8,128)S(1)}, f32[9,32,256]{2,1,0:T(8,128)S(1)}, u32[]{:S(2)}, u32[]{:S(2)}) collective-permute-start(f32[9,32,256]{2,1,0:T(8,128)S(1)} %add.21), channel_id=1, source_target_pairs={{8,0},{16,24},{9,1},{17,25},{10,2},{18,26},{11,3},{19,27},{12,4},{... | collective-permute-start | bytes 884744 | tf_op jit(solution)/shard_map/ppermute | solution.py:258
  62.1 8.6 %collective-permute-start.27 = (f32[9,32,256]{2,1,0:T(8,128)S(1)}, f32[9,32,256]{2,1,0:T(8,128)S(1)}, u32[]{:S(2)}, u32[]{:S(2)}) collective-permute-start(f32[9,32,256]{2,1,0:T(8,128)S(1)} %add.22), channel_id=1, source_target_pairs={{8,16},{16,8},{9,17},{17,9},{10,18},{18,10},{11,19},{19,11},{12,20... | collective-permute-start | bytes 884744 | tf_op jit(solution)/shard_map/ppermute | solution.py:258
  66.6 10.8 %collective-permute-start.32 = (f32[2,9,16,256]{3,2,1,0:T(8,128)S(1)}, f32[2,9,16,256]{3,2,1,0:T(8,128)S(1)}, u32[]{:S(2)}, u32[]{:S(2)}) collective-permute-start(f32[2,9,16,256]{3,2,1,0:T(8,128)S(1)} %pad_maximum_fusion.7.refs_0_), channel_id=1, source_target_pairs={{0,4},{2,6},{4,0},{6,2},{1,5},{3,7},{5,1},{7,3},{8,12},{10,14},{12... | collective-permute-start | bytes 884744 | tf_op jit(solution)/shard_map/ppermute | solution.py:258
  67.1 10.4 %collective-permute-start.33 = (f32[2,9,16,256]{3,2,1,0:T(8,128)S(1)}, f32[2,9,16,256]{3,2,1,0:T(8,128)S(1)}, u32[]{:S(2)}, u32[]{:S(2)}) collective-permute-start(f32[2,9,16,256]{3,2,1,0:T(8,128)S(1)} %pad_maximum_fusion.8.refs_1_), channel_id=1, source_target_pairs={{0,2},{2,0},{4,6},{6,4},{1,3},{3,1},{5,7},{7,5},{8,10},{10,8},{12,... | collective-permute-start | bytes 884744 | tf_op jit(solution)/shard_map/ppermute | solution.py:258
  70.9 8.7 %collective-permute-start.29 = (f32[9,32,256]{2,1,0:T(8,128)S(1)}, f32[9,32,256]{2,1,0:T(8,128)S(1)}, u32[]{:S(2)}, u32[]{:S(2)}) collective-permute-start(f32[9,32,256]{2,1,0:T(8,128)S(1)} %add.23), channel_id=1, source_target_pairs={{8,0},{16,24},{9,1},{17,25},{10,2},{18,26},{11,3},{19,27},{12,4},{... | collective-permute-start | bytes 884744 | tf_op jit(solution)/shard_map/ppermute | solution.py:258
  72.4 6.8 %collective-permute-start.31 = (f32[9,16,256]{2,1,0:T(8,128)S(1)}, f32[9,16,256]{2,1,0:T(8,128)S(1)}, u32[]{:S(2)}, u32[]{:S(2)}) collective-permute-start(f32[9,16,256]{2,1,0:T(8,128)S(1)} %get-tuple-element.137), channel_id=1, source_target_pairs={{0,4},{2,6},{4,0},{6,2},{1,5},{3,7},{5,1},{7,3},{8,12},{10,14},{12... | collective-permute-start | bytes 442376 | tf_op jit(solution)/shard_map/ppermute | solution.py:258
  79.7 9.0 %collective-permute-start.35 = (f32[9,16,256]{2,1,0:T(8,128)S(1)}, f32[9,16,256]{2,1,0:T(8,128)S(1)}, u32[]{:S(2)}, u32[]{:S(2)}) collective-permute-start(f32[9,16,256]{2,1,0:T(8,128)S(1)} %get-tuple-element.133), channel_id=1, source_target_pairs={{0,4},{2,6},{4,0},{6,2},{1,5},{3,7},{5,1},{7,3},{8,12},{10,14},{12... | collective-permute-start | bytes 442376 | tf_op jit(solution)/shard_map/ppermute | solution.py:258
  81.3 6.8 %collective-permute-start.34 = (f32[9,16,256]{2,1,0:T(8,128)S(1)}, f32[9,16,256]{2,1,0:T(8,128)S(1)}, u32[]{:S(2)}, u32[]{:S(2)}) collective-permute-start(f32[9,16,256]{2,1,0:T(8,128)S(1)} %get-tuple-element.134), channel_id=1, source_target_pairs={{0,2},{2,0},{4,6},{6,4},{1,3},{3,1},{5,7},{7,5},{8,10},{10,8},{12,... | collective-permute-start | bytes 442376 | tf_op jit(solution)/shard_map/ppermute | solution.py:258
  82.1 12.3 %collective-permute-start.37 = (f32[2,9,16,256]{3,2,1,0:T(8,128)S(1)}, f32[2,9,16,256]{3,2,1,0:T(8,128)S(1)}, u32[]{:S(2)}, u32[]{:S(2)}) collective-permute-start(f32[2,9,16,256]{3,2,1,0:T(8,128)S(1)} %pad_maximum_fusion.10.refs_5_), channel_id=1, source_target_pairs={{0,2},{2,0},{4,6},{6,4},{1,3},{3,1},{5,7},{7,5},{8,10},{10,8},{12,... | collective-permute-start | bytes 884744 | tf_op jit(solution)/shard_map/ppermute | solution.py:258
  83.4 11.0 %collective-permute-start.36 = (f32[2,9,16,256]{3,2,1,0:T(8,128)S(1)}, f32[2,9,16,256]{3,2,1,0:T(8,128)S(1)}, u32[]{:S(2)}, u32[]{:S(2)}) collective-permute-start(f32[2,9,16,256]{3,2,1,0:T(8,128)S(1)} %pad_maximum_fusion.9.refs_4_), channel_id=1, source_target_pairs={{0,4},{2,6},{4,0},{6,2},{1,5},{3,7},{5,1},{7,3},{8,12},{10,14},{12... | collective-permute-start | bytes 884744 | tf_op jit(solution)/shard_map/ppermute | solution.py:258
  88.1 11.1 %collective-permute-start.38 = (f32[2,9,16,256]{3,2,1,0:T(8,128)S(1)}, f32[2,9,16,256]{3,2,1,0:T(8,128)S(1)}, u32[]{:S(2)}, u32[]{:S(2)}) collective-permute-start(f32[2,9,16,256]{3,2,1,0:T(8,128)S(1)} %pad_maximum_fusion.11.refs_0_), channel_id=1, source_target_pairs={{0,4},{2,6},{4,0},{6,2},{1,5},{3,7},{5,1},{7,3},{8,12},{10,14},{12... | collective-permute-start | bytes 884744 | tf_op jit(solution)/shard_map/ppermute | solution.py:258
  88.7 10.5 %collective-permute-start.39 = (f32[2,9,16,256]{3,2,1,0:T(8,128)S(1)}, f32[2,9,16,256]{3,2,1,0:T(8,128)S(1)}, u32[]{:S(2)}, u32[]{:S(2)}) collective-permute-start(f32[2,9,16,256]{3,2,1,0:T(8,128)S(1)} %pad_maximum_fusion.12.refs_1_), channel_id=1, source_target_pairs={{0,2},{2,0},{4,6},{6,4},{1,3},{3,1},{5,7},{7,5},{8,10},{10,8},{12,... | collective-permute-start | bytes 884744 | tf_op jit(solution)/shard_map/ppermute | solution.py:258
  (22 other events, 130.1 us)
